TPU v7x, 32 devices: a whole 2x2x4 slice. The times are simulated.
32 devices in a mesh: seq: 8 (over z, y), tensor: 4 (over x, core).
Axes of the slice: x: 2, y: 2, z: 4, core: 2. Of those that a mesh axis runs over, the one named last changes fastest.
Arguments:
- hidden_in: float32 [2048, 3840], P('seq'), may hold values from -6 to 6
- query_proj: float32 [3840, 4096], P(None, 'tensor'), may hold values from -0.09375 to 0.09375
- key_proj: float32 [3840, 2048], P(None, 'tensor'), may hold values from -0.09375 to 0.09375
- value_proj: float32 [3840, 2048], P(None, 'tensor'), may hold values from -0.09375 to 0.09375
- query_gain: float32 [256], replicated, may hold values from 0.1 to 1.9
- key_gain: float32 [256], replicated, may hold values from 0.1 to 1.9
- segment_ids: int32 [2048], replicated, may hold values from 0 to 3, never falling along the last dimension, each value on 1 to 1024 neighbouring positions
- grad_out: float32 [2048, 4096], P('seq', 'tensor'), may hold values from -6 to 6
Outputs:
- attended: float32 [2048, 4096], P('seq', 'tensor')
- grad_input: float32 [2048, 3840], P('seq', 'tensor')
- grad_query: float32 [3840, 4096], P('seq', 'tensor')
- grad_key: float32 [3840, 2048], P('seq', 'tensor')
- grad_value: float32 [3840, 2048], P('seq', 'tensor')
Inputs may be any that keep to these rules, and one draw needn't show every extreme that they name: `segment_ids`: segment ids never fall along the transcript; each of the 4 documents holds 1 to 1024 tokens and one holds exactly 1024.
All inputs are finite; a program needn't handle non-finite values.
Results may differ from a plain program's by a relative error of at most 0.0003.
Values sent between devices are 32-bit elements; how exact they have to be, the bound alone decides.
No kernel may reach another device: no remote copies, remote signals or barrier semaphores. Data moves between devices by JAX's collectives and lax.ppermute only.
A program may use at most 192 MiB of HBM per device.

v0:
```python
import functools

import jax
import jax.numpy as jnp
from jax import lax
from jax.experimental import pallas as pl
from jax.experimental.pallas import tpu as pltpu
from jax.sharding import Mesh, PartitionSpec as P

WINDOW = 1024
CHAIN = 4
CORES = 2

MIB = 1024 * 1024
SOON = pl.CostEstimate(flops=1024, bytes_accessed=1024, transcendentals=0)
epsilon = 1e-06


def after(block, *earlier):
    return lax.optimization_barrier((block, earlier))[0]


def rope_tables(positions, head_width):
    middle = head_width // 2
    exponent = 2.0 * jnp.arange(middle).astype(jnp.float32) / head_width
    frequency = 10000.0 ** (-exponent)
    angles = positions.astype(jnp.float32)[:, None] * frequency[None, :]
    return jnp.cos(angles), jnp.sin(angles)


def inverse_rms(vector):
    return lax.rsqrt(jnp.mean(vector * vector, axis=-1, keepdims=True) + epsilon)


def norm_rotate(vector, scaling, cosine, sine):
    middle = vector.shape[-1] // 2
    normed = vector * inverse_rms(vector) * scaling
    low, high = normed[:, :middle], normed[:, middle:]
    return jnp.concatenate([low * cosine - high * sine, high * cosine + low * sine], axis=1)


def norm_rotate_back(grad, vector, scaling, cosine, sine):
    middle = vector.shape[-1] // 2
    low, high = grad[:, :middle], grad[:, middle:]
    d_normed = jnp.concatenate([low * cosine + high * sine, high * cosine - low * sine], axis=1)
    d_normed = d_normed * scaling
    inverse = inverse_rms(vector)
    unit = vector * inverse
    return inverse * (d_normed - unit * jnp.mean(d_normed * unit, axis=-1, keepdims=True))


def halves(array):
    high = array.astype(jnp.bfloat16)
    return high, (array - high.astype(jnp.float32)).astype(jnp.bfloat16)


def three(left, right, left_dim, right_dim):
    def once(a, b):
        return lax.dot_general(
            a, b, (((left_dim,), (right_dim,)), ((), ())), preferred_element_type=jnp.float32
        )

    return once(left[0], right[0]) + (once(left[0], right[1]) + once(left[1], right[0]))


def attention_kernel(blocks, per_kv, *refs):
    query_ref, grad_ref, gain_ref, cos_ref, sin_ref, seg_ref, key_seg_ref = refs[:7]
    kv_refs = refs[7 : 7 + blocks]
    out_ref, d_query_ref = refs[7 + blocks : 9 + blocks]
    d_kv_refs = refs[9 + blocks : 9 + 2 * blocks]
    weight_ref, d_share_ref, share_high, share_low, score_high, score_low = refs[9 + 2 * blocks :]
    rows = query_ref.shape[0]
    head = gain_ref.shape[1]
    factor = head ** (-0.5)
    gain, cosine, sine = gain_ref[...], cos_ref[...], sin_ref[...]
    raw = [query_ref[:, h * head : (h + 1) * head] for h in range(per_kv)]
    q_rot = halves(
        jnp.concatenate([norm_rotate(u, gain, cosine, sine) for u in raw], axis=0)
    )
    grad = halves(
        jnp.concatenate([grad_ref[:, h * head : (h + 1) * head] for h in range(per_kv)], axis=0)
    )
    total = jnp.zeros((1, per_kv * rows), jnp.float32)
    mixed = jnp.zeros((1, per_kv * rows), jnp.float32)
    seg = jnp.concatenate([seg_ref[...]] * per_kv, axis=1)
    turned_keys, turned_values = [], []
    lane = lax.broadcasted_iota(jnp.int32, (rows, rows), 1)
    lane = jnp.concatenate([lane] * per_kv, axis=1)
    row = lax.broadcasted_iota(jnp.int32, (rows, per_kv * rows), 0)
    for j in range(blocks):
        place = slice(j * rows, (j + 1) * rows)
        key, value = kv_refs[j][:, :head], kv_refs[j][:, head:]
        turned_keys.append(key.T)
        turned_values.append(value.T)
        scores = three(halves(key), q_rot, 1, 1) * factor
        distance = (blocks - 1 - j) * rows + lane - row
        allowed = (distance >= 0) & (distance < WINDOW) & (key_seg_ref[place, :] == seg)
        weights = jnp.where(allowed, jnp.exp(scores), 0.0)
        d_shares = three(halves(value), grad, 1, 1)
        weight_ref[place, :] = weights
        d_share_ref[place, :] = d_shares
        total = total + jnp.sum(weights, axis=0, keepdims=True)
        mixed = mixed + jnp.sum(weights * d_shares, axis=0, keepdims=True)
    scale = 1.0 / total
    delta = mixed * scale
    for j in range(blocks):
        place = slice(j * rows, (j + 1) * rows)
        shares = weight_ref[place, :] * scale
        d_scores = shares * (d_share_ref[place, :] - delta) * factor
        share_pair = halves(shares)
        score_pair = halves(d_scores)
        share_high[place, :], share_low[place, :] = share_pair
        score_high[place, :], score_low[place, :] = score_pair
        d_kv_refs[j][:, :head] = three(score_pair, q_rot, 1, 0)
        d_kv_refs[j][:, head:] = three(share_pair, grad, 1, 0)
    turned_out = three(
        halves(jnp.concatenate(turned_values, axis=1)), (share_high[...], share_low[...]), 1, 0
    )
    turned_query = three(
        halves(jnp.concatenate(turned_keys, axis=1)), (score_high[...], score_low[...]), 1, 0
    )
    for h in range(per_kv):
        place = slice(h * rows, (h + 1) * rows)
        columns = slice(h * head, (h + 1) * head)
        out_ref[:, columns] = turned_out[:, place].T
        d_query_ref[:, columns] = norm_rotate_back(
            turned_query[:, place].T, raw[h], gain, cosine, sine
        )


def attention(queries, grads, gain, cosine, sine, query_seg, key_seg, window, per_kv):
    rows, width = queries.shape
    blocks = len(window)
    span = blocks * rows
    flat = jax.ShapeDtypeStruct((rows, width), jnp.float32)
    part = jax.ShapeDtypeStruct(window[0].shape, jnp.float32)
    wide = per_kv * rows
    results = pl.pallas_call(
        functools.partial(attention_kernel, blocks, per_kv),
        out_shape=[flat, flat] + [part] * blocks,
        scratch_shapes=[
            pltpu.VMEM((span, wide), jnp.float32),
            pltpu.VMEM((span, wide), jnp.float32),
            pltpu.VMEM((span, wide), jnp.bfloat16),
            pltpu.VMEM((span, wide), jnp.bfloat16),
            pltpu.VMEM((span, wide), jnp.bfloat16),
            pltpu.VMEM((span, wide), jnp.bfloat16),
        ],
        compiler_params=pltpu.CompilerParams(vmem_limit_bytes=40 * 1024 * 1024),
        cost_estimate=SOON,
    )(queries, grads, gain, cosine, sine, query_seg, key_seg, *window)
    return results[0], results[1], results[2:]


def project_kernel(normed, lanes, source_ref, *refs):
    if normed:
        weight_refs, rest = refs[: 2 * lanes], refs[2 * lanes :]
        gain_ref, cos_ref, sin_ref, raw_ref, packed_ref, total_ref = rest
    else:
        weight_refs, (raw_ref, total_ref) = refs[:lanes], refs[lanes:]
    step = pl.program_id(0)
    stacked = [
        jnp.concatenate([ref[...] for ref in weight_refs[start : start + lanes]], axis=0)
        for start in range(0, len(weight_refs), lanes)
    ]
    weight = stacked[0] if len(stacked) == 1 else jnp.concatenate(stacked, axis=1)
    product = three(halves(source_ref[...]), halves(weight), 1, 0)

    @pl.when(step == 0)
    def _():
        total_ref[...] = product

    @pl.when(step > 0)
    def _():
        total_ref[...] += product

    @pl.when(step == pl.num_programs(0) - 1)
    def _():
        if normed:
            head = gain_ref.shape[1]
            raw = total_ref[:, :head]
            raw_ref[...] = raw
            packed_ref[:, :head] = norm_rotate(raw, gain_ref[...], cos_ref[...], sin_ref[...])
            packed_ref[:, head:] = total_ref[:, head:]
        else:
            raw_ref[...] = total_ref[...]


def project(source, weights, group, columns, extra):
    rows, width = source.shape
    steps, lanes = 5, 3
    tile = width // steps
    thin = tile // lanes
    normed = len(weights) > 1
    wide = columns * len(weights)
    whole = [pl.BlockSpec(e.shape, lambda k: (0, 0)) for e in extra]
    outs = [jax.ShapeDtypeStruct((rows, columns), jnp.float32)]
    if normed:
        outs.append(jax.ShapeDtypeStruct((rows, wide), jnp.float32))
    return pl.pallas_call(
        functools.partial(project_kernel, normed, lanes),
        grid=(steps,),
        out_shape=outs,
        in_specs=[pl.BlockSpec((rows, tile), lambda k: (0, k))]
        + [
            pl.BlockSpec((thin, columns), lambda k, lane=lane: (k * lanes + lane, group))
            for lane in range(lanes)
        ]
        * len(weights)
        + whole,
        out_specs=[pl.BlockSpec(o.shape, lambda k: (0, 0)) for o in outs],
        scratch_shapes=[pltpu.VMEM((rows, wide), jnp.float32)],
        compiler_params=pltpu.CompilerParams(vmem_limit_bytes=56 * MIB),
        cost_estimate=SOON
        if normed
        else pl.CostEstimate(
            flops=24 * rows * width * wide, bytes_accessed=1024, transcendentals=0
        ),
    )(source, *[w for w in weights for _ in range(lanes)], *extra)


def settle_kernel(mine_ref, one_ref, far_ref, keep_ref, raw_ref, gain_ref, cos_ref, sin_ref, out_ref):
    head = gain_ref.shape[1]
    total = mine_ref[...] + one_ref[...] * keep_ref[...] + far_ref[...]
    out_ref[:, :head] = norm_rotate_back(
        total[:, :head], raw_ref[...], gain_ref[...], cos_ref[...], sin_ref[...]
    )
    out_ref[:, head:] = total[:, head:]


def settle(mine, one, far, keep, raw, gain, cosine, sine):
    return pl.pallas_call(
        settle_kernel,
        out_shape=jax.ShapeDtypeStruct(mine.shape, jnp.float32),
        compiler_params=pltpu.CompilerParams(vmem_limit_bytes=16 * MIB),
        cost_estimate=SOON,
    )(mine, one, far, keep, raw, gain, cosine, sine)


def flip_kernel(source_ref, out_ref):
    out_ref[...] = source_ref[...].T


def flip(source):
    rows, width = source.shape
    tile = width // 5
    return pl.pallas_call(
        flip_kernel,
        grid=(5,),
        out_shape=jax.ShapeDtypeStruct((width, rows), jnp.float32),
        in_specs=[pl.BlockSpec((rows, tile), lambda k: (0, k))],
        out_specs=pl.BlockSpec((tile, rows), lambda k: (k, 0)),
        compiler_params=pltpu.CompilerParams(vmem_limit_bytes=16 * MIB),
        cost_estimate=SOON,
    )(source)


def turn_kernel(place_ref, others_ref, own_ref, high_ref, low_ref):
    step = pl.program_id(0)

    @pl.when(step < CHAIN - 1)
    def _():
        high_ref[0], low_ref[0] = halves(others_ref[0])

    @pl.when(step == CHAIN - 1)
    def _():
        high_ref[0], low_ref[0] = halves(own_ref[...])


def turn(place, others, own):
    slab, rows = own.shape
    half = jax.ShapeDtypeStruct((CHAIN, slab, rows), jnp.bfloat16)
    out_spec = pl.BlockSpec((1, slab, rows), lambda i, p: ((p[0] + 1 + i) % CHAIN, 0, 0))
    return pl.pallas_call(
        turn_kernel,
        grid_spec=pltpu.PrefetchScalarGridSpec(
            num_scalar_prefetch=1,
            grid=(CHAIN,),
            in_specs=[
                pl.BlockSpec((1, slab, rows), lambda i, p: (jnp.minimum(i, CHAIN - 2), 0, 0)),
                pl.BlockSpec((slab, rows), lambda i, p: (0, 0)),
            ],
            out_specs=[out_spec, out_spec],
        ),
        out_shape=[half, half],
        compiler_params=pltpu.CompilerParams(vmem_limit_bytes=24 * MIB),
        cost_estimate=SOON,
    )(place, others, own)


def product_kernel(place_ref, high_ref, low_ref, *refs):
    blocks, out_ref = refs[:-1], refs[-1]
    total = None
    for hop in range(CHAIN):
        slot = lax.rem(place_ref[0] + (CHAIN - hop), CHAIN)
        term = three((high_ref[slot], low_ref[slot]), halves(blocks[hop][...]), 1, 0)
        total = term if total is None else total + term
    out_ref[...] = total


def product(place, step, turned, blocks, pair):
    high, low = turned
    part = high.shape[1] // pair
    rows = high.shape[2]
    columns = blocks[0].shape[1]
    spec = pl.BlockSpec((CHAIN, part, rows), lambda i, p: (0, (p[1] + step) % pair, 0))
    return pl.pallas_call(
        product_kernel,
        grid_spec=pltpu.PrefetchScalarGridSpec(
            num_scalar_prefetch=1,
            grid=(1,),
            in_specs=[spec, spec] + [pl.BlockSpec(b.shape, lambda i, p: (0, 0)) for b in blocks],
            out_specs=pl.BlockSpec((part, columns), lambda i, p: (0, 0)),
        ),
        out_shape=jax.ShapeDtypeStruct((part, columns), jnp.float32),
        compiler_params=pltpu.CompilerParams(vmem_limit_bytes=28 * MIB),
        cost_estimate=SOON,
    )(place, high, low, *blocks)


def strip_kernel(pieces, strips_ref, *refs):
    weight_refs, left_refs = refs[: len(pieces)], refs[len(pieces) : -1]
    total = None
    left_at = 0
    for ref, (count, start, wide) in zip(weight_refs, pieces):
        for group in range(count):
            left = left_refs[left_at + group][:, start : start + wide]
            right = ref[:, group * wide : (group + 1) * wide]
            term = three(halves(right), halves(left), 1, 1)
            total = term if total is None else total + term
        left_at = left_at if start == 0 and len(pieces) > 1 else left_at + count
    refs[-1][0] = total


def input_strips(strips, strip, weights, lefts, pieces):
    count = strips.shape[0]
    rows = lefts[0].shape[0]
    wide = sum(w.shape[1] for w in weights)
    whole = [pl.BlockSpec(d.shape, lambda i, p: (0, 0)) for d in lefts]
    return pl.pallas_call(
        functools.partial(strip_kernel, pieces),
        grid_spec=pltpu.PrefetchScalarGridSpec(
            num_scalar_prefetch=1,
            grid=(count,),
            in_specs=[pl.BlockSpec((strip, w.shape[1]), lambda i, p: (p[i], 0)) for w in weights]
            + whole,
            out_specs=pl.BlockSpec((1, strip, rows), lambda i, p: (i, 0, 0)),
        ),
        out_shape=jax.ShapeDtypeStruct((count, strip, rows), jnp.float32),
        compiler_params=pltpu.CompilerParams(vmem_limit_bytes=56 * MIB),
        cost_estimate=SOON,
    )(strips, *weights, *lefts)


def local(hidden_in, query_proj, key_proj, value_proj, query_gain, key_gain, segment_ids, grad_out):
    rows_dev, width = hidden_in.shape
    head = query_gain.shape[0]
    kv_local = key_proj.shape[1] // head
    per_kv = query_proj.shape[1] // key_proj.shape[1]
    pair = lax.axis_size("y")
    count = CHAIN * pair
    members = lax.axis_size("tensor")
    member = lax.axis_index("tensor")
    along = lax.axis_index("z")
    across = lax.axis_index("y")
    seq_index = along * pair + across
    reach = (WINDOW - 1) // rows_dev + 1
    span = (reach + 1) * rows_dev
    slab = width // CHAIN
    part = width // count
    piece = slab // members
    groups = range(kv_local)
    short = pair == 2 and reach == 4

    def z_shift(block, step):
        route = [(i, i + step) for i in range(CHAIN) if 0 <= i + step < CHAIN]
        return lax.ppermute(block, "z", route)

    def z_ring(block, step):
        return lax.ppermute(block, "z", [(i, (i + step) % CHAIN) for i in range(CHAIN)])

    def y_ring(block, step):
        return lax.ppermute(block, "y", [(i, (i + step) % pair) for i in range(pair)])

    def shifted(block, distance):
        route = [(i - distance, i) for i in range(count) if 0 <= i - distance < count]
        return lax.ppermute(block, ("z", "y"), route)

    first_row = seq_index * rows_dev
    positions = first_row + jnp.arange(rows_dev, dtype=jnp.int32)
    cosine, sine = rope_tables(positions, head)
    seg_pad = jnp.concatenate([jnp.full((reach * rows_dev,), -1, jnp.int32), segment_ids])
    key_seg = lax.dynamic_slice_in_dim(seg_pad, first_row, span, 0)[:, None]
    query_seg = lax.dynamic_slice_in_dim(segment_ids, first_row, rows_dev, 0)[None, :]

    def q_columns(array, group):
        return array[:, group * per_kv * head : (group + 1) * per_kv * head]

    key_raw, own, two, queries = [], [], [], []
    tables = (key_gain[None, :], cosine, sine)
    for group in groups:
        source = after(hidden_in, own[-1]) if own else hidden_in
        raw, packed = project(source, (key_proj, value_proj), group, head, tables)
        key_raw.append(raw)
        own.append(packed)
        if short:
            two.append(z_shift(own[group], 1))

    def neighbour(group, *earlier):
        block = jnp.where(across == 0, own[group], two[group])
        return y_ring(after(block, *earlier) if earlier else block, 1)

    def farthest(group, four, *earlier):
        back = after(two[group], *earlier)
        return y_ring(jnp.where(across == 0, back, four), 1)

    for group in groups:
        source = after(hidden_in, *own, *queries)
        queries.append(project(source, (query_proj,), group, per_kv * head, ())[0])

    hidden_rows = flip(after(hidden_in, *queries))
    windows, fours, ones = [], [], []
    if short:
        for group in groups:
            ones.append(neighbour(group))
        for group in groups:
            fours.append(z_shift(after(two[group], own[-1], *ones[:group]), 1))
        for group in groups:
            earlier = [w[1] for w in windows]
            three_back = farthest(group, fours[group], *ones, hidden_rows, *earlier)
            windows.append([fours[group], three_back, two[group], ones[group], own[group]])
    else:
        for group in groups:
            windows.append([shifted(own[group], d) for d in range(reach, 0, -1)] + [own[group]])
    pieces = []
    for step in range(CHAIN - 1, 0, -1):
        target = (along + step) % CHAIN
        start = target * slab + member * piece
        pieces.append(z_ring(lax.dynamic_slice_in_dim(hidden_rows, start, piece, 0), step))
    chips = members // CORES
    chip, core = member // CORES, member % CORES

    def to_core(block):
        return lax.ppermute(block, "tensor", [(i, i ^ 1) for i in range(members)])

    def to_chip(block, step):
        route = [(i, (i + step * CORES) % members) for i in range(members)]
        return lax.ppermute(block, "tensor", route)

    def in_order(blocks, index, axis):
        size = blocks[0].shape[axis]
        both = jnp.concatenate(blocks + blocks[:-1], axis=axis)
        start = (len(blocks) - 1 - index) * size
        return lax.dynamic_slice_in_dim(both, start, len(blocks) * size, axis)

    mine = jnp.stack(pieces)
    chip_rows = in_order([to_core(mine), mine], core, 1)
    arrivals = [to_chip(chip_rows, step) for step in range(chips - 1, 0, -1)]
    others = in_order(arrivals + [chip_rows], chip, 1)
    own_slab = lax.dynamic_slice_in_dim(hidden_rows, along * slab, slab, 0)
    place = jnp.stack([along, across]).astype(jnp.int32)
    turned = turn(place, others, own_slab)

    attended, d_query, parts = [], [], []
    for group in groups:
        ready = attended or (pieces + [w[1] for w in windows])
        out, d_q, d_kv = attention(
            after(queries[group], *ready),
            q_columns(grad_out, group),
            query_gain[None, :],
            cosine,
            sine,
            query_seg,
            key_seg,
            windows[group],
            per_kv,
        )
        attended.append(out)
        d_query.append(d_q)
        parts.append(d_kv)

    strip = width // members
    turns = [(chip + step) % chips for step in range(chips)]
    theirs_at = jnp.stack([c * CORES + 1 - core for c in turns]).astype(jnp.int32)
    mine_at = jnp.stack([c * CORES + core for c in turns]).astype(jnp.int32)

    def query_strips(which):
        pieces = ((kv_local, 0, per_kv * head),)
        return input_strips(which, strip, (query_proj,), d_query, pieces)

    def kv_strips(which):
        pieces = ((kv_local, 0, head), (kv_local, head, head))
        return input_strips(which, strip, (key_proj, value_proj), d_kv, pieces)

    def product_of(ring, step):
        return product(place, step, turned, ring, pair)

    def terms(ring):
        return [product_of(ring, step) for step in range(pair - 1, 0, -1)]

    def exchange(sent):
        return [y_ring(term, pair - 1 - i) for i, term in enumerate(sent)]

    sent = []

    def follow(block, send, extra):
        earlier = sent[-2:-1] + list(extra)
        sent.append(send(after(block, *earlier) if earlier else block))
        return sent[-1]

    keep = jnp.where(across == 0, 1.0, 0.0).reshape(1, 1).astype(jnp.float32)
    q_rings = [[d] for d in d_query]
    d_kv, k_rings, held = [], [], []

    def q_hop(group, *extra):
        q_rings[group].append(follow(q_rings[group][-1], lambda b: z_ring(b, 1), extra))

    def k_hop(group, *extra):
        k_rings[group].append(follow(k_rings[group][-1], lambda b: z_ring(b, 1), extra))

    def far_return(group, *extra):
        four, three_back, two_back, one, mine = parts[group]
        from_three = y_ring(three_back, 1)
        from_one = y_ring(one, 1)
        block = four + jnp.where(across == 0, 0.0, from_three)
        got = follow(block, lambda b: z_shift(b, -1), extra)
        held.append((two_back + jnp.where(across == 0, from_three, from_one) + got, from_one))

    def near_return(group, *extra):
        block, from_one = held[group]
        far = follow(block, lambda b: z_shift(b, -1), extra)
        mine = parts[group][-1]
        d_kv.append(settle(mine, from_one, far, keep, key_raw[group], *tables))
        k_rings.append([d_kv[group]])

    if short and kv_local == 2:
        q_hop(0)
        far_return(0, q_rings[0][1])
        q_hop(0)
        near_return(0)
        q_hop(1)
        far_return(1)
        theirs_q = query_strips(theirs_at)
        q_hop(0)
        near_return(1)
        mine_q = query_strips(mine_at)
        q_hop(1, theirs_q)
        k_hop(0, mine_q)
        q_terms = [terms(q_rings[0])]
        q_hop(1, *q_terms[0])
        k_hop(0)
        theirs = theirs_q + kv_strips(theirs_at)
        q_sent = [exchange(q_terms[0])]
        k_hop(1, theirs)
        q_terms.append(terms(q_rings[1]))
        k_hop(0, *q_terms[1])
        sums = mine_q + kv_strips(mine_at)
        k_hop(1, sums, *q_sent[0])
        k_terms = [terms(k_rings[0])]
        q_sent.append(exchange(q_terms[1]))
        k_hop(1, *k_terms[0], *q_sent[1])
        k_terms.append(terms(k_rings[1]))
    else:
        for group in groups:
            mine = parts[group][reach]
            total = jnp.zeros_like(mine)
            for distance in range(1, reach + 1):
                total = total + shifted(parts[group][reach - distance], -distance)
            d_kv.append(settle(mine, mine, total, 0.0 * keep, key_raw[group], *tables))
            k_rings.append([d_kv[group]])
            for _ in range(CHAIN - 1):
                q_hop(group)
            for _ in range(CHAIN - 1):
                k_hop(group)
        theirs = query_strips(theirs_at) + kv_strips(theirs_at)
        sums = query_strips(mine_at) + kv_strips(mine_at)
        q_sent = [exchange(terms(ring)) for ring in q_rings]
        k_terms = [terms(ring) for ring in k_rings]

    sums = sums + to_core(theirs)
    grad_input = sums[0]
    for step in range(1, chips):
        grad_input = grad_input + to_chip(sums[step], step)

    def finish(ring, arrived):
        total = product_of(ring, 0)
        for term in arrived:
            total = total + term
        return total

    grad_query = [finish(ring, arrived) for ring, arrived in zip(q_rings, q_sent)]
    grad_kv = [finish(ring, exchange(term)) for ring, term in zip(k_rings, k_terms)]

    return (
        jnp.concatenate(attended, axis=1),
        grad_input.T,
        jnp.concatenate(grad_query, axis=1),
        jnp.concatenate([g[:, :head] for g in grad_kv], axis=1),
        jnp.concatenate([g[:, head:] for g in grad_kv], axis=1),
    )


def solution(mesh):
    seq, members = mesh.devices.shape
    split = Mesh(mesh.devices.reshape(CHAIN, seq // CHAIN, members), ("z", "y", "tensor"))
    tokens = ("z", "y")
    return jax.shard_map(
        local,
        mesh=split,
        in_specs=(
            P(tokens, None),
            P(None, "tensor"),
            P(None, "tensor"),
            P(None, "tensor"),
            P(),
            P(),
            P(),
            P(tokens, "tensor"),
        ),
        out_specs=(
            P(tokens, "tensor"),
            P(tokens, "tensor"),
            P(tokens, "tensor"),
            P(tokens, "tensor"),
            P(tokens, "tensor"),
        ),
        check_vma=False,
    )
```

profile of v0, /device:TPU:0, one launch (start us, length us, event | category | flops | bytes accessed | tf_op | source)
XLA Modules:
  0.0 350.4 jit_solution(6668491717183194235)
XLA Ops:
  1.9 8.7 %shard_map.119 = (f32[256,256]{1,0:T(8,128)}, f32[256,512]{1,0:T(8,128)}) custom-call(f32[256,3840]{1,0:T(8,128)} %source_ref.5, f32[3840,512]{1,0:T(8,128)} %refs_0_.15, f32[3840,512]{1,0:T(8,128)} %refs_0_.15, f32[3840,512]{1,0:T(8,128)} %refs_0_.15, f32[3840,512]{1,0:T(8,128)} %refs_1_.11, f32[3840,512]{1,0:T(8,128)} %refs_1_.11, f32[3840,512]{1,0:T(8,128)} %refs_1_.11, ...), custom_call_target="tpu_custom_call" | custom-call | flops 1024 | bytes 1024 | tf_op jit(solution)/shard_map/pallas_call | solution.py:200
  10.6 4.9 %collective-permute-start.3 = (f32[256,512]{1,0:T(8,128)}, f32[256,512]{1,0:T(8,128)S(1)}, u32[]{:S(2)}, u32[]{:S(2)}) collective-permute-start(f32[256,512]{1,0:T(8,128)} %get-tuple-element.50.refs_11_), channel_id=1, source_target_pairs={{0,8},{8,16},{16,24},{1,9},{9,17},{17,25},{2,10},{10,18},{18,26},{... | collective-permute-start | bytes 1572872 | tf_op jit(solution)/shard_map/ppermute | solution.py:377
  15.6 8.7 %shard_map.120 = (f32[256,256]{1,0:T(8,128)}, f32[256,512]{1,0:T(8,128)}) custom-call(f32[256,3840]{1,0:T(8,128)} %source_ref.5, f32[3840,512]{1,0:T(8,128)} %refs_0_.15, f32[3840,512]{1,0:T(8,128)} %refs_0_.15, f32[3840,512]{1,0:T(8,128)} %refs_0_.15, f32[3840,512]{1,0:T(8,128)} %refs_1_.11, f32[3840,512]{1,0:T(8,128)} %refs_1_.11, f32[3840,512]{1,0:T(8,128)} %refs_1_.11, ...), custom_call_target="tpu_custom_call" | custom-call | flops 1024 | bytes 1024 | tf_op jit(solution)/shard_map/pallas_call | solution.py:200
  24.3 3.6 %collective-permute-start.5 = (f32[256,512]{1,0:T(8,128)}, f32[256,512]{1,0:T(8,128)S(1)}, u32[]{:S(2)}, u32[]{:S(2)}) collective-permute-start(f32[256,512]{1,0:T(8,128)} %get-tuple-element.52.refs_11_), channel_id=1, source_target_pairs={{0,8},{8,16},{16,24},{1,9},{9,17},{17,25},{2,10},{10,18},{18,26},{... | collective-permute-start | bytes 1572872 | tf_op jit(solution)/shard_map/ppermute | solution.py:377
  27.9 8.2 %shard_map.121.refs_0_ = f32[256,512]{1,0:T(8,128)} custom-call(f32[256,3840]{1,0:T(8,128)} %source_ref.5, f32[3840,1024]{1,0:T(8,128)} %refs_0_.14, f32[3840,1024]{1,0:T(8,128)} %refs_0_.14, f32[3840,1024]{1,0:T(8,128)} %refs_0_.14), custom_call_target="tpu_custom_call" | custom-call | flops 12079595520 | bytes 1024 | tf_op jit(solution)/shard_map/pallas_call | solution.py:200
  38.5 3.5 collective-permute-start.7
  43.4 8.3 %shard_map.122.refs_0_ = f32[256,512]{1,0:T(8,128)} custom-call(f32[256,3840]{1,0:T(8,128)} %source_ref.5, f32[3840,1024]{1,0:T(8,128)} %refs_0_.14, f32[3840,1024]{1,0:T(8,128)} %refs_0_.14, f32[3840,1024]{1,0:T(8,128)} %refs_0_.14), custom_call_target="tpu_custom_call" | custom-call | flops 12079595520 | bytes 1024 | tf_op jit(solution)/shard_map/pallas_call | solution.py:200
  55.3 6.2 %collective-permute-done.6.refs_10_ = f32[256,512]{1,0:T(8,128)S(1)} collective-permute-done((f32[256,512]{1,0:T(8,128)}, f32[256,512]{1,0:T(8,128)S(1)}, u32[]{:S(2)}, u32[]{:S(2)}) %collective-permute-start.6) | collective-permute-done | bytes 524320 | tf_op jit(solution)/shard_map/ppermute | solution.py:383
  63.3 3.5 collective-permute-start.9
  66.8 7.2 %collective-permute-done.8.refs_8_ = f32[256,512]{1,0:T(8,128)S(1)} collective-permute-done((f32[256,512]{1,0:T(8,128)S(1)}, f32[256,512]{1,0:T(8,128)S(1)}, u32[]{:S(2)}, u32[]{:S(2)}) %collective-permute-start.8) | collective-permute-done | bytes 524320 | tf_op jit(solution)/shard_map/ppermute | solution.py:383
  90.7 6.5 %collective-permute-done.1 = f32[240,256]{1,0:T(8,128)} collective-permute-done((f32[240,256]{1,0:T(8,128)}, f32[240,256]{1,0:T(8,128)}, u32[]{:S(2)}, u32[]{:S(2)}) %collective-permute-start.1) | collective-permute-done | bytes 245792 | tf_op jit(solution)/shard_map/ppermute | solution.py:380
  97.3 7.4 %shard_map.124 = (f32[256,512]{1,0:T(8,128)S(1)}, f32[256,512]{1,0:T(8,128)S(1)}, f32[256,512]{1,0:T(8,128)S(1)}, f32[256,512]{1,0:T(8,128)S(1)}, f32[256,512]{1...) custom-call(f32[256,512]{1,0:T(8,128)S(1)} %copy-done.15, f32[256,512]{1,0:T(8,128)S(1)} %get-tuple-element.101.refs_1_, ...), custom_call_target="tpu_custom_call" | custom-call | flops 1024 | bytes 1024 | tf_op jit(solution)/shard_map/pallas_call | solution.py:138
  106.3 5.7 %collective-permute-start.13 = (f32[256,512]{1,0:T(8,128)S(1)}, f32[256,512]{1,0:T(8,128)S(1)}, u32[]{:S(2)}, u32[]{:S(2)}) collective-permute-start(f32[256,512]{1,0:T(8,128)S(1)} %get-tuple-element.64.refs_1_.refs_0_), channel_id=1, source_target_pairs={{0,8},{8,16},{16,24},{24,0},{1,9},{9,17},{17,25},{25,1},{2,10},{10... | collective-permute-start | bytes 1572872 | tf_op jit(solution)/shard_map/ppermute | solution.py:380
  112.6 7.0 %collective-permute-done.12 = f32[256,512]{1,0:T(8,128)S(1)} collective-permute-done((f32[256,512]{1,0:T(8,128)S(1)}, f32[256,512]{1,0:T(8,128)S(1)}, u32[]{:S(2)}, u32[]{:S(2)}) %collective-permute-start.12) | collective-permute-done | bytes 524320 | tf_op jit(solution)/shard_map/ppermute | solution.py:383
  124.7 8.5 %shard_map.125 = (f32[256,512]{1,0:T(8,128)S(1)}, f32[256,512]{1,0:T(8,128)S(1)}, f32[256,512]{1,0:T(8,128)S(1)}, f32[256,512]{1,0:T(8,128)S(1)}, f32[256,512]{1...) custom-call(f32[256,512]{1,0:T(8,128)S(1)} %copy-done.14, f32[256,512]{1,0:T(8,128)S(1)} %get-tuple-element.100.refs_1_, ...), custom_call_target="tpu_custom_call" | custom-call | flops 1024 | bytes 1024 | tf_op jit(solution)/shard_map/pallas_call | solution.py:138
  133.7 4.7 %collective-permute-done.14 = f32[256,512]{1,0:T(8,128)S(1)} collective-permute-done((f32[256,512]{1,0:T(8,128)S(1)}, f32[256,512]{1,0:T(8,128)S(1)}, u32[]{:S(2)}, u32[]{:S(2)}) %collective-permute-start.14) | collective-permute-done | bytes 524320 | tf_op jit(solution)/shard_map/ppermute | solution.py:377
  140.8 7.3 %collective-permute-done.17 = f32[256,512]{1,0:T(8,128)S(1)} collective-permute-done((f32[256,512]{1,0:T(8,128)S(1)}, f32[256,512]{1,0:T(8,128)S(1)}, u32[]{:S(2)}, u32[]{:S(2)}) %collective-permute-start.17) | collective-permute-done | bytes 524320 | tf_op jit(solution)/shard_map/ppermute | solution.py:383
  148.2 4.4 %collective-permute-done.15.far_ref = f32[256,512]{1,0:T(8,128)S(1)} collective-permute-done((f32[256,512]{1,0:T(8,128)S(1)}, f32[256,512]{1,0:T(8,128)S(1)}, u32[]{:S(2)}, u32[]{:S(2)}) %collective-permute-start.15) | collective-permute-done | bytes 524320 | tf_op jit(solution)/shard_map/ppermute | solution.py:377
  158.7 9.4 %collective-permute-done.18 = f32[256,512]{1,0:T(8,128)S(1)} collective-permute-done((f32[256,512]{1,0:T(8,128)S(1)}, f32[256,512]{1,0:T(8,128)S(1)}, u32[]{:S(2)}, u32[]{:S(2)}) %collective-permute-start.18) | collective-permute-done | bytes 524320 | tf_op jit(solution)/shard_map/ppermute | solution.py:377
  174.9 7.0 %collective-permute-done.24.refs_2_ = f32[256,512]{1,0:T(8,128)S(1)} collective-permute-done((f32[256,512]{1,0:T(8,128)S(1)}, f32[256,512]{1,0:T(8,128)S(1)}, u32[]{:S(2)}, u32[]{:S(2)}) %collective-permute-start.24) | collective-permute-done | bytes 524320 | tf_op jit(solution)/shard_map/ppermute | solution.py:380
  192.7 7.5 %shard_map.130 = f32[2,960,256]{2,1,0:T(8,128)} custom-call(s32[2]{0:T(128)} %pad_add_fusion.1.strips_ref, f32[3840,1024]{1,0:T(8,128)} %refs_0_.14, f32[256,512]{1,0:T(8,128)} %copy-done.7, f32[256,512]{1,0:T(8,128)} %copy-done.9), custom_call_target="tpu_custom_call" | custom-call | flops 1024 | bytes 1024 | tf_op jit(solution)/shard_map/pallas_call | solution.py:340
  200.2 7.7 %shard_map.131 = f32[2,960,256]{2,1,0:T(8,128)} custom-call(s32[2]{0:T(128)} %pad_add_fusion.1.strips_ref, f32[3840,512]{1,0:T(8,128)} %refs_0_.15, f32[3840,512]{1,0:T(8,128)} %refs_1_.11, f32[256,512]{1,0:T(8,128)} %copy-done.4, f32[256,512]{1,0:T(8,128)} %copy-done.1), custom_call_target="tpu_custom_call" | custom-call | flops 1024 | bytes 1024 | tf_op jit(solution)/shard_map/pallas_call | solution.py:340
  212.8 14.3 %collective-permute-done.26.refs_3_ = f32[256,512]{1,0:T(8,128)S(1)} collective-permute-done((f32[256,512]{1,0:T(8,128)S(1)}, f32[256,512]{1,0:T(8,128)S(1)}, u32[]{:S(2)}, u32[]{:S(2)}) %collective-permute-start.26) | collective-permute-done | bytes 524320 | tf_op jit(solution)/shard_map/ppermute | solution.py:380
  227.8 7.7 %shard_map.126 = f32[2,960,256]{2,1,0:T(8,128)} custom-call(s32[2]{0:T(128)} %pad_add_fusion.strips_ref, f32[3840,1024]{1,0:T(8,128)} %refs_0_.14, f32[256,512]{1,0:T(8,128)} %copy-done.7, f32[256,512]{1,0:T(8,128)} %copy-done.9), custom_call_target="tpu_custom_call" | custom-call | flops 1024 | bytes 1024 | tf_op jit(solution)/shard_map/pallas_call | solution.py:340
  246.2 8.9 %collective-permute-done.31.refs_1_ = f32[256,512]{1,0:T(8,128)} collective-permute-done((f32[256,512]{1,0:T(8,128)S(1)}, f32[256,512]{1,0:T(8,128)}, u32[]{:S(2)}, u32[]{:S(2)}) %collective-permute-start.31) | collective-permute-done | bytes 524320 | tf_op jit(solution)/shard_map/ppermute | solution.py:380
  255.1 11.1 %collective-permute-done.29.refs_3_ = f32[256,512]{1,0:T(8,128)S(1)} collective-permute-done((f32[256,512]{1,0:T(8,128)}, f32[256,512]{1,0:T(8,128)S(1)}, u32[]{:S(2)}, u32[]{:S(2)}) %collective-permute-start.29) | collective-permute-done | bytes 524320 | tf_op jit(solution)/shard_map/ppermute | solution.py:380
  266.2 4.4 %shard_map.136 = f32[480,512]{1,0:T(8,128)} custom-call(s32[2]{0:T(128)S(1)} %pad_add_fusion.2.place_ref, bf16[4,960,256]{2,1,0:T(8,128)(2,1)S(1)} %get-tuple-element.82.high_ref, bf16[4,960,256]{2,1,0:T(8,128)(2,1)S(1)} %get-tuple-element.83.low_ref, f32[256,512]{1,0:T(8,128)S(1)} %copy-done.10, f32[256,512]{1,0:T(8,128)S(1)} %collective-permute-done.25.refs_1_, ...), custom_call_target="tpu_custom_call" | custom-call | flops 1024 | bytes 1024 | tf_op jit(solution)/shard_map/pallas_call | solution.py:307
  270.6 7.5 %shard_map.129 = f32[2,960,256]{2,1,0:T(8,128)} custom-call(s32[2]{0:T(128)} %pad_add_fusion.strips_ref, f32[3840,512]{1,0:T(8,128)} %refs_0_.15, f32[3840,512]{1,0:T(8,128)} %refs_1_.11, f32[256,512]{1,0:T(8,128)} %copy-done.4, f32[256,512]{1,0:T(8,128)} %copy-done.1), custom_call_target="tpu_custom_call" | custom-call | flops 1024 | bytes 1024 | tf_op jit(solution)/shard_map/pallas_call | solution.py:340
  281.6 7.1 %collective-permute-done.35.refs_1_ = f32[256,512]{1,0:T(8,128)S(1)} collective-permute-done((f32[256,512]{1,0:T(8,128)S(1)}, f32[256,512]{1,0:T(8,128)S(1)}, u32[]{:S(2)}, u32[]{:S(2)}) %collective-permute-start.35) | collective-permute-done | bytes 524320 | tf_op jit(solution)/shard_map/ppermute | solution.py:380
  288.9 11.0 %collective-permute-done.33.refs_3_ = f32[256,512]{1,0:T(8,128)S(1)} collective-permute-done((f32[256,512]{1,0:T(8,128)}, f32[256,512]{1,0:T(8,128)S(1)}, u32[]{:S(2)}, u32[]{:S(2)}) %collective-permute-start.33) | collective-permute-done | bytes 524320 | tf_op jit(solution)/shard_map/ppermute | solution.py:380
  303.5 6.4 %collective-permute-done.36.refs_2_ = f32[256,512]{1,0:T(8,128)S(1)} collective-permute-done((f32[256,512]{1,0:T(8,128)S(1)}, f32[256,512]{1,0:T(8,128)S(1)}, u32[]{:S(2)}, u32[]{:S(2)}) %collective-permute-start.36) | collective-permute-done | bytes 524320 | tf_op jit(solution)/shard_map/ppermute | solution.py:380
  311.6 12.8 %collective-permute-done.37.refs_3_ = f32[256,512]{1,0:T(8,128)S(1)} collective-permute-done((f32[256,512]{1,0:T(8,128)S(1)}, f32[256,512]{1,0:T(8,128)S(1)}, u32[]{:S(2)}, u32[]{:S(2)}) %collective-permute-start.37) | collective-permute-done | bytes 524320 | tf_op jit(solution)/shard_map/ppermute | solution.py:380
  (192 shorter events, 111.4 us)
Async XLA Ops:
  10.6 25.5 %collective-permute-start.3 = (f32[256,512]{1,0:T(8,128)}, f32[256,512]{1,0:T(8,128)S(1)}, u32[]{:S(2)}, u32[]{:S(2)}) collective-permute-start(f32[256,512]{1,0:T(8,128)} %get-tuple-element.50.refs_11_), channel_id=1, source_target_pairs={{0,8},{8,16},{16,24},{1,9},{9,17},{17,25},{2,10},{10,18},{18,26},{... | collective-permute-start | bytes 1572872 | tf_op jit(solution)/shard_map/ppermute | solution.py:377
  24.3 17.7 %collective-permute-start.5 = (f32[256,512]{1,0:T(8,128)}, f32[256,512]{1,0:T(8,128)S(1)}, u32[]{:S(2)}, u32[]{:S(2)}) collective-permute-start(f32[256,512]{1,0:T(8,128)} %get-tuple-element.52.refs_11_), channel_id=1, source_target_pairs={{0,8},{8,16},{16,24},{1,9},{9,17},{17,25},{2,10},{10,18},{18,26},{... | collective-permute-start | bytes 1572872 | tf_op jit(solution)/shard_map/ppermute | solution.py:377
  37.0 18.3 %collective-permute-start.4 = (f32[256,512]{1,0:T(8,128)}, f32[256,512]{1,0:T(8,128)S(1)}, u32[]{:S(2)}, u32[]{:S(2)}) collective-permute-start(f32[256,512]{1,0:T(8,128)} %broadcast_select_fusion.3), channel_id=1, source_target_pairs={{0,4},{4,0},{1,5},{5,1},{2,6},{6,2},{3,7},{7,3},{8,12},{12,8},{9,1... | collective-permute-start | bytes 1572872 | tf_op jit(solution)/shard_map/ppermute | solution.py:383
  38.5 23.0 %collective-permute-start.7 = (f32[256,512]{1,0:T(8,128)S(1)}, f32[256,512]{1,0:T(8,128)S(1)}, u32[]{:S(2)}, u32[]{:S(2)}) collective-permute-start(f32[256,512]{1,0:T(8,128)S(1)} %collective-permute-done.3.refs_9_), channel_id=1, source_target_pairs={{0,8},{8,16},{16,24},{1,9},{9,17},{17,25},{2,10},{10,18},{18,26},{... | collective-permute-start | bytes 1572872 | tf_op jit(solution)/shard_map/ppermute | solution.py:377
  42.9 18.7 %collective-permute-start.6 = (f32[256,512]{1,0:T(8,128)}, f32[256,512]{1,0:T(8,128)S(1)}, u32[]{:S(2)}, u32[]{:S(2)}) collective-permute-start(f32[256,512]{1,0:T(8,128)} %broadcast_select_fusion.2), channel_id=1, source_target_pairs={{0,4},{4,0},{1,5},{5,1},{2,6},{6,2},{3,7},{7,3},{8,12},{12,8},{9,1... | collective-permute-start | bytes 1572872 | tf_op jit(solution)/shard_map/ppermute | solution.py:383
  77.0 20.2 %collective-permute-start.10 = (f32[256,512]{1,0:T(8,128)}, f32[256,512]{1,0:T(8,128)}, u32[]{:S(2)}, u32[]{:S(2)}) collective-permute-start(f32[256,512]{1,0:T(8,128)} %broadcast_select_fusion), channel_id=1, source_target_pairs={{0,4},{4,0},{1,5},{5,1},{2,6},{6,2},{3,7},{7,3},{8,12},{12,8},{9,1... | collective-permute-start | bytes 1572872 | tf_op jit(solution)/shard_map/ppermute | solution.py:383
  82.2 15.0 %collective-permute-start.1 = (f32[240,256]{1,0:T(8,128)}, f32[240,256]{1,0:T(8,128)}, u32[]{:S(2)}, u32[]{:S(2)}) collective-permute-start(f32[240,256]{1,0:T(8,128)} %get-tuple-element.98), channel_id=1, source_target_pairs={{0,16},{8,24},{16,0},{24,8},{1,17},{9,25},{17,1},{25,9},{2,18},{10... | collective-permute-start | bytes 737288 | tf_op jit(solution)/shard_map/ppermute | solution.py:380
  104.7 14.9 %collective-permute-start.12 = (f32[256,512]{1,0:T(8,128)S(1)}, f32[256,512]{1,0:T(8,128)S(1)}, u32[]{:S(2)}, u32[]{:S(2)}) collective-permute-start(f32[256,512]{1,0:T(8,128)S(1)} %get-tuple-element.69), channel_id=1, source_target_pairs={{0,4},{4,0},{1,5},{5,1},{2,6},{6,2},{3,7},{7,3},{8,12},{12,8},{9,1... | collective-permute-start | bytes 1572872 | tf_op jit(solution)/shard_map/ppermute | solution.py:383
  106.3 16.8 %collective-permute-start.13 = (f32[256,512]{1,0:T(8,128)S(1)}, f32[256,512]{1,0:T(8,128)S(1)}, u32[]{:S(2)}, u32[]{:S(2)}) collective-permute-start(f32[256,512]{1,0:T(8,128)S(1)} %get-tuple-element.64.refs_1_.refs_0_), channel_id=1, source_target_pairs={{0,8},{8,16},{16,24},{24,0},{1,9},{9,17},{17,25},{25,1},{2,10},{10... | collective-permute-start | bytes 1572872 | tf_op jit(solution)/shard_map/ppermute | solution.py:380
  112.1 21.6 %collective-permute-start.11 = (f32[256,512]{1,0:T(8,128)S(1)}, f32[256,512]{1,0:T(8,128)S(1)}, u32[]{:S(2)}, u32[]{:S(2)}) collective-permute-start(f32[256,512]{1,0:T(8,128)S(1)} %get-tuple-element.67), channel_id=1, source_target_pairs={{0,4},{4,0},{1,5},{5,1},{2,6},{6,2},{3,7},{7,3},{8,12},{12,8},{9,1... | collective-permute-start | bytes 1572872 | tf_op jit(solution)/shard_map/ppermute | solution.py:383
  123.2 15.3 %collective-permute-start.14 = (f32[256,512]{1,0:T(8,128)S(1)}, f32[256,512]{1,0:T(8,128)S(1)}, u32[]{:S(2)}, u32[]{:S(2)}) collective-permute-start(f32[256,512]{1,0:T(8,128)S(1)} %select_add_fusion.1), channel_id=1, source_target_pairs={{8,0},{16,8},{24,16},{9,1},{17,9},{25,17},{10,2},{18,10},{26,18},{... | collective-permute-start | bytes 1572872 | tf_op jit(solution)/shard_map/ppermute | solution.py:377
  133.2 14.9 %collective-permute-start.17 = (f32[256,512]{1,0:T(8,128)S(1)}, f32[256,512]{1,0:T(8,128)S(1)}, u32[]{:S(2)}, u32[]{:S(2)}) collective-permute-start(f32[256,512]{1,0:T(8,128)S(1)} %get-tuple-element.77), channel_id=1, source_target_pairs={{0,4},{4,0},{1,5},{5,1},{2,6},{6,2},{3,7},{7,3},{8,12},{12,8},{9,1... | collective-permute-start | bytes 1572872 | tf_op jit(solution)/shard_map/ppermute | solution.py:383
  140.0 18.7 %collective-permute-start.16 = (f32[256,512]{1,0:T(8,128)S(1)}, f32[256,512]{1,0:T(8,128)S(1)}, u32[]{:S(2)}, u32[]{:S(2)}) collective-permute-start(f32[256,512]{1,0:T(8,128)S(1)} %get-tuple-element.75), channel_id=1, source_target_pairs={{0,4},{4,0},{1,5},{5,1},{2,6},{6,2},{3,7},{7,3},{8,12},{12,8},{9,1... | collective-permute-start | bytes 1572872 | tf_op jit(solution)/shard_map/ppermute | solution.py:383
  152.6 15.5 %collective-permute-start.18 = (f32[256,512]{1,0:T(8,128)S(1)}, f32[256,512]{1,0:T(8,128)S(1)}, u32[]{:S(2)}, u32[]{:S(2)}) collective-permute-start(f32[256,512]{1,0:T(8,128)S(1)} %select_add_fusion), channel_id=1, source_target_pairs={{8,0},{16,8},{24,16},{9,1},{17,9},{25,17},{10,2},{18,10},{26,18},{... | collective-permute-start | bytes 1572872 | tf_op jit(solution)/shard_map/ppermute | solution.py:377
  156.0 25.9 %collective-permute-start.24 = (f32[256,512]{1,0:T(8,128)S(1)}, f32[256,512]{1,0:T(8,128)S(1)}, u32[]{:S(2)}, u32[]{:S(2)}) collective-permute-start(f32[256,512]{1,0:T(8,128)S(1)} %collective-permute-done.13.refs_1_), channel_id=1, source_target_pairs={{0,8},{8,16},{16,24},{24,0},{1,9},{9,17},{17,25},{25,1},{2,10},{10... | collective-permute-start | bytes 1572872 | tf_op jit(solution)/shard_map/ppermute | solution.py:380
  169.1 21.4 %collective-permute-start.19 = (f32[256,512]{1,0:T(8,128)}, f32[256,512]{1,0:T(8,128)}, u32[]{:S(2)}, u32[]{:S(2)}) collective-permute-start(f32[256,512]{1,0:T(8,128)} %add_add_fusion), channel_id=1, source_target_pairs={{8,0},{16,8},{24,16},{9,1},{17,9},{25,17},{10,2},{18,10},{26,18},{... | collective-permute-start | bytes 1572872 | tf_op jit(solution)/shard_map/ppermute | solution.py:377
  173.4 65.5 %collective-permute-start.23 = (f32[3,480,256]{2,1,0:T(8,128)}, f32[3,480,256]{2,1,0:T(8,128)}, u32[]{:S(2)}, u32[]{:S(2)}) collective-permute-start(f32[3,480,256]{2,1,0:T(8,128)} %fusion.3), channel_id=1, source_target_pairs={{0,2},{1,3},{2,0},{3,1},{4,6},{5,7},{6,4},{7,5},{8,10},{9,11},{10,... | collective-permute-start | bytes 4423688 | tf_op jit(solution)/shard_map/ppermute | solution.py:448
  181.9 29.1 %collective-permute-start.25 = (f32[256,512]{1,0:T(8,128)S(1)}, f32[256,512]{1,0:T(8,128)S(1)}, u32[]{:S(2)}, u32[]{:S(2)}) collective-permute-start(f32[256,512]{1,0:T(8,128)S(1)} %get-tuple-element.85.refs_2_.refs_0_), channel_id=1, source_target_pairs={{0,8},{8,16},{16,24},{24,0},{1,9},{9,17},{17,25},{25,1},{2,10},{10... | collective-permute-start | bytes 1572872 | tf_op jit(solution)/shard_map/ppermute | solution.py:380
  211.0 67.5 %collective-permute-start.20 = (f32[2,960,256]{2,1,0:T(8,128)}, f32[2,960,256]{2,1,0:T(8,128)}, u32[]{:S(2)}, u32[]{:S(2)}) collective-permute-start(f32[2,960,256]{2,1,0:T(8,128)} %add.166), channel_id=1, source_target_pairs={{0,1},{1,0},{2,3},{3,2},{4,5},{5,4},{6,7},{7,6},{8,9},{9,8},{10,11... | collective-permute-start | bytes 5898248 | tf_op jit(solution)/shard_map/ppermute | solution.py:444
  211.0 16.1 %collective-permute-start.26 = (f32[256,512]{1,0:T(8,128)S(1)}, f32[256,512]{1,0:T(8,128)S(1)}, u32[]{:S(2)}, u32[]{:S(2)}) collective-permute-start(f32[256,512]{1,0:T(8,128)S(1)} %collective-permute-done.24.refs_2_), channel_id=1, source_target_pairs={{0,8},{8,16},{16,24},{24,0},{1,9},{9,17},{17,25},{25,1},{2,10},{10... | collective-permute-start | bytes 1572872 | tf_op jit(solution)/shard_map/ppermute | solution.py:380
  227.1 18.7 %collective-permute-start.28 = (f32[256,512]{1,0:T(8,128)S(1)}, f32[256,512]{1,0:T(8,128)}, u32[]{:S(2)}, u32[]{:S(2)}) collective-permute-start(f32[256,512]{1,0:T(8,128)S(1)} %collective-permute-done.25.refs_1_), channel_id=1, source_target_pairs={{0,8},{8,16},{16,24},{24,0},{1,9},{9,17},{17,25},{25,1},{2,10},{10... | collective-permute-start | bytes 1572872 | tf_op jit(solution)/shard_map/ppermute | solution.py:380
  235.5 19.6 %collective-permute-start.31 = (f32[256,512]{1,0:T(8,128)S(1)}, f32[256,512]{1,0:T(8,128)}, u32[]{:S(2)}, u32[]{:S(2)}) collective-permute-start(f32[256,512]{1,0:T(8,128)S(1)} %copy-done.5), channel_id=1, source_target_pairs={{0,8},{8,16},{16,24},{24,0},{1,9},{9,17},{17,25},{25,1},{2,10},{10... | collective-permute-start | bytes 1572872 | tf_op jit(solution)/shard_map/ppermute | solution.py:380
  245.8 20.4 %collective-permute-start.29 = (f32[256,512]{1,0:T(8,128)}, f32[256,512]{1,0:T(8,128)S(1)}, u32[]{:S(2)}, u32[]{:S(2)}) collective-permute-start(f32[256,512]{1,0:T(8,128)} %collective-permute-done.28.refs_2_), channel_id=1, source_target_pairs={{0,8},{8,16},{16,24},{24,0},{1,9},{9,17},{17,25},{25,1},{2,10},{10... | collective-permute-start | bytes 1572872 | tf_op jit(solution)/shard_map/ppermute | solution.py:380
  246.1 35.5 %collective-permute-start.27 = (f32[480,512]{1,0:T(8,128)}, f32[480,512]{1,0:T(8,128)}, u32[]{:S(2)}, u32[]{:S(2)}) collective-permute-start(f32[480,512]{1,0:T(8,128)} %shard_map.134), channel_id=1, source_target_pairs={{0,4},{4,0},{1,5},{5,1},{2,6},{6,2},{3,7},{7,3},{8,12},{12,8},{9,1... | collective-permute-start | bytes 2949128 | tf_op jit(solution)/shard_map/ppermute | solution.py:383
  255.1 23.1 %collective-permute-start.32 = (f32[256,512]{1,0:T(8,128)}, f32[256,512]{1,0:T(8,128)}, u32[]{:S(2)}, u32[]{:S(2)}) collective-permute-start(f32[256,512]{1,0:T(8,128)} %collective-permute-done.31.refs_1_), channel_id=1, source_target_pairs={{0,8},{8,16},{16,24},{24,0},{1,9},{9,17},{17,25},{25,1},{2,10},{10... | collective-permute-start | bytes 1572872 | tf_op jit(solution)/shard_map/ppermute | solution.py:380
  266.2 22.5 %collective-permute-start.35 = (f32[256,512]{1,0:T(8,128)S(1)}, f32[256,512]{1,0:T(8,128)S(1)}, u32[]{:S(2)}, u32[]{:S(2)}) collective-permute-start(f32[256,512]{1,0:T(8,128)S(1)} %copy-done.2), channel_id=1, source_target_pairs={{0,8},{8,16},{16,24},{24,0},{1,9},{9,17},{17,25},{25,1},{2,10},{10... | collective-permute-start | bytes 1572872 | tf_op jit(solution)/shard_map/ppermute | solution.py:380
  270.6 32.9 %collective-permute-start.30 = (f32[480,512]{1,0:T(8,128)}, f32[480,512]{1,0:T(8,128)}, u32[]{:S(2)}, u32[]{:S(2)}) collective-permute-start(f32[480,512]{1,0:T(8,128)} %shard_map.136), channel_id=1, source_target_pairs={{0,4},{4,0},{1,5},{5,1},{2,6},{6,2},{3,7},{7,3},{8,12},{12,8},{9,1... | collective-permute-start | bytes 2949128 | tf_op jit(solution)/shard_map/ppermute | solution.py:383
  278.2 21.8 %collective-permute-start.33 = (f32[256,512]{1,0:T(8,128)}, f32[256,512]{1,0:T(8,128)S(1)}, u32[]{:S(2)}, u32[]{:S(2)}) collective-permute-start(f32[256,512]{1,0:T(8,128)} %collective-permute-done.32.refs_2_), channel_id=1, source_target_pairs={{0,8},{8,16},{16,24},{24,0},{1,9},{9,17},{17,25},{25,1},{2,10},{10... | collective-permute-start | bytes 1572872 | tf_op jit(solution)/shard_map/ppermute | solution.py:380
  288.7 21.2 %collective-permute-start.36 = (f32[256,512]{1,0:T(8,128)S(1)}, f32[256,512]{1,0:T(8,128)S(1)}, u32[]{:S(2)}, u32[]{:S(2)}) collective-permute-start(f32[256,512]{1,0:T(8,128)S(1)} %collective-permute-done.35.refs_1_), channel_id=1, source_target_pairs={{0,8},{8,16},{16,24},{24,0},{1,9},{9,17},{17,25},{25,1},{2,10},{10... | collective-permute-start | bytes 1572872 | tf_op jit(solution)/shard_map/ppermute | solution.py:380
  303.4 37.9 %collective-permute-start.34 = (f32[480,512]{1,0:T(8,128)S(1)}, f32[480,512]{1,0:T(8,128)S(1)}, u32[]{:S(2)}, u32[]{:S(2)}) collective-permute-start(f32[480,512]{1,0:T(8,128)S(1)} %shard_map.138), channel_id=1, source_target_pairs={{0,4},{4,0},{1,5},{5,1},{2,6},{6,2},{3,7},{7,3},{8,12},{12,8},{9,1... | collective-permute-start | bytes 2949128 | tf_op jit(solution)/shard_map/ppermute | solution.py:383
  310.0 31.6 %collective-permute-start.21 = (f32[960,256]{1,0:T(8,128)S(1)}, f32[960,256]{1,0:T(8,128)S(1)}, u32[]{:S(2)}, u32[]{:S(2)}) collective-permute-start(f32[960,256]{1,0:T(8,128)S(1)} %slice_bitcast_fusion), channel_id=1, source_target_pairs={{0,2},{1,3},{2,0},{3,1},{4,6},{5,7},{6,4},{7,5},{8,10},{9,11},{10,... | collective-permute-start | bytes 2949128 | tf_op jit(solution)/shard_map/ppermute | solution.py:448
  326.7 21.6 %collective-permute-start.38 = (f32[480,512]{1,0:T(8,128)S(1)}, f32[480,512]{1,0:T(8,128)S(1)}, u32[]{:S(2)}, u32[]{:S(2)}) collective-permute-start(f32[480,512]{1,0:T(8,128)S(1)} %shard_map.140), channel_id=1, source_target_pairs={{0,4},{4,0},{1,5},{5,1},{2,6},{6,2},{3,7},{7,3},{8,12},{12,8},{9,1... | collective-permute-start | bytes 2949128 | tf_op jit(solution)/shard_map/ppermute | solution.py:383
  (51 other events, 687.9 us)
where the time goes:
time: 356 us; the launch traced here: 350 us
  waiting for transfers between devices  147 us (41%)
  Pallas kernels  110 us (31%)
  starting transfers between devices  51 us (14%)
  other arithmetic  28.7 us (8%)
  local copies, waits for them, and re-layouts  12.8 us (4%)
    ppermute x15, waiting for transfers between devices, z_ring(): lax.ppermute(block, 'z', [(i, (i + step) % CHAIN) for i in range(CHAIN)])  92 us
    pallas_call x4, Pallas kernels, project(): pl.pallas_call(functools.partial(project_kernel, normed, lanes), grid=(st...  34 us
    ppermute x12, waiting for transfers between devices, y_ring(): lax.ppermute(block, 'y', [(i, (i + step) % pair) for i in range(pair)])  31.1 us
    pallas_call x4, Pallas kernels, input_strips(): pl.pallas_call(functools.partial(strip_kernel, pieces), grid_spec=pltpu.P...  30.4 us
    pallas_call x8, Pallas kernels, product(): pl.pallas_call(product_kernel, grid_spec=pltpu.PrefetchScalarGridSpec(num...  24.8 us
    ppermute x8, waiting for transfers between devices, z_shift(): return lax.ppermute(block, 'z', route)  23.5 us
    ppermute x8, starting transfers between devices, z_shift(): return lax.ppermute(block, 'z', route)  21 us
    ppermute x15, starting transfers between devices, z_ring(): lax.ppermute(block, 'z', [(i, (i + step) % CHAIN) for i in range(CHAIN)])  19.2 us
  transfers between devices with their start and end apart: 39, of which 21 were waited for; matrix products, arithmetic and copies ran while one was open for 9% of the time, Pallas kernels for 27%

commit v1 on v0

--- a/solution.py
+++ b/solution.py
@@ -288,24 +288,29 @@
     )(place, others, own)
 
 
-def product_kernel(place_ref, high_ref, low_ref, *refs):
+def product_kernel(start, place_ref, high_ref, low_ref, *refs):
     blocks, out_ref = refs[:-1], refs[-1]
     total = None
     for hop in range(CHAIN):
         slot = lax.rem(place_ref[0] + (CHAIN - hop), CHAIN)
-        term = three((high_ref[slot], low_ref[slot]), halves(blocks[hop][...]), 1, 0)
+        block = blocks[hop]
+        if block.shape[1] == out_ref.shape[1]:
+            block = block[...]
+        else:
+            block = block[:, start : start + out_ref.shape[1]]
+        term = three((high_ref[slot], low_ref[slot]), halves(block), 1, 0)
         total = term if total is None else total + term
     out_ref[...] = total
 
 
-def product(place, step, turned, blocks, pair):
+def product(place, step, turned, blocks, pair, span):
     high, low = turned
     part = high.shape[1] // pair
     rows = high.shape[2]
-    columns = blocks[0].shape[1]
+    columns = span[1] or blocks[0].shape[1]
     spec = pl.BlockSpec((CHAIN, part, rows), lambda i, p: (0, (p[1] + step) % pair, 0))
     return pl.pallas_call(
-        product_kernel,
+        functools.partial(product_kernel, span[0]),
         grid_spec=pltpu.PrefetchScalarGridSpec(
             num_scalar_prefetch=1,
             grid=(1,),
@@ -424,10 +429,9 @@
         for group in groups:
             ones.append(neighbour(group))
         for group in groups:
-            fours.append(z_shift(after(two[group], own[-1], *ones[:group]), 1))
+            fours.append(z_shift(after(two[group], own[-1]), 1))
         for group in groups:
-            earlier = [w[1] for w in windows]
-            three_back = farthest(group, fours[group], *ones, hidden_rows, *earlier)
+            three_back = farthest(group, fours[group], *ones, *fours, hidden_rows)
             windows.append([fours[group], three_back, two[group], ones[group], own[group]])
     else:
         for group in groups:
@@ -463,7 +467,7 @@
 
     attended, d_query, parts = [], [], []
     for group in groups:
-        ready = attended or (pieces + [w[1] for w in windows])
+        ready = attended or pieces
         out, d_q, d_kv = attention(
             after(queries[group], *ready),
             q_columns(grad_out, group),
@@ -492,11 +496,11 @@
         pieces = ((kv_local, 0, head), (kv_local, head, head))
         return input_strips(which, strip, (key_proj, value_proj), d_kv, pieces)
 
-    def product_of(ring, step):
-        return product(place, step, turned, ring, pair)
-
-    def terms(ring):
-        return [product_of(ring, step) for step in range(pair - 1, 0, -1)]
+    def product_of(ring, step, span=(0, 0)):
+        return product(place, step, turned, ring, pair, span)
+
+    def terms(ring, span=(0, 0)):
+        return [product_of(ring, step, span) for step in range(pair - 1, 0, -1)]
 
     def exchange(sent):
         return [y_ring(term, pair - 1 - i) for i, term in enumerate(sent)]
@@ -535,17 +539,17 @@
 
     if short and kv_local == 2:
         q_hop(0)
-        far_return(0, q_rings[0][1])
+        far_return(0, q_rings[0][1], *attended)
         q_hop(0)
-        near_return(0)
+        near_return(0, q_rings[0][2])
         q_hop(1)
-        far_return(1)
         theirs_q = query_strips(theirs_at)
+        far_return(1, theirs_q, q_rings[1][1])
         q_hop(0)
-        near_return(1)
         mine_q = query_strips(mine_at)
-        q_hop(1, theirs_q)
-        k_hop(0, mine_q)
+        q_hop(1)
+        near_return(1, mine_q, q_rings[0][3])
+        k_hop(0)
         q_terms = [terms(q_rings[0])]
         q_hop(1, *q_terms[0])
         k_hop(0)
@@ -558,8 +562,10 @@
         k_hop(1, sums, *q_sent[0])
         k_terms = [terms(k_rings[0])]
         q_sent.append(exchange(q_terms[1]))
-        k_hop(1, *k_terms[0], *q_sent[1])
-        k_terms.append(terms(k_rings[1]))
+        last = after(k_rings[1][-1], sent[-2], *k_terms[0], *q_sent[1])
+        tails = [z_ring(last[:, head:], 1), z_ring(last[:, :head], 1)]
+        tail_rings = [k_rings[1] + [tail] for tail in tails]
+        tail_spans = [(head, head), (0, head)]
     else:
         for group in groups:
             mine = parts[group][reach]
@@ -575,21 +581,25 @@
         theirs = query_strips(theirs_at) + kv_strips(theirs_at)
         sums = query_strips(mine_at) + kv_strips(mine_at)
         q_sent = [exchange(terms(ring)) for ring in q_rings]
-        k_terms = [terms(ring) for ring in k_rings]
+        k_terms = [terms(ring) for ring in k_rings[:-1]]
+        tail_rings, tail_spans = [k_rings[-1]], [(0, 2 * head)]
 
     sums = sums + to_core(theirs)
     grad_input = sums[0]
     for step in range(1, chips):
         grad_input = grad_input + to_chip(sums[step], step)
 
-    def finish(ring, arrived):
-        total = product_of(ring, 0)
+    def finish(ring, arrived, span=(0, 0)):
+        total = product_of(ring, 0, span)
         for term in arrived:
             total = total + term
         return total
 
     grad_query = [finish(ring, arrived) for ring, arrived in zip(q_rings, q_sent)]
+    tail_sent = [exchange(terms(ring, span)) for ring, span in zip(tail_rings, tail_spans)]
     grad_kv = [finish(ring, exchange(term)) for ring, term in zip(k_rings, k_terms)]
+    ends = [finish(*each) for each in zip(tail_rings, tail_sent, tail_spans)]
+    grad_kv.append(jnp.concatenate(ends[::-1], axis=1))
 
     return (
         jnp.concatenate(attended, axis=1),

time: 356 us -> 344 us (0.966)
  waiting for transfers between devices: 147 us -> 128 us
    ppermute x12 -> x13, waiting for transfers between devices: 31.1 us -> 20 us  [y_ring(): lax.ppermute(block, 'y', [(i, (i + step) % pair) for i in range(pair)])]
    ppermute x12 -> x13, starting transfers between devices: 7.77 us -> 14.5 us  [y_ring(): lax.ppermute(block, 'y', [(i, (i + step) % pair) for i in range(pair)])]
    ppermute x15 -> x16, waiting for transfers between devices: 92 us -> 86.5 us  [z_ring(): lax.ppermute(block, 'z', [(i, (i + step) % CHAIN) for i in range(CHAIN)])]
    ppermute x15 -> x16, starting transfers between devices: 19.2 us -> 16.5 us  [z_ring(): lax.ppermute(block, 'z', [(i, (i + step) % CHAIN) for i in range(CHAIN)])]
    unnamed x88 -> x102, local copies, waits for them, and re-layouts: 7.51 us -> 6.56 us
    pallas_call x8 -> x10, Pallas kernels: 24.8 us -> 24.3 us  [product(): pl.pallas_call(functools.partial(product_kernel, span[0]), grid_spec=pltp...]
  transfers between devices with their start and end apart: 39 -> 41, of which waited for: 21 -> 20; matrix products, arithmetic and copies ran while one was open for 9% -> 10% of each run, Pallas kernels for 27% -> 31%
where the time goes in v1:
time: 344 us; the launch traced here: 338 us
  waiting for transfers between devices  128 us (37%)
  Pallas kernels  112 us (33%)
  starting transfers between devices  54.3 us (16%)
  other arithmetic  31.2 us (9%)
  local copies, waits for them, and re-layouts  10.6 us (3%)
    ppermute x16, waiting for transfers between devices, z_ring(): lax.ppermute(block, 'z', [(i, (i + step) % CHAIN) for i in range(CHAIN)])  86.5 us
    pallas_call x4, Pallas kernels, project(): pl.pallas_call(functools.partial(project_kernel, normed, lanes), grid=(st...  34 us
    pallas_call x4, Pallas kernels, input_strips(): pl.pallas_call(functools.partial(strip_kernel, pieces), grid_spec=pltpu.P...  30.6 us
    pallas_call x10, Pallas kernels, product(): pl.pallas_call(functools.partial(product_kernel, span[0]), grid_spec=pltp...  24.3 us
    ppermute x8, waiting for transfers between devices, z_shift(): return lax.ppermute(block, 'z', route)  21.6 us
    ppermute x8, starting transfers between devices, z_shift(): return lax.ppermute(block, 'z', route)  20.2 us
    ppermute x13, waiting for transfers between devices, y_ring(): lax.ppermute(block, 'y', [(i, (i + step) % pair) for i in range(pair)])  20 us
    pallas_call x2, Pallas kernels, attention(): pl.pallas_call(functools.partial(attention_kernel, blocks, per_kv), out_s...  17.7 us
  transfers between devices with their start and end apart: 41, of which 20 were waited for; matrix products, arithmetic and copies ran while one was open for 10% of the time, Pallas kernels for 31%

profile of v1, /device:TPU:0, one launch (start us, length us, event | category | flops | bytes accessed | tf_op | source)
XLA Modules:
  0.0 338.3 jit_solution(1044318448733229344)
XLA Ops:
  1.9 8.7 %shard_map.119 = (f32[256,256]{1,0:T(8,128)}, f32[256,512]{1,0:T(8,128)}) custom-call(f32[256,3840]{1,0:T(8,128)} %source_ref.5, f32[3840,512]{1,0:T(8,128)} %refs_0_.15, f32[3840,512]{1,0:T(8,128)} %refs_0_.15, f32[3840,512]{1,0:T(8,128)} %refs_0_.15, f32[3840,512]{1,0:T(8,128)} %refs_1_.11, f32[3840,512]{1,0:T(8,128)} %refs_1_.11, f32[3840,512]{1,0:T(8,128)} %refs_1_.11, ...), custom_call_target="tpu_custom_call" | custom-call | flops 1024 | bytes 1024 | tf_op jit(solution)/shard_map/pallas_call | solution.py:200
  10.6 5.0 %collective-permute-start.3 = (f32[256,512]{1,0:T(8,128)}, f32[256,512]{1,0:T(8,128)S(1)}, u32[]{:S(2)}, u32[]{:S(2)}) collective-permute-start(f32[256,512]{1,0:T(8,128)} %get-tuple-element.50.refs_11_), channel_id=1, source_target_pairs={{0,8},{8,16},{16,24},{1,9},{9,17},{17,25},{2,10},{10,18},{18,26},{... | collective-permute-start | bytes 1572872 | tf_op jit(solution)/shard_map/ppermute | solution.py:382
  15.6 8.7 %shard_map.120 = (f32[256,256]{1,0:T(8,128)}, f32[256,512]{1,0:T(8,128)}) custom-call(f32[256,3840]{1,0:T(8,128)} %source_ref.5, f32[3840,512]{1,0:T(8,128)} %refs_0_.15, f32[3840,512]{1,0:T(8,128)} %refs_0_.15, f32[3840,512]{1,0:T(8,128)} %refs_0_.15, f32[3840,512]{1,0:T(8,128)} %refs_1_.11, f32[3840,512]{1,0:T(8,128)} %refs_1_.11, f32[3840,512]{1,0:T(8,128)} %refs_1_.11, ...), custom_call_target="tpu_custom_call" | custom-call | flops 1024 | bytes 1024 | tf_op jit(solution)/shard_map/pallas_call | solution.py:200
  24.3 3.6 %collective-permute-start.6 = (f32[256,512]{1,0:T(8,128)}, f32[256,512]{1,0:T(8,128)S(1)}, u32[]{:S(2)}, u32[]{:S(2)}) collective-permute-start(f32[256,512]{1,0:T(8,128)} %get-tuple-element.52.refs_11_), channel_id=1, source_target_pairs={{0,8},{8,16},{16,24},{1,9},{9,17},{17,25},{2,10},{10,18},{18,26},{... | collective-permute-start | bytes 1572872 | tf_op jit(solution)/shard_map/ppermute | solution.py:382
  27.9 8.2 %shard_map.121.refs_0_ = f32[256,512]{1,0:T(8,128)} custom-call(f32[256,3840]{1,0:T(8,128)} %source_ref.5, f32[3840,1024]{1,0:T(8,128)} %refs_0_.13, f32[3840,1024]{1,0:T(8,128)} %refs_0_.13, f32[3840,1024]{1,0:T(8,128)} %refs_0_.13), custom_call_target="tpu_custom_call" | custom-call | flops 12079595520 | bytes 1024 | tf_op jit(solution)/shard_map/pallas_call | solution.py:200
  36.1 3.5 %collective-permute-start.4 = (f32[256,512]{1,0:T(8,128)S(1)}, f32[256,512]{1,0:T(8,128)S(1)}, u32[]{:S(2)}, u32[]{:S(2)}) collective-permute-start(f32[256,512]{1,0:T(8,128)S(1)} %collective-permute-done.3.refs_9_), channel_id=1, source_target_pairs={{0,8},{8,16},{16,24},{1,9},{9,17},{17,25},{2,10},{10,18},{18,26},{... | collective-permute-start | bytes 1572872 | tf_op jit(solution)/shard_map/ppermute | solution.py:382
  46.3 8.4 %shard_map.122.refs_0_ = f32[256,512]{1,0:T(8,128)} custom-call(f32[256,3840]{1,0:T(8,128)} %source_ref.5, f32[3840,1024]{1,0:T(8,128)} %refs_0_.13, f32[3840,1024]{1,0:T(8,128)} %refs_0_.13, f32[3840,1024]{1,0:T(8,128)} %refs_0_.13), custom_call_target="tpu_custom_call" | custom-call | flops 12079595520 | bytes 1024 | tf_op jit(solution)/shard_map/pallas_call | solution.py:200
  69.0 13.7 %collective-permute-done.1 = f32[240,256]{1,0:T(8,128)S(1)} collective-permute-done((f32[240,256]{1,0:T(8,128)}, f32[240,256]{1,0:T(8,128)S(1)}, u32[]{:S(2)}, u32[]{:S(2)}) %collective-permute-start.1) | collective-permute-done | bytes 245792 | tf_op jit(solution)/shard_map/ppermute | solution.py:385
  83.5 8.5 %shard_map.124 = (f32[256,512]{1,0:T(8,128)S(1)}, f32[256,512]{1,0:T(8,128)S(1)}, f32[256,512]{1,0:T(8,128)S(1)}, f32[256,512]{1,0:T(8,128)S(1)}, f32[256,512]{1...) custom-call(f32[256,512]{1,0:T(8,128)S(1)} %copy-done.15, f32[256,512]{1,0:T(8,128)S(1)} %get-tuple-element.101.refs_1_, ...), custom_call_target="tpu_custom_call" | custom-call | flops 1024 | bytes 1024 | tf_op jit(solution)/shard_map/pallas_call | solution.py:138
  97.5 9.1 %shard_map.125 = (f32[256,512]{1,0:T(8,128)S(1)}, f32[256,512]{1,0:T(8,128)S(1)}, f32[256,512]{1,0:T(8,128)S(1)}, f32[256,512]{1,0:T(8,128)}, f32[256,512]{1,0:T...) custom-call(f32[256,512]{1,0:T(8,128)S(1)} %copy-done.14, f32[256,512]{1,0:T(8,128)S(1)} %get-tuple-element.100.refs_1_, ...), custom_call_target="tpu_custom_call" | custom-call | flops 1024 | bytes 1024 | tf_op jit(solution)/shard_map/pallas_call | solution.py:138
  113.3 4.9 %collective-permute-done.11.one_ref = f32[256,512]{1,0:T(8,128)S(1)} collective-permute-done((f32[256,512]{1,0:T(8,128)S(1)}, f32[256,512]{1,0:T(8,128)S(1)}, u32[]{:S(2)}, u32[]{:S(2)}) %collective-permute-start.11) | collective-permute-done | bytes 524320 | tf_op jit(solution)/shard_map/ppermute | solution.py:388
  118.2 4.1 %collective-permute-done.14 = f32[256,512]{1,0:T(8,128)S(1)} collective-permute-done((f32[256,512]{1,0:T(8,128)S(1)}, f32[256,512]{1,0:T(8,128)S(1)}, u32[]{:S(2)}, u32[]{:S(2)}) %collective-permute-start.14) | collective-permute-done | bytes 524320 | tf_op jit(solution)/shard_map/ppermute | solution.py:382
  123.4 14.1 %collective-permute-done.15.refs_2_ = f32[256,512]{1,0:T(8,128)S(1)} collective-permute-done((f32[256,512]{1,0:T(8,128)S(1)}, f32[256,512]{1,0:T(8,128)S(1)}, u32[]{:S(2)}, u32[]{:S(2)}) %collective-permute-start.15) | collective-permute-done | bytes 524320 | tf_op jit(solution)/shard_map/ppermute | solution.py:385
  142.1 7.7 %shard_map.128 = f32[2,960,256]{2,1,0:T(8,128)} custom-call(s32[2]{0:T(128)} %pad_add_fusion.1.strips_ref, f32[3840,1024]{1,0:T(8,128)} %refs_0_.13, f32[256,512]{1,0:T(8,128)} %copy-done.7, f32[256,512]{1,0:T(8,128)} %copy-done.9), custom_call_target="tpu_custom_call" | custom-call | flops 1024 | bytes 1024 | tf_op jit(solution)/shard_map/pallas_call | solution.py:345
  151.4 7.7 %collective-permute-done.16.far_ref = f32[256,512]{1,0:T(8,128)} collective-permute-done((f32[256,512]{1,0:T(8,128)}, f32[256,512]{1,0:T(8,128)}, u32[]{:S(2)}, u32[]{:S(2)}) %collective-permute-start.16) | collective-permute-done | bytes 524320 | tf_op jit(solution)/shard_map/ppermute | solution.py:382
  167.1 7.7 %shard_map.126 = f32[2,960,256]{2,1,0:T(8,128)} custom-call(s32[2]{0:T(128)} %pad_add_fusion.strips_ref, f32[3840,1024]{1,0:T(8,128)} %refs_0_.13, f32[256,512]{1,0:T(8,128)} %copy-done.7, f32[256,512]{1,0:T(8,128)} %copy-done.9), custom_call_target="tpu_custom_call" | custom-call | flops 1024 | bytes 1024 | tf_op jit(solution)/shard_map/pallas_call | solution.py:345
  174.7 8.5 %collective-permute-done.20 = f32[256,512]{1,0:T(8,128)} collective-permute-done((f32[256,512]{1,0:T(8,128)}, f32[256,512]{1,0:T(8,128)}, u32[]{:S(2)}, u32[]{:S(2)}) %collective-permute-start.20) | collective-permute-done | bytes 524320 | tf_op jit(solution)/shard_map/ppermute | solution.py:382
  199.1 7.7 %shard_map.131 = f32[2,960,256]{2,1,0:T(8,128)} custom-call(s32[2]{0:T(128)} %pad_add_fusion.1.strips_ref, f32[3840,512]{1,0:T(8,128)} %refs_0_.15, f32[3840,512]{1,0:T(8,128)} %refs_1_.11, f32[256,512]{1,0:T(8,128)} %copy-done.4, f32[256,512]{1,0:T(8,128)} %copy-done.1), custom_call_target="tpu_custom_call" | custom-call | flops 1024 | bytes 1024 | tf_op jit(solution)/shard_map/pallas_call | solution.py:345
  211.3 14.7 %collective-permute-done.28.refs_2_ = f32[256,512]{1,0:T(8,128)S(1)} collective-permute-done((f32[256,512]{1,0:T(8,128)S(1)}, f32[256,512]{1,0:T(8,128)S(1)}, u32[]{:S(2)}, u32[]{:S(2)}) %collective-permute-start.28) | collective-permute-done | bytes 524320 | tf_op jit(solution)/shard_map/ppermute | solution.py:385
  231.3 3.2 shard_map.134
  235.8 7.0 %collective-permute-done.31.refs_1_ = f32[256,512]{1,0:T(8,128)} collective-permute-done((f32[256,512]{1,0:T(8,128)S(1)}, f32[256,512]{1,0:T(8,128)}, u32[]{:S(2)}, u32[]{:S(2)}) %collective-permute-start.31) | collective-permute-done | bytes 524320 | tf_op jit(solution)/shard_map/ppermute | solution.py:385
  242.8 11.1 %collective-permute-done.29.refs_3_ = f32[256,512]{1,0:T(8,128)S(1)} collective-permute-done((f32[256,512]{1,0:T(8,128)S(1)}, f32[256,512]{1,0:T(8,128)S(1)}, u32[]{:S(2)}, u32[]{:S(2)}) %collective-permute-start.29) | collective-permute-done | bytes 524320 | tf_op jit(solution)/shard_map/ppermute | solution.py:385
  253.9 3.2 shard_map.136
  258.4 6.7 %collective-permute-done.32.refs_2_ = f32[256,512]{1,0:T(8,128)S(1)} collective-permute-done((f32[256,512]{1,0:T(8,128)}, f32[256,512]{1,0:T(8,128)S(1)}, u32[]{:S(2)}, u32[]{:S(2)}) %collective-permute-start.32) | collective-permute-done | bytes 524320 | tf_op jit(solution)/shard_map/ppermute | solution.py:385
  265.2 7.5 %shard_map.130 = f32[2,960,256]{2,1,0:T(8,128)} custom-call(s32[2]{0:T(128)} %pad_add_fusion.strips_ref, f32[3840,512]{1,0:T(8,128)} %refs_0_.15, f32[3840,512]{1,0:T(8,128)} %refs_1_.11, f32[256,512]{1,0:T(8,128)} %copy-done.4, f32[256,512]{1,0:T(8,128)} %copy-done.1), custom_call_target="tpu_custom_call" | custom-call | flops 1024 | bytes 1024 | tf_op jit(solution)/shard_map/pallas_call | solution.py:345
  272.7 3.2 fusion.8
  276.4 11.3 %collective-permute-done.33.refs_3_ = f32[256,512]{1,0:T(8,128)} collective-permute-done((f32[256,512]{1,0:T(8,128)S(1)}, f32[256,512]{1,0:T(8,128)}, u32[]{:S(2)}, u32[]{:S(2)}) %collective-permute-start.33) | collective-permute-done | bytes 524320 | tf_op jit(solution)/shard_map/ppermute | solution.py:385
  287.7 3.5 %shard_map.138 = f32[480,512]{1,0:T(8,128)S(1)} custom-call(s32[2]{0:T(128)S(1)} %pad_add_fusion.2.place_ref, bf16[4,960,256]{2,1,0:T(8,128)(2,1)S(1)} %get-tuple-element.85.high_ref, bf16[4,960,256]{2,1,0:T(8,128)(2,1)S(1)} %get-tuple-element.86.low_ref, f32[256,512]{1,0:T(8,128)S(1)} %copy-done.6, f32[256,512]{1,0:T(8,128)} %collective-permute-done.31.refs_1_, ...), custom_call_target="tpu_custom_call" | custom-call | flops 1024 | bytes 1024 | tf_op jit(solution)/shard_map/pallas_call | solution.py:312
  294.2 3.4 %collective-permute-done.36.refs_2_ = f32[256,512]{1,0:T(8,128)S(1)} collective-permute-done((f32[256,512]{1,0:T(8,128)S(1)}, f32[256,512]{1,0:T(8,128)S(1)}, u32[]{:S(2)}, u32[]{:S(2)}) %collective-permute-start.36) | collective-permute-done | bytes 524320 | tf_op jit(solution)/shard_map/ppermute | solution.py:385
  308.1 3.5 %shard_map.137 = f32[480,512]{1,0:T(8,128)S(1)} custom-call(s32[2]{0:T(128)S(1)} %pad_add_fusion.2.place_ref, bf16[4,960,256]{2,1,0:T(8,128)(2,1)S(1)} %get-tuple-element.85.high_ref, bf16[4,960,256]{2,1,0:T(8,128)(2,1)S(1)} %get-tuple-element.86.low_ref, f32[256,512]{1,0:T(8,128)S(1)} %copy-done.6, f32[256,512]{1,0:T(8,128)} %collective-permute-done.31.refs_1_, ...), custom_call_target="tpu_custom_call" | custom-call | flops 1024 | bytes 1024 | tf_op jit(solution)/shard_map/pallas_call | solution.py:312
  322.4 6.1 %collective-permute-done.38 = f32[480,256]{1,0:T(8,128)S(1)} collective-permute-done((f32[480,256]{1,0:T(8,128)S(1)}, f32[480,256]{1,0:T(8,128)S(1)}, u32[]{:S(2)}, u32[]{:S(2)}) %collective-permute-start.38) | collective-permute-done | bytes 491552 | tf_op jit(solution)/shard_map/ppermute | solution.py:388
  329.7 7.0 %collective-permute-done.40 = f32[480,256]{1,0:T(8,128)S(1)} collective-permute-done((f32[480,256]{1,0:T(8,128)S(1)}, f32[480,256]{1,0:T(8,128)S(1)}, u32[]{:S(2)}, u32[]{:S(2)}) %collective-permute-start.40) | collective-permute-done | bytes 491552 | tf_op jit(solution)/shard_map/ppermute | solution.py:388
  (214 shorter events, 105.1 us)
Async XLA Ops:
  10.6 25.5 %collective-permute-start.3 = (f32[256,512]{1,0:T(8,128)}, f32[256,512]{1,0:T(8,128)S(1)}, u32[]{:S(2)}, u32[]{:S(2)}) collective-permute-start(f32[256,512]{1,0:T(8,128)} %get-tuple-element.50.refs_11_), channel_id=1, source_target_pairs={{0,8},{8,16},{16,24},{1,9},{9,17},{17,25},{2,10},{10,18},{18,26},{... | collective-permute-start | bytes 1572872 | tf_op jit(solution)/shard_map/ppermute | solution.py:382
  24.3 17.7 %collective-permute-start.6 = (f32[256,512]{1,0:T(8,128)}, f32[256,512]{1,0:T(8,128)S(1)}, u32[]{:S(2)}, u32[]{:S(2)}) collective-permute-start(f32[256,512]{1,0:T(8,128)} %get-tuple-element.52.refs_11_), channel_id=1, source_target_pairs={{0,8},{8,16},{16,24},{1,9},{9,17},{17,25},{2,10},{10,18},{18,26},{... | collective-permute-start | bytes 1572872 | tf_op jit(solution)/shard_map/ppermute | solution.py:382
  36.1 25.3 %collective-permute-start.4 = (f32[256,512]{1,0:T(8,128)S(1)}, f32[256,512]{1,0:T(8,128)S(1)}, u32[]{:S(2)}, u32[]{:S(2)}) collective-permute-start(f32[256,512]{1,0:T(8,128)S(1)} %collective-permute-done.3.refs_9_), channel_id=1, source_target_pairs={{0,8},{8,16},{16,24},{1,9},{9,17},{17,25},{2,10},{10,18},{18,26},{... | collective-permute-start | bytes 1572872 | tf_op jit(solution)/shard_map/ppermute | solution.py:382
  40.5 24.0 %collective-permute-start.5 = (f32[256,512]{1,0:T(8,128)}, f32[256,512]{1,0:T(8,128)}, u32[]{:S(2)}, u32[]{:S(2)}) collective-permute-start(f32[256,512]{1,0:T(8,128)} %broadcast_select_fusion.3), channel_id=1, source_target_pairs={{0,4},{4,0},{1,5},{5,1},{2,6},{6,2},{3,7},{7,3},{8,12},{12,8},{9,1... | collective-permute-start | bytes 1572872 | tf_op jit(solution)/shard_map/ppermute | solution.py:388
  42.9 22.3 %collective-permute-start.7 = (f32[256,512]{1,0:T(8,128)}, f32[256,512]{1,0:T(8,128)}, u32[]{:S(2)}, u32[]{:S(2)}) collective-permute-start(f32[256,512]{1,0:T(8,128)} %broadcast_select_fusion.2), channel_id=1, source_target_pairs={{0,4},{4,0},{1,5},{5,1},{2,6},{6,2},{3,7},{7,3},{8,12},{12,8},{9,1... | collective-permute-start | bytes 1572872 | tf_op jit(solution)/shard_map/ppermute | solution.py:388
  43.4 21.8 %collective-permute-start.8 = (f32[256,512]{1,0:T(8,128)S(1)}, f32[256,512]{1,0:T(8,128)S(1)}, u32[]{:S(2)}, u32[]{:S(2)}) collective-permute-start(f32[256,512]{1,0:T(8,128)S(1)} %collective-permute-done.6.refs_9_), channel_id=1, source_target_pairs={{0,8},{8,16},{16,24},{1,9},{9,17},{17,25},{2,10},{10,18},{18,26},{... | collective-permute-start | bytes 1572872 | tf_op jit(solution)/shard_map/ppermute | solution.py:382
  61.5 21.3 %collective-permute-start.1 = (f32[240,256]{1,0:T(8,128)}, f32[240,256]{1,0:T(8,128)S(1)}, u32[]{:S(2)}, u32[]{:S(2)}) collective-permute-start(f32[240,256]{1,0:T(8,128)} %get-tuple-element.98), channel_id=1, source_target_pairs={{0,16},{8,24},{16,0},{24,8},{1,17},{9,25},{17,1},{25,9},{2,18},{10... | collective-permute-start | bytes 737288 | tf_op jit(solution)/shard_map/ppermute | solution.py:385
  64.5 18.2 %collective-permute-start.2 = (f32[240,256]{1,0:T(8,128)}, f32[240,256]{1,0:T(8,128)S(1)}, u32[]{:S(2)}, u32[]{:S(2)}) collective-permute-start(f32[240,256]{1,0:T(8,128)} %get-tuple-element.97), channel_id=1, source_target_pairs={{0,8},{8,16},{16,24},{24,0},{1,9},{9,17},{17,25},{25,1},{2,10},{10... | collective-permute-start | bytes 737288 | tf_op jit(solution)/shard_map/ppermute | solution.py:385
  65.4 18.1 %collective-permute-start.9 = (f32[256,512]{1,0:T(8,128)S(1)}, f32[256,512]{1,0:T(8,128)S(1)}, u32[]{:S(2)}, u32[]{:S(2)}) collective-permute-start(f32[256,512]{1,0:T(8,128)S(1)} %broadcast_select_fusion.1), channel_id=1, source_target_pairs={{0,4},{4,0},{1,5},{5,1},{2,6},{6,2},{3,7},{7,3},{8,12},{12,8},{9,1... | collective-permute-start | bytes 1572872 | tf_op jit(solution)/shard_map/ppermute | solution.py:388
  96.0 22.2 %collective-permute-start.11 = (f32[256,512]{1,0:T(8,128)S(1)}, f32[256,512]{1,0:T(8,128)S(1)}, u32[]{:S(2)}, u32[]{:S(2)}) collective-permute-start(f32[256,512]{1,0:T(8,128)S(1)} %get-tuple-element.67), channel_id=1, source_target_pairs={{0,4},{4,0},{1,5},{5,1},{2,6},{6,2},{3,7},{7,3},{8,12},{12,8},{9,1... | collective-permute-start | bytes 1572872 | tf_op jit(solution)/shard_map/ppermute | solution.py:388
  109.1 28.4 %collective-permute-start.15 = (f32[256,512]{1,0:T(8,128)S(1)}, f32[256,512]{1,0:T(8,128)S(1)}, u32[]{:S(2)}, u32[]{:S(2)}) collective-permute-start(f32[256,512]{1,0:T(8,128)S(1)} %collective-permute-done.13.refs_1_), channel_id=1, source_target_pairs={{0,8},{8,16},{16,24},{24,0},{1,9},{9,17},{17,25},{25,1},{2,10},{10... | collective-permute-start | bytes 1572872 | tf_op jit(solution)/shard_map/ppermute | solution.py:385
  112.3 38.1 %collective-permute-start.18 = (f32[256,512]{1,0:T(8,128)}, f32[256,512]{1,0:T(8,128)}, u32[]{:S(2)}, u32[]{:S(2)}) collective-permute-start(f32[256,512]{1,0:T(8,128)} %get-tuple-element.78), channel_id=1, source_target_pairs={{0,4},{4,0},{1,5},{5,1},{2,6},{6,2},{3,7},{7,3},{8,12},{12,8},{9,1... | collective-permute-start | bytes 1572872 | tf_op jit(solution)/shard_map/ppermute | solution.py:388
  137.5 21.6 %collective-permute-start.16 = (f32[256,512]{1,0:T(8,128)}, f32[256,512]{1,0:T(8,128)}, u32[]{:S(2)}, u32[]{:S(2)}) collective-permute-start(f32[256,512]{1,0:T(8,128)} %add_add_fusion.1), channel_id=1, source_target_pairs={{8,0},{16,8},{24,16},{9,1},{17,9},{25,17},{10,2},{18,10},{26,18},{... | collective-permute-start | bytes 1572872 | tf_op jit(solution)/shard_map/ppermute | solution.py:382
  138.8 21.8 %collective-permute-start.19 = (f32[256,512]{1,0:T(8,128)S(1)}, f32[256,512]{1,0:T(8,128)S(1)}, u32[]{:S(2)}, u32[]{:S(2)}) collective-permute-start(f32[256,512]{1,0:T(8,128)S(1)} %get-tuple-element.80.refs_2_.refs_0_), channel_id=1, source_target_pairs={{0,8},{8,16},{16,24},{24,0},{1,9},{9,17},{17,25},{25,1},{2,10},{10... | collective-permute-start | bytes 1572872 | tf_op jit(solution)/shard_map/ppermute | solution.py:385
  149.8 24.9 %collective-permute-start.17 = (f32[256,512]{1,0:T(8,128)}, f32[256,512]{1,0:T(8,128)S(1)}, u32[]{:S(2)}, u32[]{:S(2)}) collective-permute-start(f32[256,512]{1,0:T(8,128)} %get-tuple-element.76), channel_id=1, source_target_pairs={{0,4},{4,0},{1,5},{5,1},{2,6},{6,2},{3,7},{7,3},{8,12},{12,8},{9,1... | collective-permute-start | bytes 1572872 | tf_op jit(solution)/shard_map/ppermute | solution.py:388
  160.6 22.6 %collective-permute-start.20 = (f32[256,512]{1,0:T(8,128)}, f32[256,512]{1,0:T(8,128)}, u32[]{:S(2)}, u32[]{:S(2)}) collective-permute-start(f32[256,512]{1,0:T(8,128)} %select_add_fusion), channel_id=1, source_target_pairs={{8,0},{16,8},{24,16},{9,1},{17,9},{25,17},{10,2},{18,10},{26,18},{... | collective-permute-start | bytes 1572872 | tf_op jit(solution)/shard_map/ppermute | solution.py:382
  163.8 23.2 %collective-permute-start.25 = (f32[3,240,256]{2,1,0:T(8,128)}, f32[3,240,256]{2,1,0:T(8,128)}, u32[]{:S(2)}, u32[]{:S(2)}) collective-permute-start(f32[3,240,256]{2,1,0:T(8,128)} %pad_maximum_fusion.4), channel_id=1, source_target_pairs={{0,1},{1,0},{2,3},{3,2},{4,5},{5,4},{6,7},{7,6},{8,9},{9,8},{10,11... | collective-permute-start | bytes 2211848 | tf_op jit(solution)/shard_map/ppermute | solution.py:448
  163.8 21.7 %collective-permute-start.21 = (f32[256,512]{1,0:T(8,128)S(1)}, f32[256,512]{1,0:T(8,128)S(1)}, u32[]{:S(2)}, u32[]{:S(2)}) collective-permute-start(f32[256,512]{1,0:T(8,128)S(1)} %collective-permute-done.15.refs_2_), channel_id=1, source_target_pairs={{0,8},{8,16},{16,24},{24,0},{1,9},{9,17},{17,25},{25,1},{2,10},{10... | collective-permute-start | bytes 1572872 | tf_op jit(solution)/shard_map/ppermute | solution.py:385
  189.8 37.7 %collective-permute-start.26 = (f32[3,480,256]{2,1,0:T(8,128)}, f32[3,480,256]{2,1,0:T(8,128)}, u32[]{:S(2)}, u32[]{:S(2)}) collective-permute-start(f32[3,480,256]{2,1,0:T(8,128)} %fusion.3), channel_id=1, source_target_pairs={{0,2},{1,3},{2,0},{3,1},{4,6},{5,7},{6,4},{7,5},{8,10},{9,11},{10,... | collective-permute-start | bytes 4423688 | tf_op jit(solution)/shard_map/ppermute | solution.py:452
  209.9 62.8 %collective-permute-start.23 = (f32[2,960,256]{2,1,0:T(8,128)}, f32[2,960,256]{2,1,0:T(8,128)}, u32[]{:S(2)}, u32[]{:S(2)}) collective-permute-start(f32[2,960,256]{2,1,0:T(8,128)} %add.169), channel_id=1, source_target_pairs={{0,1},{1,0},{2,3},{3,2},{4,5},{5,4},{6,7},{7,6},{8,9},{9,8},{10,11... | collective-permute-start | bytes 5898248 | tf_op jit(solution)/shard_map/ppermute | solution.py:448
  226.1 16.7 %collective-permute-start.31 = (f32[256,512]{1,0:T(8,128)S(1)}, f32[256,512]{1,0:T(8,128)}, u32[]{:S(2)}, u32[]{:S(2)}) collective-permute-start(f32[256,512]{1,0:T(8,128)S(1)} %copy-done.5), channel_id=1, source_target_pairs={{0,8},{8,16},{16,24},{24,0},{1,9},{9,17},{17,25},{25,1},{2,10},{10... | collective-permute-start | bytes 1572872 | tf_op jit(solution)/shard_map/ppermute | solution.py:385
  234.5 19.4 %collective-permute-start.29 = (f32[256,512]{1,0:T(8,128)S(1)}, f32[256,512]{1,0:T(8,128)S(1)}, u32[]{:S(2)}, u32[]{:S(2)}) collective-permute-start(f32[256,512]{1,0:T(8,128)S(1)} %copy-done.22), channel_id=1, source_target_pairs={{0,8},{8,16},{16,24},{24,0},{1,9},{9,17},{17,25},{25,1},{2,10},{10... | collective-permute-start | bytes 1572872 | tf_op jit(solution)/shard_map/ppermute | solution.py:385
  234.5 41.4 %collective-permute-start.27 = (f32[480,512]{1,0:T(8,128)}, f32[480,512]{1,0:T(8,128)}, u32[]{:S(2)}, u32[]{:S(2)}) collective-permute-start(f32[480,512]{1,0:T(8,128)} %shard_map.134), channel_id=1, source_target_pairs={{0,4},{4,0},{1,5},{5,1},{2,6},{6,2},{3,7},{7,3},{8,12},{12,8},{9,1... | collective-permute-start | bytes 2949128 | tf_op jit(solution)/shard_map/ppermute | solution.py:388
  242.8 22.4 %collective-permute-start.32 = (f32[256,512]{1,0:T(8,128)}, f32[256,512]{1,0:T(8,128)S(1)}, u32[]{:S(2)}, u32[]{:S(2)}) collective-permute-start(f32[256,512]{1,0:T(8,128)} %collective-permute-done.31.refs_1_), channel_id=1, source_target_pairs={{0,8},{8,16},{16,24},{24,0},{1,9},{9,17},{17,25},{25,1},{2,10},{10... | collective-permute-start | bytes 1572872 | tf_op jit(solution)/shard_map/ppermute | solution.py:385
  253.9 22.5 %collective-permute-start.35 = (f32[256,512]{1,0:T(8,128)S(1)}, f32[256,512]{1,0:T(8,128)S(1)}, u32[]{:S(2)}, u32[]{:S(2)}) collective-permute-start(f32[256,512]{1,0:T(8,128)S(1)} %copy-done.2), channel_id=1, source_target_pairs={{0,8},{8,16},{16,24},{24,0},{1,9},{9,17},{17,25},{25,1},{2,10},{10... | collective-permute-start | bytes 1572872 | tf_op jit(solution)/shard_map/ppermute | solution.py:385
  257.2 37.0 %collective-permute-start.30 = (f32[480,512]{1,0:T(8,128)}, f32[480,512]{1,0:T(8,128)}, u32[]{:S(2)}, u32[]{:S(2)}) collective-permute-start(f32[480,512]{1,0:T(8,128)} %shard_map.136), channel_id=1, source_target_pairs={{0,4},{4,0},{1,5},{5,1},{2,6},{6,2},{3,7},{7,3},{8,12},{12,8},{9,1... | collective-permute-start | bytes 2949128 | tf_op jit(solution)/shard_map/ppermute | solution.py:388
  265.2 22.6 %collective-permute-start.33 = (f32[256,512]{1,0:T(8,128)S(1)}, f32[256,512]{1,0:T(8,128)}, u32[]{:S(2)}, u32[]{:S(2)}) collective-permute-start(f32[256,512]{1,0:T(8,128)S(1)} %collective-permute-done.32.refs_2_), channel_id=1, source_target_pairs={{0,8},{8,16},{16,24},{24,0},{1,9},{9,17},{17,25},{25,1},{2,10},{10... | collective-permute-start | bytes 1572872 | tf_op jit(solution)/shard_map/ppermute | solution.py:385
  276.4 21.2 %collective-permute-start.36 = (f32[256,512]{1,0:T(8,128)S(1)}, f32[256,512]{1,0:T(8,128)S(1)}, u32[]{:S(2)}, u32[]{:S(2)}) collective-permute-start(f32[256,512]{1,0:T(8,128)S(1)} %collective-permute-done.35.refs_1_), channel_id=1, source_target_pairs={{0,8},{8,16},{16,24},{24,0},{1,9},{9,17},{17,25},{25,1},{2,10},{10... | collective-permute-start | bytes 1572872 | tf_op jit(solution)/shard_map/ppermute | solution.py:385
  291.2 21.3 %collective-permute-start.34 = (f32[480,512]{1,0:T(8,128)S(1)}, f32[480,512]{1,0:T(8,128)S(1)}, u32[]{:S(2)}, u32[]{:S(2)}) collective-permute-start(f32[480,512]{1,0:T(8,128)S(1)} %shard_map.138), channel_id=1, source_target_pairs={{0,4},{4,0},{1,5},{5,1},{2,6},{6,2},{3,7},{7,3},{8,12},{12,8},{9,1... | collective-permute-start | bytes 2949128 | tf_op jit(solution)/shard_map/ppermute | solution.py:388
  292.6 28.7 %collective-permute-start.24 = (f32[960,256]{1,0:T(8,128)S(1)}, f32[960,256]{1,0:T(8,128)S(1)}, u32[]{:S(2)}, u32[]{:S(2)}) collective-permute-start(f32[960,256]{1,0:T(8,128)S(1)} %slice_bitcast_fusion), channel_id=1, source_target_pairs={{0,2},{1,3},{2,0},{3,1},{4,6},{5,7},{6,4},{7,5},{8,10},{9,11},{10,... | collective-permute-start | bytes 2949128 | tf_op jit(solution)/shard_map/ppermute | solution.py:452
  297.7 17.9 %collective-permute-start.39 = (f32[256,256]{1,0:T(8,128)S(1)}, f32[256,256]{1,0:T(8,128)S(1)}, u32[]{:S(2)}, u32[]{:S(2)}) collective-permute-start(f32[256,256]{1,0:T(8,128)S(1)} %get-tuple-element.104), channel_id=1, source_target_pairs={{0,8},{8,16},{16,24},{24,0},{1,9},{9,17},{17,25},{25,1},{2,10},{10... | collective-permute-start | bytes 786440 | tf_op jit(solution)/shard_map/ppermute | solution.py:385
  317.2 19.5 %collective-permute-start.40 = (f32[480,256]{1,0:T(8,128)S(1)}, f32[480,256]{1,0:T(8,128)S(1)}, u32[]{:S(2)}, u32[]{:S(2)}) collective-permute-start(f32[480,256]{1,0:T(8,128)S(1)} %shard_map.142), channel_id=1, source_target_pairs={{0,4},{4,0},{1,5},{5,1},{2,6},{6,2},{3,7},{7,3},{8,12},{12,8},{9,1... | collective-permute-start | bytes 1474568 | tf_op jit(solution)/shard_map/ppermute | solution.py:388
  (60 other events, 649.2 us)

commit v2 on v1

--- a/solution.py
+++ b/solution.py
@@ -323,9 +323,9 @@
     )(place, high, low, *blocks)
 
 
-def strip_kernel(pieces, strips_ref, *refs):
+def strip_kernel(pieces, added, strips_ref, *refs):
     weight_refs, left_refs = refs[: len(pieces)], refs[len(pieces) : -1]
-    total = None
+    total = left_refs[-1][0] if added else None
     left_at = 0
     for ref, (count, start, wide) in zip(weight_refs, pieces):
         for group in range(count):
@@ -337,24 +337,26 @@
     refs[-1][0] = total
 
 
-def input_strips(strips, strip, weights, lefts, pieces):
+def input_strips(strips, strip, weights, lefts, pieces, partial):
     count = strips.shape[0]
     rows = lefts[0].shape[0]
     wide = sum(w.shape[1] for w in weights)
     whole = [pl.BlockSpec(d.shape, lambda i, p: (0, 0)) for d in lefts]
+    out_spec = pl.BlockSpec((1, strip, rows), lambda i, p: (i, 0, 0))
     return pl.pallas_call(
-        functools.partial(strip_kernel, pieces),
+        functools.partial(strip_kernel, pieces, partial is not None),
         grid_spec=pltpu.PrefetchScalarGridSpec(
             num_scalar_prefetch=1,
             grid=(count,),
             in_specs=[pl.BlockSpec((strip, w.shape[1]), lambda i, p: (p[i], 0)) for w in weights]
-            + whole,
-            out_specs=pl.BlockSpec((1, strip, rows), lambda i, p: (i, 0, 0)),
+            + whole
+            + ([] if partial is None else [out_spec]),
+            out_specs=out_spec,
         ),
         out_shape=jax.ShapeDtypeStruct((count, strip, rows), jnp.float32),
         compiler_params=pltpu.CompilerParams(vmem_limit_bytes=56 * MIB),
         cost_estimate=SOON,
-    )(strips, *weights, *lefts)
+    )(strips, *weights, *lefts, *([] if partial is None else [partial]))
 
 
 def local(hidden_in, query_proj, key_proj, value_proj, query_gain, key_gain, segment_ids, grad_out):
@@ -431,16 +433,17 @@
         for group in groups:
             fours.append(z_shift(after(two[group], own[-1]), 1))
         for group in groups:
-            three_back = farthest(group, fours[group], *ones, *fours, hidden_rows)
+            three_back = farthest(group, fours[group], *ones, *fours[:group], hidden_rows)
             windows.append([fours[group], three_back, two[group], ones[group], own[group]])
     else:
         for group in groups:
             windows.append([shifted(own[group], d) for d in range(reach, 0, -1)] + [own[group]])
+    shared = after(hidden_rows, *fours) if fours else hidden_rows
     pieces = []
     for step in range(CHAIN - 1, 0, -1):
         target = (along + step) % CHAIN
         start = target * slab + member * piece
-        pieces.append(z_ring(lax.dynamic_slice_in_dim(hidden_rows, start, piece, 0), step))
+        pieces.append(z_ring(lax.dynamic_slice_in_dim(shared, start, piece, 0), step))
     chips = members // CORES
     chip, core = member // CORES, member % CORES
 
@@ -490,11 +493,11 @@
 
     def query_strips(which):
         pieces = ((kv_local, 0, per_kv * head),)
-        return input_strips(which, strip, (query_proj,), d_query, pieces)
-
-    def kv_strips(which):
+        return input_strips(which, strip, (query_proj,), d_query, pieces, None)
+
+    def kv_strips(which, partial):
         pieces = ((kv_local, 0, head), (kv_local, head, head))
-        return input_strips(which, strip, (key_proj, value_proj), d_kv, pieces)
+        return input_strips(which, strip, (key_proj, value_proj), d_kv, pieces, partial)
 
     def product_of(ring, step, span=(0, 0)):
         return product(place, step, turned, ring, pair, span)
@@ -530,9 +533,10 @@
         got = follow(block, lambda b: z_shift(b, -1), extra)
         held.append((two_back + jnp.where(across == 0, from_three, from_one) + got, from_one))
 
-    def near_return(group, *extra):
+    def near_return(group, extra, before):
         block, from_one = held[group]
         far = follow(block, lambda b: z_shift(b, -1), extra)
+        far = after(far, *before) if before else far
         mine = parts[group][-1]
         d_kv.append(settle(mine, from_one, far, keep, key_raw[group], *tables))
         k_rings.append([d_kv[group]])
@@ -541,29 +545,30 @@
         q_hop(0)
         far_return(0, q_rings[0][1], *attended)
         q_hop(0)
-        near_return(0, q_rings[0][2])
+        near_return(0, [q_rings[0][2]], [])
         q_hop(1)
         theirs_q = query_strips(theirs_at)
         far_return(1, theirs_q, q_rings[1][1])
         q_hop(0)
         mine_q = query_strips(mine_at)
         q_hop(1)
-        near_return(1, mine_q, q_rings[0][3])
         k_hop(0)
+        near_return(1, [mine_q, q_rings[0][3], q_rings[1][2]], [k_rings[0][1]])
         q_terms = [terms(q_rings[0])]
         q_hop(1, *q_terms[0])
         k_hop(0)
-        theirs = theirs_q + kv_strips(theirs_at)
+        theirs = kv_strips(theirs_at, theirs_q)
         q_sent = [exchange(q_terms[0])]
-        k_hop(1, theirs)
+        k_hop(1)
         q_terms.append(terms(q_rings[1]))
         k_hop(0, *q_terms[1])
-        sums = mine_q + kv_strips(mine_at)
-        k_hop(1, sums, *q_sent[0])
+        sums = kv_strips(mine_at, mine_q)
+        k_hop(1, theirs, *q_sent[0])
         k_terms = [terms(k_rings[0])]
         q_sent.append(exchange(q_terms[1]))
-        last = after(k_rings[1][-1], sent[-2], *k_terms[0], *q_sent[1])
-        tails = [z_ring(last[:, head:], 1), z_ring(last[:, :head], 1)]
+        last = after(k_rings[1][-1], sent[-2], sums, *k_terms[0], *q_sent[1])
+        tails = [z_ring(last[:, head:], 1)]
+        tails.append(z_ring(after(last[:, :head], tails[0]), 1))
         tail_rings = [k_rings[1] + [tail] for tail in tails]
         tail_spans = [(head, head), (0, head)]
     else:
@@ -578,8 +583,8 @@
                 q_hop(group)
             for _ in range(CHAIN - 1):
                 k_hop(group)
-        theirs = query_strips(theirs_at) + kv_strips(theirs_at)
-        sums = query_strips(mine_at) + kv_strips(mine_at)
+        theirs = kv_strips(theirs_at, query_strips(theirs_at))
+        sums = kv_strips(mine_at, query_strips(mine_at))
         q_sent = [exchange(terms(ring)) for ring in q_rings]
         k_terms = [terms(ring) for ring in k_rings[:-1]]
         tail_rings, tail_spans = [k_rings[-1]], [(0, 2 * head)]

time: 344 us -> 350 us (1.017)
  starting transfers between devices: 54.3 us -> 61.3 us
  Pallas kernels: 112 us -> 118 us
  other arithmetic: 31.2 us -> 25.9 us
    ppermute x8, waiting for transfers between devices: 21.6 us -> 52.2 us  [z_shift(): return lax.ppermute(block, 'z', route)]
    ppermute x16, waiting for transfers between devices: 86.5 us -> 65.2 us  [z_ring(): lax.ppermute(block, 'z', [(i, (i + step) % CHAIN) for i in range(CHAIN)])]
    ppermute x13, waiting for transfers between devices: 20 us -> 9.53 us  [y_ring(): lax.ppermute(block, 'y', [(i, (i + step) % pair) for i in range(pair)])]
    ppermute x16, starting transfers between devices: 16.5 us -> 22.9 us  [z_ring(): lax.ppermute(block, 'z', [(i, (i + step) % CHAIN) for i in range(CHAIN)])]
    pallas_call x10, Pallas kernels: 24.3 us -> 28.9 us  [product(): pl.pallas_call(functools.partial(product_kernel, span[0]), grid_spec=pltp...]
  transfers between devices with their start and end apart: 41 -> 41, of which waited for: 20 -> 18; matrix products, arithmetic and copies ran while one was open for 10% -> 8% of each run, Pallas kernels for 31% -> 32%
where the time goes in v2:
time: 350 us; the launch traced here: 345 us
  waiting for transfers between devices  127 us (36%)
  Pallas kernels  118 us (34%)
  starting transfers between devices  61.3 us (18%)
  other arithmetic  25.9 us (7%)
  local copies, waits for them, and re-layouts  10.2 us (3%)
    ppermute x16, waiting for transfers between devices, z_ring(): lax.ppermute(block, 'z', [(i, (i + step) % CHAIN) for i in range(CHAIN)])  65.2 us
    ppermute x8, waiting for transfers between devices, z_shift(): return lax.ppermute(block, 'z', route)  52.2 us
    pallas_call x4, Pallas kernels, project(): pl.pallas_call(functools.partial(project_kernel, normed, lanes), grid=(st...  34 us
    pallas_call x4, Pallas kernels, input_strips(): pl.pallas_call(functools.partial(strip_kernel, pieces, partial is not Non...  32.4 us
    pallas_call x10, Pallas kernels, product(): pl.pallas_call(functools.partial(product_kernel, span[0]), grid_spec=pltp...  28.9 us
    ppermute x16, starting transfers between devices, z_ring(): lax.ppermute(block, 'z', [(i, (i + step) % CHAIN) for i in range(CHAIN)])  22.9 us
    ppermute x8, starting transfers between devices, z_shift(): return lax.ppermute(block, 'z', route)  20.4 us
    pallas_call x2, Pallas kernels, attention(): pl.pallas_call(functools.partial(attention_kernel, blocks, per_kv), out_s...  18.4 us
  transfers between devices with their start and end apart: 41, of which 18 were waited for; matrix products, arithmetic and copies ran while one was open for 8% of the time, Pallas kernels for 32%

profile of v2, /device:TPU:0, one launch (start us, length us, event | category | flops | bytes accessed | tf_op | source)
XLA Modules:
  0.0 344.7 jit_solution(13769439919705784202)
XLA Ops:
  1.9 8.7 %shard_map.119 = (f32[256,256]{1,0:T(8,128)}, f32[256,512]{1,0:T(8,128)}) custom-call(f32[256,3840]{1,0:T(8,128)} %source_ref.5, f32[3840,512]{1,0:T(8,128)} %refs_0_.15, f32[3840,512]{1,0:T(8,128)} %refs_0_.15, f32[3840,512]{1,0:T(8,128)} %refs_0_.15, f32[3840,512]{1,0:T(8,128)} %refs_1_.11, f32[3840,512]{1,0:T(8,128)} %refs_1_.11, f32[3840,512]{1,0:T(8,128)} %refs_1_.11, ...), custom_call_target="tpu_custom_call" | custom-call | flops 1024 | bytes 1024 | tf_op jit(solution)/shard_map/pallas_call | solution.py:200
  10.6 4.9 %collective-permute-start = (f32[256,512]{1,0:T(8,128)}, f32[256,512]{1,0:T(8,128)S(1)}, u32[]{:S(2)}, u32[]{:S(2)}) collective-permute-start(f32[256,512]{1,0:T(8,128)} %get-tuple-element.53.refs_11_), channel_id=1, source_target_pairs={{0,8},{8,16},{16,24},{1,9},{9,17},{17,25},{2,10},{10,18},{18,26},{... | collective-permute-start | bytes 1572872 | tf_op jit(solution)/shard_map/ppermute | solution.py:384
  15.6 8.7 %shard_map.120 = (f32[256,256]{1,0:T(8,128)}, f32[256,512]{1,0:T(8,128)}) custom-call(f32[256,3840]{1,0:T(8,128)} %source_ref.5, f32[3840,512]{1,0:T(8,128)} %refs_0_.15, f32[3840,512]{1,0:T(8,128)} %refs_0_.15, f32[3840,512]{1,0:T(8,128)} %refs_0_.15, f32[3840,512]{1,0:T(8,128)} %refs_1_.11, f32[3840,512]{1,0:T(8,128)} %refs_1_.11, f32[3840,512]{1,0:T(8,128)} %refs_1_.11, ...), custom_call_target="tpu_custom_call" | custom-call | flops 1024 | bytes 1024 | tf_op jit(solution)/shard_map/pallas_call | solution.py:200
  24.3 3.6 %collective-permute-start.2 = (f32[256,512]{1,0:T(8,128)}, f32[256,512]{1,0:T(8,128)S(1)}, u32[]{:S(2)}, u32[]{:S(2)}) collective-permute-start(f32[256,512]{1,0:T(8,128)} %get-tuple-element.55.refs_11_), channel_id=1, source_target_pairs={{0,8},{8,16},{16,24},{1,9},{9,17},{17,25},{2,10},{10,18},{18,26},{... | collective-permute-start | bytes 1572872 | tf_op jit(solution)/shard_map/ppermute | solution.py:384
  28.0 8.2 %shard_map.121.refs_0_ = f32[256,512]{1,0:T(8,128)} custom-call(f32[256,3840]{1,0:T(8,128)} %source_ref.5, f32[3840,1024]{1,0:T(8,128)} %refs_0_.13, f32[3840,1024]{1,0:T(8,128)} %refs_0_.13, f32[3840,1024]{1,0:T(8,128)} %refs_0_.13), custom_call_target="tpu_custom_call" | custom-call | flops 12079595520 | bytes 1024 | tf_op jit(solution)/shard_map/pallas_call | solution.py:200
  38.6 3.5 %collective-permute-start.1 = (f32[256,512]{1,0:T(8,128)S(1)}, f32[256,512]{1,0:T(8,128)S(1)}, u32[]{:S(2)}, u32[]{:S(2)}) collective-permute-start(f32[256,512]{1,0:T(8,128)S(1)} %collective-permute-done.refs_9_), channel_id=1, source_target_pairs={{0,8},{8,16},{16,24},{1,9},{9,17},{17,25},{2,10},{10,18},{18,26},{... | collective-permute-start | bytes 1572872 | tf_op jit(solution)/shard_map/ppermute | solution.py:384
  43.5 8.3 %shard_map.122.refs_0_ = f32[256,512]{1,0:T(8,128)} custom-call(f32[256,3840]{1,0:T(8,128)} %source_ref.5, f32[3840,1024]{1,0:T(8,128)} %refs_0_.13, f32[3840,1024]{1,0:T(8,128)} %refs_0_.13, f32[3840,1024]{1,0:T(8,128)} %refs_0_.13), custom_call_target="tpu_custom_call" | custom-call | flops 12079595520 | bytes 1024 | tf_op jit(solution)/shard_map/pallas_call | solution.py:200
  80.3 7.4 %collective-permute-done.5 = f32[240,256]{1,0:T(8,128)S(1)} collective-permute-done((f32[240,256]{1,0:T(8,128)S(1)}, f32[240,256]{1,0:T(8,128)S(1)}, u32[]{:S(2)}, u32[]{:S(2)}) %collective-permute-start.5) | collective-permute-done | bytes 245792 | tf_op jit(solution)/shard_map/ppermute | solution.py:387
  87.8 9.2 %shard_map.124 = (f32[256,512]{1,0:T(8,128)S(1)}, f32[256,512]{1,0:T(8,128)S(1)}, f32[256,512]{1,0:T(8,128)S(1)}, f32[256,512]{1,0:T(8,128)S(1)}, f32[256,512]{1...) custom-call(f32[256,512]{1,0:T(8,128)S(1)} %copy-done.13, f32[256,512]{1,0:T(8,128)S(1)} %copy-done.19, ...), custom_call_target="tpu_custom_call" | custom-call | flops 1024 | bytes 1024 | tf_op jit(solution)/shard_map/pallas_call | solution.py:138
  97.9 5.9 %collective-permute-start.13 = (f32[256,512]{1,0:T(8,128)S(1)}, f32[256,512]{1,0:T(8,128)S(1)}, u32[]{:S(2)}, u32[]{:S(2)}) collective-permute-start(f32[256,512]{1,0:T(8,128)S(1)} %get-tuple-element.73.refs_1_.refs_0_), channel_id=1, source_target_pairs={{0,8},{8,16},{16,24},{24,0},{1,9},{9,17},{17,25},{25,1},{2,10},{10... | collective-permute-start | bytes 1572872 | tf_op jit(solution)/shard_map/ppermute | solution.py:387
  105.8 9.1 %shard_map.125 = (f32[256,512]{1,0:T(8,128)S(1)}, f32[256,512]{1,0:T(8,128)S(1)}, f32[256,512]{1,0:T(8,128)S(1)}, f32[256,512]{1,0:T(8,128)S(1)}, f32[256,512]{1...) custom-call(f32[256,512]{1,0:T(8,128)S(1)} %copy-done.12, f32[256,512]{1,0:T(8,128)S(1)} %copy-done.18, ...), custom_call_target="tpu_custom_call" | custom-call | flops 1024 | bytes 1024 | tf_op jit(solution)/shard_map/pallas_call | solution.py:138
  123.1 10.2 %collective-permute-done.15.refs_2_ = f32[256,512]{1,0:T(8,128)S(1)} collective-permute-done((f32[256,512]{1,0:T(8,128)S(1)}, f32[256,512]{1,0:T(8,128)S(1)}, u32[]{:S(2)}, u32[]{:S(2)}) %collective-permute-start.15) | collective-permute-done | bytes 524320 | tf_op jit(solution)/shard_map/ppermute | solution.py:387
  133.4 9.4 %collective-permute-done.14 = f32[256,512]{1,0:T(8,128)} collective-permute-done((f32[256,512]{1,0:T(8,128)S(1)}, f32[256,512]{1,0:T(8,128)}, u32[]{:S(2)}, u32[]{:S(2)}) %collective-permute-start.14) | collective-permute-done | bytes 524320 | tf_op jit(solution)/shard_map/ppermute | solution.py:384
  149.6 7.7 %shard_map.127.refs_4_ = f32[2,960,256]{2,1,0:T(8,128)} custom-call(s32[2]{0:T(128)} %pad_add_fusion.1.strips_ref, f32[3840,1024]{1,0:T(8,128)} %refs_0_.13, f32[256,512]{1,0:T(8,128)} %copy-done.5, f32[256,512]{1,0:T(8,128)} %copy-done.7), custom_call_target="tpu_custom_call" | custom-call | flops 1024 | bytes 1024 | tf_op jit(solution)/shard_map/pallas_call | solution.py:346
  161.6 10.6 %collective-permute-done.16.far_ref = f32[256,512]{1,0:T(8,128)} collective-permute-done((f32[256,512]{1,0:T(8,128)}, f32[256,512]{1,0:T(8,128)}, u32[]{:S(2)}, u32[]{:S(2)}) %collective-permute-start.16) | collective-permute-done | bytes 524320 | tf_op jit(solution)/shard_map/ppermute | solution.py:384
  177.1 19.9 %collective-permute-done.20 = f32[256,512]{1,0:T(8,128)S(1)} collective-permute-done((f32[256,512]{1,0:T(8,128)S(1)}, f32[256,512]{1,0:T(8,128)S(1)}, u32[]{:S(2)}, u32[]{:S(2)}) %collective-permute-start.20) | collective-permute-done | bytes 524320 | tf_op jit(solution)/shard_map/ppermute | solution.py:384
  200.4 7.6 %shard_map.128.refs_4_ = f32[2,960,256]{2,1,0:T(8,128)} custom-call(s32[2]{0:T(128)} %pad_add_fusion.strips_ref, f32[3840,1024]{1,0:T(8,128)} %refs_0_.13, f32[256,512]{1,0:T(8,128)} %copy-done.5, f32[256,512]{1,0:T(8,128)} %copy-done.7), custom_call_target="tpu_custom_call" | custom-call | flops 1024 | bytes 1024 | tf_op jit(solution)/shard_map/pallas_call | solution.py:346
  217.5 4.4 %shard_map.134 = f32[480,512]{1,0:T(8,128)} custom-call(s32[2]{0:T(128)S(1)} %pad_add_fusion.2.place_ref, bf16[4,960,256]{2,1,0:T(8,128)(2,1)S(1)} %get-tuple-element.92.high_ref, bf16[4,960,256]{2,1,0:T(8,128)(2,1)S(1)} %get-tuple-element.93.low_ref, f32[256,512]{1,0:T(8,128)S(1)} %copy-done.6, f32[256,512]{1,0:T(8,128)S(1)} %collective-permute-done.13.refs_1_, ...), custom_call_target="tpu_custom_call" | custom-call | flops 1024 | bytes 1024 | tf_op jit(solution)/shard_map/pallas_call | solution.py:312
  221.9 4.4 %collective-permute-done.24.refs_1_ = f32[256,512]{1,0:T(8,128)S(1)} collective-permute-done((f32[256,512]{1,0:T(8,128)S(1)}, f32[256,512]{1,0:T(8,128)S(1)}, u32[]{:S(2)}, u32[]{:S(2)}) %collective-permute-start.24) | collective-permute-done | bytes 524320 | tf_op jit(solution)/shard_map/ppermute | solution.py:387
  227.1 10.3 %collective-permute-done.23.far_ref = f32[256,512]{1,0:T(8,128)S(1)} collective-permute-done((f32[256,512]{1,0:T(8,128)S(1)}, f32[256,512]{1,0:T(8,128)S(1)}, u32[]{:S(2)}, u32[]{:S(2)}) %collective-permute-start.23) | collective-permute-done | bytes 524320 | tf_op jit(solution)/shard_map/ppermute | solution.py:384
  238.6 8.7 %shard_map.131 = f32[2,960,256]{2,1,0:T(8,128)} custom-call(s32[2]{0:T(128)} %pad_add_fusion.1.strips_ref, f32[3840,512]{1,0:T(8,128)} %refs_0_.15, f32[3840,512]{1,0:T(8,128)} %refs_1_.11, f32[256,512]{1,0:T(8,128)} %copy-done.3, f32[256,512]{1,0:T(8,128)} %copy-done.1, f32[2,960,256]{2,1,0:T(8,128)} %shard_map.127.refs_4_), custom_call_target="tpu_custom_call" | custom-call | flops 1024 | bytes 1024 | tf_op jit(solution)/shard_map/pallas_call | solution.py:346
  248.5 4.4 %shard_map.136 = f32[480,512]{1,0:T(8,128)} custom-call(s32[2]{0:T(128)S(1)} %pad_add_fusion.2.place_ref, bf16[4,960,256]{2,1,0:T(8,128)(2,1)S(1)} %get-tuple-element.92.high_ref, bf16[4,960,256]{2,1,0:T(8,128)(2,1)S(1)} %get-tuple-element.93.low_ref, f32[256,512]{1,0:T(8,128)S(1)} %copy-done.8, f32[256,512]{1,0:T(8,128)S(1)} %collective-permute-done.19.refs_1_, ...), custom_call_target="tpu_custom_call" | custom-call | flops 1024 | bytes 1024 | tf_op jit(solution)/shard_map/pallas_call | solution.py:312
  253.8 10.1 %collective-permute-done.32.refs_2_ = f32[256,512]{1,0:T(8,128)} collective-permute-done((f32[256,512]{1,0:T(8,128)S(1)}, f32[256,512]{1,0:T(8,128)}, u32[]{:S(2)}, u32[]{:S(2)}) %collective-permute-start.32) | collective-permute-done | bytes 524320 | tf_op jit(solution)/shard_map/ppermute | solution.py:387
  263.9 11.1 %collective-permute-done.35.refs_1_ = f32[256,512]{1,0:T(8,128)S(1)} collective-permute-done((f32[256,512]{1,0:T(8,128)}, f32[256,512]{1,0:T(8,128)S(1)}, u32[]{:S(2)}, u32[]{:S(2)}) %collective-permute-start.35) | collective-permute-done | bytes 524320 | tf_op jit(solution)/shard_map/ppermute | solution.py:387
  275.0 8.4 %shard_map.130 = f32[2,960,256]{2,1,0:T(8,128)} custom-call(s32[2]{0:T(128)} %pad_add_fusion.strips_ref, f32[3840,512]{1,0:T(8,128)} %refs_0_.15, f32[3840,512]{1,0:T(8,128)} %refs_1_.11, f32[256,512]{1,0:T(8,128)} %copy-done.3, f32[256,512]{1,0:T(8,128)} %copy-done.1, f32[2,960,256]{2,1,0:T(8,128)} %shard_map.128.refs_4_), custom_call_target="tpu_custom_call" | custom-call | flops 1024 | bytes 1024 | tf_op jit(solution)/shard_map/pallas_call | solution.py:346
  286.4 3.5 %shard_map.138 = f32[480,512]{1,0:T(8,128)S(1)} custom-call(s32[2]{0:T(128)S(1)} %pad_add_fusion.2.place_ref, bf16[4,960,256]{2,1,0:T(8,128)(2,1)S(1)} %get-tuple-element.92.high_ref, bf16[4,960,256]{2,1,0:T(8,128)(2,1)S(1)} %get-tuple-element.93.low_ref, f32[256,512]{1,0:T(8,128)S(1)} %copy-done.4, f32[256,512]{1,0:T(8,128)S(1)} %collective-permute-done.24.refs_1_, ...), custom_call_target="tpu_custom_call" | custom-call | flops 1024 | bytes 1024 | tf_op jit(solution)/shard_map/pallas_call | solution.py:312
  289.8 7.3 %collective-permute-done.36.refs_2_ = f32[256,512]{1,0:T(8,128)S(1)} collective-permute-done((f32[256,512]{1,0:T(8,128)S(1)}, f32[256,512]{1,0:T(8,128)S(1)}, u32[]{:S(2)}, u32[]{:S(2)}) %collective-permute-start.36) | collective-permute-done | bytes 524320 | tf_op jit(solution)/shard_map/ppermute | solution.py:387
  298.4 8.8 %collective-permute-done.37.refs_3_ = f32[256,256]{1,0:T(8,128)S(1)} collective-permute-done((f32[256,256]{1,0:T(8,128)S(1)}, f32[256,256]{1,0:T(8,128)S(1)}, u32[]{:S(2)}, u32[]{:S(2)}) %collective-permute-start.37) | collective-permute-done | bytes 262176 | tf_op jit(solution)/shard_map/ppermute | solution.py:387
  314.4 3.4 shard_map.133
  319.2 3.5 %shard_map.135 = f32[480,512]{1,0:T(8,128)S(1)} custom-call(s32[2]{0:T(128)S(1)} %pad_add_fusion.2.place_ref, bf16[4,960,256]{2,1,0:T(8,128)(2,1)S(1)} %get-tuple-element.92.high_ref, bf16[4,960,256]{2,1,0:T(8,128)(2,1)S(1)} %get-tuple-element.93.low_ref, f32[256,512]{1,0:T(8,128)S(1)} %copy-done.8, f32[256,512]{1,0:T(8,128)S(1)} %copy-done.21, ...), custom_call_target="tpu_custom_call" | custom-call | flops 1024 | bytes 1024 | tf_op jit(solution)/shard_map/pallas_call | solution.py:312
  328.4 3.5 %shard_map.137 = f32[480,512]{1,0:T(8,128)S(1)} custom-call(s32[2]{0:T(128)S(1)} %pad_add_fusion.2.place_ref, bf16[4,960,256]{2,1,0:T(8,128)(2,1)S(1)} %get-tuple-element.92.high_ref, bf16[4,960,256]{2,1,0:T(8,128)(2,1)S(1)} %get-tuple-element.93.low_ref, f32[256,512]{1,0:T(8,128)S(1)} %copy-done.4, f32[256,512]{1,0:T(8,128)S(1)} %collective-permute-done.24.refs_1_, ...), custom_call_target="tpu_custom_call" | custom-call | flops 1024 | bytes 1024 | tf_op jit(solution)/shard_map/pallas_call | solution.py:312
  336.5 5.5 %collective-permute-done.39 = f32[480,256]{1,0:T(8,128)S(1)} collective-permute-done((f32[480,256]{1,0:T(8,128)S(1)}, f32[480,256]{1,0:T(8,128)S(1)}, u32[]{:S(2)}, u32[]{:S(2)}) %collective-permute-start.39) | collective-permute-done | bytes 491552 | tf_op jit(solution)/shard_map/ppermute | solution.py:390
  (223 shorter events, 102.4 us)
Async XLA Ops:
  10.6 25.5 %collective-permute-start = (f32[256,512]{1,0:T(8,128)}, f32[256,512]{1,0:T(8,128)S(1)}, u32[]{:S(2)}, u32[]{:S(2)}) collective-permute-start(f32[256,512]{1,0:T(8,128)} %get-tuple-element.53.refs_11_), channel_id=1, source_target_pairs={{0,8},{8,16},{16,24},{1,9},{9,17},{17,25},{2,10},{10,18},{18,26},{... | collective-permute-start | bytes 1572872 | tf_op jit(solution)/shard_map/ppermute | solution.py:384
  24.3 17.7 %collective-permute-start.2 = (f32[256,512]{1,0:T(8,128)}, f32[256,512]{1,0:T(8,128)S(1)}, u32[]{:S(2)}, u32[]{:S(2)}) collective-permute-start(f32[256,512]{1,0:T(8,128)} %get-tuple-element.55.refs_11_), channel_id=1, source_target_pairs={{0,8},{8,16},{16,24},{1,9},{9,17},{17,25},{2,10},{10,18},{18,26},{... | collective-permute-start | bytes 1572872 | tf_op jit(solution)/shard_map/ppermute | solution.py:384
  37.0 21.6 %collective-permute-start.7 = (f32[256,512]{1,0:T(8,128)}, f32[256,512]{1,0:T(8,128)S(1)}, u32[]{:S(2)}, u32[]{:S(2)}) collective-permute-start(f32[256,512]{1,0:T(8,128)} %broadcast_select_fusion.3), channel_id=1, source_target_pairs={{0,4},{4,0},{1,5},{5,1},{2,6},{6,2},{3,7},{7,3},{8,12},{12,8},{9,1... | collective-permute-start | bytes 1572872 | tf_op jit(solution)/shard_map/ppermute | solution.py:390
  38.6 23.0 %collective-permute-start.1 = (f32[256,512]{1,0:T(8,128)S(1)}, f32[256,512]{1,0:T(8,128)S(1)}, u32[]{:S(2)}, u32[]{:S(2)}) collective-permute-start(f32[256,512]{1,0:T(8,128)S(1)} %collective-permute-done.refs_9_), channel_id=1, source_target_pairs={{0,8},{8,16},{16,24},{1,9},{9,17},{17,25},{2,10},{10,18},{18,26},{... | collective-permute-start | bytes 1572872 | tf_op jit(solution)/shard_map/ppermute | solution.py:384
  42.9 18.7 %collective-permute-start.8 = (f32[256,512]{1,0:T(8,128)}, f32[256,512]{1,0:T(8,128)S(1)}, u32[]{:S(2)}, u32[]{:S(2)}) collective-permute-start(f32[256,512]{1,0:T(8,128)} %broadcast_select_fusion.2), channel_id=1, source_target_pairs={{0,4},{4,0},{1,5},{5,1},{2,6},{6,2},{3,7},{7,3},{8,12},{12,8},{9,1... | collective-permute-start | bytes 1572872 | tf_op jit(solution)/shard_map/ppermute | solution.py:390
  62.6 25.1 %collective-permute-start.9 = (f32[256,512]{1,0:T(8,128)}, f32[256,512]{1,0:T(8,128)}, u32[]{:S(2)}, u32[]{:S(2)}) collective-permute-start(f32[256,512]{1,0:T(8,128)} %broadcast_select_fusion.1), channel_id=1, source_target_pairs={{0,4},{4,0},{1,5},{5,1},{2,6},{6,2},{3,7},{7,3},{8,12},{12,8},{9,1... | collective-permute-start | bytes 1572872 | tf_op jit(solution)/shard_map/ppermute | solution.py:390
  76.0 29.8 %collective-permute-start.10 = (f32[256,512]{1,0:T(8,128)S(1)}, f32[256,512]{1,0:T(8,128)S(1)}, u32[]{:S(2)}, u32[]{:S(2)}) collective-permute-start(f32[256,512]{1,0:T(8,128)S(1)} %broadcast_select_fusion), channel_id=1, source_target_pairs={{0,4},{4,0},{1,5},{5,1},{2,6},{6,2},{3,7},{7,3},{8,12},{12,8},{9,1... | collective-permute-start | bytes 1572872 | tf_op jit(solution)/shard_map/ppermute | solution.py:390
  97.9 18.7 %collective-permute-start.13 = (f32[256,512]{1,0:T(8,128)S(1)}, f32[256,512]{1,0:T(8,128)S(1)}, u32[]{:S(2)}, u32[]{:S(2)}) collective-permute-start(f32[256,512]{1,0:T(8,128)S(1)} %get-tuple-element.73.refs_1_.refs_0_), channel_id=1, source_target_pairs={{0,8},{8,16},{16,24},{24,0},{1,9},{9,17},{17,25},{25,1},{2,10},{10... | collective-permute-start | bytes 1572872 | tf_op jit(solution)/shard_map/ppermute | solution.py:387
  104.8 28.6 %collective-permute-start.11 = (f32[256,512]{1,0:T(8,128)}, f32[256,512]{1,0:T(8,128)S(1)}, u32[]{:S(2)}, u32[]{:S(2)}) collective-permute-start(f32[256,512]{1,0:T(8,128)} %get-tuple-element.69), channel_id=1, source_target_pairs={{0,4},{4,0},{1,5},{5,1},{2,6},{6,2},{3,7},{7,3},{8,12},{12,8},{9,1... | collective-permute-start | bytes 1572872 | tf_op jit(solution)/shard_map/ppermute | solution.py:390
  116.6 16.8 %collective-permute-start.15 = (f32[256,512]{1,0:T(8,128)S(1)}, f32[256,512]{1,0:T(8,128)S(1)}, u32[]{:S(2)}, u32[]{:S(2)}) collective-permute-start(f32[256,512]{1,0:T(8,128)S(1)} %collective-permute-done.13.refs_1_), channel_id=1, source_target_pairs={{0,8},{8,16},{16,24},{24,0},{1,9},{9,17},{17,25},{25,1},{2,10},{10... | collective-permute-start | bytes 1572872 | tf_op jit(solution)/shard_map/ppermute | solution.py:387
  118.8 24.0 %collective-permute-start.14 = (f32[256,512]{1,0:T(8,128)S(1)}, f32[256,512]{1,0:T(8,128)}, u32[]{:S(2)}, u32[]{:S(2)}) collective-permute-start(f32[256,512]{1,0:T(8,128)S(1)} %select_add_fusion.1), channel_id=1, source_target_pairs={{8,0},{16,8},{24,16},{9,1},{17,9},{25,17},{10,2},{18,10},{26,18},{... | collective-permute-start | bytes 1572872 | tf_op jit(solution)/shard_map/ppermute | solution.py:384
  121.1 36.2 %collective-permute-start.27 = (f32[3,240,256]{2,1,0:T(8,128)}, f32[3,240,256]{2,1,0:T(8,128)}, u32[]{:S(2)}, u32[]{:S(2)}) collective-permute-start(f32[3,240,256]{2,1,0:T(8,128)} %pad_maximum_fusion.4), channel_id=1, source_target_pairs={{0,1},{1,0},{2,3},{3,2},{4,5},{5,4},{6,7},{7,6},{8,9},{9,8},{10,11... | collective-permute-start | bytes 2211848 | tf_op jit(solution)/shard_map/ppermute | solution.py:451
  121.1 40.4 %collective-permute-start.18 = (f32[256,512]{1,0:T(8,128)}, f32[256,512]{1,0:T(8,128)}, u32[]{:S(2)}, u32[]{:S(2)}) collective-permute-start(f32[256,512]{1,0:T(8,128)} %copy-done.44), channel_id=1, source_target_pairs={{0,4},{4,0},{1,5},{5,1},{2,6},{6,2},{3,7},{7,3},{8,12},{12,8},{9,1... | collective-permute-start | bytes 1572872 | tf_op jit(solution)/shard_map/ppermute | solution.py:390
  145.0 27.2 %collective-permute-start.16 = (f32[256,512]{1,0:T(8,128)}, f32[256,512]{1,0:T(8,128)}, u32[]{:S(2)}, u32[]{:S(2)}) collective-permute-start(f32[256,512]{1,0:T(8,128)} %add_add_fusion.1), channel_id=1, source_target_pairs={{8,0},{16,8},{24,16},{9,1},{17,9},{25,17},{10,2},{18,10},{26,18},{... | collective-permute-start | bytes 1572872 | tf_op jit(solution)/shard_map/ppermute | solution.py:384
  146.3 25.9 %collective-permute-start.19 = (f32[256,512]{1,0:T(8,128)S(1)}, f32[256,512]{1,0:T(8,128)S(1)}, u32[]{:S(2)}, u32[]{:S(2)}) collective-permute-start(f32[256,512]{1,0:T(8,128)S(1)} %get-tuple-element.84.refs_2_.refs_0_), channel_id=1, source_target_pairs={{0,8},{8,16},{16,24},{24,0},{1,9},{9,17},{17,25},{25,1},{2,10},{10... | collective-permute-start | bytes 1572872 | tf_op jit(solution)/shard_map/ppermute | solution.py:387
  160.1 53.8 %collective-permute-start.28 = (f32[3,480,256]{2,1,0:T(8,128)}, f32[3,480,256]{2,1,0:T(8,128)}, u32[]{:S(2)}, u32[]{:S(2)}) collective-permute-start(f32[3,480,256]{2,1,0:T(8,128)} %fusion.3), channel_id=1, source_target_pairs={{0,2},{1,3},{2,0},{3,1},{4,6},{5,7},{6,4},{7,5},{8,10},{9,11},{10,... | collective-permute-start | bytes 4423688 | tf_op jit(solution)/shard_map/ppermute | solution.py:455
  172.3 24.8 %collective-permute-start.20 = (f32[256,512]{1,0:T(8,128)S(1)}, f32[256,512]{1,0:T(8,128)S(1)}, u32[]{:S(2)}, u32[]{:S(2)}) collective-permute-start(f32[256,512]{1,0:T(8,128)S(1)} %select_add_fusion), channel_id=1, source_target_pairs={{8,0},{16,8},{24,16},{9,1},{17,9},{25,17},{10,2},{18,10},{26,18},{... | collective-permute-start | bytes 1572872 | tf_op jit(solution)/shard_map/ppermute | solution.py:384
  173.5 36.0 %collective-permute-start.22 = (f32[256,512]{1,0:T(8,128)S(1)}, f32[256,512]{1,0:T(8,128)}, u32[]{:S(2)}, u32[]{:S(2)}) collective-permute-start(f32[256,512]{1,0:T(8,128)S(1)} %collective-permute-done.15.refs_2_), channel_id=1, source_target_pairs={{0,8},{8,16},{16,24},{24,0},{1,9},{9,17},{17,25},{25,1},{2,10},{10... | collective-permute-start | bytes 1572872 | tf_op jit(solution)/shard_map/ppermute | solution.py:387
  176.2 33.4 %collective-permute-start.17 = (f32[256,512]{1,0:T(8,128)}, f32[256,512]{1,0:T(8,128)S(1)}, u32[]{:S(2)}, u32[]{:S(2)}) collective-permute-start(f32[256,512]{1,0:T(8,128)} %get-tuple-element.79), channel_id=1, source_target_pairs={{0,4},{4,0},{1,5},{5,1},{2,6},{6,2},{3,7},{7,3},{8,12},{12,8},{9,1... | collective-permute-start | bytes 1572872 | tf_op jit(solution)/shard_map/ppermute | solution.py:390
  209.5 16.8 %collective-permute-start.24 = (f32[256,512]{1,0:T(8,128)S(1)}, f32[256,512]{1,0:T(8,128)S(1)}, u32[]{:S(2)}, u32[]{:S(2)}) collective-permute-start(f32[256,512]{1,0:T(8,128)S(1)} %shard_map.126.refs_2_.refs_0_), channel_id=1, source_target_pairs={{0,8},{8,16},{16,24},{24,0},{1,9},{9,17},{17,25},{25,1},{2,10},{10... | collective-permute-start | bytes 1572872 | tf_op jit(solution)/shard_map/ppermute | solution.py:387
  211.2 26.2 %collective-permute-start.23 = (f32[256,512]{1,0:T(8,128)S(1)}, f32[256,512]{1,0:T(8,128)S(1)}, u32[]{:S(2)}, u32[]{:S(2)}) collective-permute-start(f32[256,512]{1,0:T(8,128)S(1)} %add_add_fusion), channel_id=1, source_target_pairs={{8,0},{16,8},{24,16},{9,1},{17,9},{25,17},{10,2},{18,10},{26,18},{... | collective-permute-start | bytes 1572872 | tf_op jit(solution)/shard_map/ppermute | solution.py:384
  226.3 21.6 %collective-permute-start.30 = (f32[256,512]{1,0:T(8,128)}, f32[256,512]{1,0:T(8,128)}, u32[]{:S(2)}, u32[]{:S(2)}) collective-permute-start(f32[256,512]{1,0:T(8,128)} %collective-permute-done.21.refs_2_), channel_id=1, source_target_pairs={{0,8},{8,16},{16,24},{24,0},{1,9},{9,17},{17,25},{25,1},{2,10},{10... | collective-permute-start | bytes 1572872 | tf_op jit(solution)/shard_map/ppermute | solution.py:387
  226.3 37.6 %collective-permute-start.29 = (f32[480,512]{1,0:T(8,128)}, f32[480,512]{1,0:T(8,128)}, u32[]{:S(2)}, u32[]{:S(2)}) collective-permute-start(f32[480,512]{1,0:T(8,128)} %shard_map.134), channel_id=1, source_target_pairs={{0,4},{4,0},{1,5},{5,1},{2,6},{6,2},{3,7},{7,3},{8,12},{12,8},{9,1... | collective-permute-start | bytes 2949128 | tf_op jit(solution)/shard_map/ppermute | solution.py:390
  247.3 62.5 %collective-permute-start.25 = (f32[2,960,256]{2,1,0:T(8,128)}, f32[2,960,256]{2,1,0:T(8,128)}, u32[]{:S(2)}, u32[]{:S(2)}) collective-permute-start(f32[2,960,256]{2,1,0:T(8,128)} %shard_map.131), channel_id=1, source_target_pairs={{0,1},{1,0},{2,3},{3,2},{4,5},{5,4},{6,7},{7,6},{8,9},{9,8},{10,11... | collective-permute-start | bytes 5898248 | tf_op jit(solution)/shard_map/ppermute | solution.py:451
  247.3 16.6 %collective-permute-start.32 = (f32[256,512]{1,0:T(8,128)S(1)}, f32[256,512]{1,0:T(8,128)}, u32[]{:S(2)}, u32[]{:S(2)}) collective-permute-start(f32[256,512]{1,0:T(8,128)S(1)} %collective-permute-done.24.refs_1_), channel_id=1, source_target_pairs={{0,8},{8,16},{16,24},{24,0},{1,9},{9,17},{17,25},{25,1},{2,10},{10... | collective-permute-start | bytes 1572872 | tf_op jit(solution)/shard_map/ppermute | solution.py:387
  247.8 27.2 %collective-permute-start.35 = (f32[256,512]{1,0:T(8,128)}, f32[256,512]{1,0:T(8,128)S(1)}, u32[]{:S(2)}, u32[]{:S(2)}) collective-permute-start(f32[256,512]{1,0:T(8,128)} %copy-done.1), channel_id=1, source_target_pairs={{0,8},{8,16},{16,24},{24,0},{1,9},{9,17},{17,25},{25,1},{2,10},{10... | collective-permute-start | bytes 1572872 | tf_op jit(solution)/shard_map/ppermute | solution.py:387
  252.9 36.9 %collective-permute-start.31 = (f32[480,512]{1,0:T(8,128)}, f32[480,512]{1,0:T(8,128)}, u32[]{:S(2)}, u32[]{:S(2)}) collective-permute-start(f32[480,512]{1,0:T(8,128)} %shard_map.136), channel_id=1, source_target_pairs={{0,4},{4,0},{1,5},{5,1},{2,6},{6,2},{3,7},{7,3},{8,12},{12,8},{9,1... | collective-permute-start | bytes 2949128 | tf_op jit(solution)/shard_map/ppermute | solution.py:390
  263.9 22.5 %collective-permute-start.33 = (f32[256,512]{1,0:T(8,128)}, f32[256,512]{1,0:T(8,128)}, u32[]{:S(2)}, u32[]{:S(2)}) collective-permute-start(f32[256,512]{1,0:T(8,128)} %collective-permute-done.32.refs_2_), channel_id=1, source_target_pairs={{0,8},{8,16},{16,24},{24,0},{1,9},{9,17},{17,25},{25,1},{2,10},{10... | collective-permute-start | bytes 1572872 | tf_op jit(solution)/shard_map/ppermute | solution.py:387
  275.0 22.1 %collective-permute-start.36 = (f32[256,512]{1,0:T(8,128)S(1)}, f32[256,512]{1,0:T(8,128)S(1)}, u32[]{:S(2)}, u32[]{:S(2)}) collective-permute-start(f32[256,512]{1,0:T(8,128)S(1)} %collective-permute-done.35.refs_1_), channel_id=1, source_target_pairs={{0,8},{8,16},{16,24},{24,0},{1,9},{9,17},{17,25},{25,1},{2,10},{10... | collective-permute-start | bytes 1572872 | tf_op jit(solution)/shard_map/ppermute | solution.py:387
  297.5 37.7 %collective-permute-start.34 = (f32[480,512]{1,0:T(8,128)S(1)}, f32[480,512]{1,0:T(8,128)S(1)}, u32[]{:S(2)}, u32[]{:S(2)}) collective-permute-start(f32[480,512]{1,0:T(8,128)S(1)} %shard_map.138), channel_id=1, source_target_pairs={{0,4},{4,0},{1,5},{5,1},{2,6},{6,2},{3,7},{7,3},{8,12},{12,8},{9,1... | collective-permute-start | bytes 2949128 | tf_op jit(solution)/shard_map/ppermute | solution.py:390
  308.8 26.3 %collective-permute-start.40 = (f32[480,256]{1,0:T(8,128)S(1)}, f32[480,256]{1,0:T(8,128)S(1)}, u32[]{:S(2)}, u32[]{:S(2)}) collective-permute-start(f32[480,256]{1,0:T(8,128)S(1)} %shard_map.142), channel_id=1, source_target_pairs={{0,4},{4,0},{1,5},{5,1},{2,6},{6,2},{3,7},{7,3},{8,12},{12,8},{9,1... | collective-permute-start | bytes 1474568 | tf_op jit(solution)/shard_map/ppermute | solution.py:390
  311.6 31.5 %collective-permute-start.26 = (f32[960,256]{1,0:T(8,128)S(1)}, f32[960,256]{1,0:T(8,128)S(1)}, u32[]{:S(2)}, u32[]{:S(2)}) collective-permute-start(f32[960,256]{1,0:T(8,128)S(1)} %slice_bitcast_fusion), channel_id=1, source_target_pairs={{0,2},{1,3},{2,0},{3,1},{4,6},{5,7},{6,4},{7,5},{8,10},{9,11},{10,... | collective-permute-start | bytes 2949128 | tf_op jit(solution)/shard_map/ppermute | solution.py:455
  (65 other events, 882.2 us)

commit v3 on v2

--- a/solution.py
+++ b/solution.py
@@ -433,17 +433,17 @@
         for group in groups:
             fours.append(z_shift(after(two[group], own[-1]), 1))
         for group in groups:
-            three_back = farthest(group, fours[group], *ones, *fours[:group], hidden_rows)
+            three_back = farthest(group, fours[group], *ones, *fours[: group + 1], hidden_rows)
             windows.append([fours[group], three_back, two[group], ones[group], own[group]])
     else:
         for group in groups:
             windows.append([shifted(own[group], d) for d in range(reach, 0, -1)] + [own[group]])
-    shared = after(hidden_rows, *fours) if fours else hidden_rows
-    pieces = []
-    for step in range(CHAIN - 1, 0, -1):
-        target = (along + step) % CHAIN
-        start = target * slab + member * piece
-        pieces.append(z_ring(lax.dynamic_slice_in_dim(shared, start, piece, 0), step))
+    def sent_along(source, step):
+        start = (along + step) % CHAIN * slab + member * piece
+        return z_shift(lax.dynamic_slice_in_dim(source, start, piece, 0), step)
+
+    from_above = [sent_along(hidden_rows, -step) for step in range(1, CHAIN)]
+
     chips = members // CORES
     chip, core = member // CORES, member % CORES
 
@@ -460,17 +460,9 @@
         start = (len(blocks) - 1 - index) * size
         return lax.dynamic_slice_in_dim(both, start, len(blocks) * size, axis)
 
-    mine = jnp.stack(pieces)
-    chip_rows = in_order([to_core(mine), mine], core, 1)
-    arrivals = [to_chip(chip_rows, step) for step in range(chips - 1, 0, -1)]
-    others = in_order(arrivals + [chip_rows], chip, 1)
-    own_slab = lax.dynamic_slice_in_dim(hidden_rows, along * slab, slab, 0)
-    place = jnp.stack([along, across]).astype(jnp.int32)
-    turned = turn(place, others, own_slab)
-
     attended, d_query, parts = [], [], []
     for group in groups:
-        ready = attended or pieces
+        ready = attended or from_above
         out, d_q, d_kv = attention(
             after(queries[group], *ready),
             q_columns(grad_out, group),
@@ -486,6 +478,20 @@
         d_query.append(d_q)
         parts.append(d_kv)
 
+    upward = after(hidden_rows, *attended[:1])
+    from_below = [sent_along(upward, step) for step in range(1, CHAIN)]
+    pieces = [
+        jnp.where(along >= step, from_below[step - 1], from_above[CHAIN - 1 - step])
+        for step in range(CHAIN - 1, 0, -1)
+    ]
+    mine = jnp.stack(pieces)
+    chip_rows = in_order([to_core(mine), mine], core, 1)
+    arrivals = [to_chip(chip_rows, step) for step in range(chips - 1, 0, -1)]
+    others = in_order(arrivals + [chip_rows], chip, 1)
+    own_slab = lax.dynamic_slice_in_dim(hidden_rows, along * slab, slab, 0)
+    place = jnp.stack([along, across]).astype(jnp.int32)
+    turned = turn(place, others, own_slab)
+
     strip = width // members
     turns = [(chip + step) % chips for step in range(chips)]
     theirs_at = jnp.stack([c * CORES + 1 - core for c in turns]).astype(jnp.int32)
@@ -545,30 +551,30 @@
         q_hop(0)
         far_return(0, q_rings[0][1], *attended)
         q_hop(0)
-        near_return(0, [q_rings[0][2]], [])
+        near_return(0, [q_rings[0][2]], from_below)
         q_hop(1)
         theirs_q = query_strips(theirs_at)
         far_return(1, theirs_q, q_rings[1][1])
         q_hop(0)
         mine_q = query_strips(mine_at)
         q_hop(1)
+        near_return(1, [mine_q, q_rings[0][3]], [q_rings[1][2]])
         k_hop(0)
-        near_return(1, [mine_q, q_rings[0][3], q_rings[1][2]], [k_rings[0][1]])
         q_terms = [terms(q_rings[0])]
         q_hop(1, *q_terms[0])
         k_hop(0)
         theirs = kv_strips(theirs_at, theirs_q)
         q_sent = [exchange(q_terms[0])]
-        k_hop(1)
+        k_hop(1, theirs)
         q_terms.append(terms(q_rings[1]))
-        k_hop(0, *q_terms[1])
-        sums = kv_strips(mine_at, mine_q)
-        k_hop(1, theirs, *q_sent[0])
+        sums = kv_strips(mine_at, mine_q) + to_core(theirs)
+        from_chips = [to_chip(sums[step], step) for step in range(1, chips)]
+        k_hop(0, sums, *q_terms[1])
+        k_hop(1, *q_sent[0])
         k_terms = [terms(k_rings[0])]
         q_sent.append(exchange(q_terms[1]))
-        last = after(k_rings[1][-1], sent[-2], sums, *k_terms[0], *q_sent[1])
-        tails = [z_ring(last[:, head:], 1)]
-        tails.append(z_ring(after(last[:, :head], tails[0]), 1))
+        last = after(k_rings[1][-1], sent[-2], *from_chips, *k_terms[0], *q_sent[1])
+        tails = [z_ring(last[:, head:], 1), z_ring(last[:, :head], 1)]
         tail_rings = [k_rings[1] + [tail] for tail in tails]
         tail_spans = [(head, head), (0, head)]
     else:
@@ -586,13 +592,14 @@
         theirs = kv_strips(theirs_at, query_strips(theirs_at))
         sums = kv_strips(mine_at, query_strips(mine_at))
         q_sent = [exchange(terms(ring)) for ring in q_rings]
+        sums = sums + to_core(theirs)
+        from_chips = [to_chip(sums[step], step) for step in range(1, chips)]
         k_terms = [terms(ring) for ring in k_rings[:-1]]
         tail_rings, tail_spans = [k_rings[-1]], [(0, 2 * head)]
 
-    sums = sums + to_core(theirs)
     grad_input = sums[0]
-    for step in range(1, chips):
-        grad_input = grad_input + to_chip(sums[step], step)
+    for arrival in from_chips:
+        grad_input = grad_input + arrival
 
     def finish(ring, arrived, span=(0, 0)):
         total = product_of(ring, 0, span)
@@ -601,7 +608,8 @@
         return total
 
     grad_query = [finish(ring, arrived) for ring, arrived in zip(q_rings, q_sent)]
-    tail_sent = [exchange(terms(ring, span)) for ring, span in zip(tail_rings, tail_spans)]
+    tail_terms = [terms(ring, span) for ring, span in zip(tail_rings, tail_spans)]
+    tail_sent = [exchange(term) for term in tail_terms]
     grad_kv = [finish(ring, exchange(term)) for ring, term in zip(k_rings, k_terms)]
     ends = [finish(*each) for each in zip(tail_rings, tail_sent, tail_spans)]
     grad_kv.append(jnp.concatenate(ends[::-1], axis=1))

time: 350 us -> 343 us (0.980)
  waiting for transfers between devices: 127 us -> 96.9 us
  starting transfers between devices: 61.3 us -> 81.9 us
  local copies, waits for them, and re-layouts: 10.2 us -> 17.1 us
  Pallas kernels: 118 us -> 112 us
    ppermute x8 -> x14, waiting for transfers between devices: 52.2 us -> 29.5 us  [z_shift(): return lax.ppermute(block, 'z', route)]
    ppermute x8 -> x14, starting transfers between devices: 20.4 us -> 35.4 us  [z_shift(): return lax.ppermute(block, 'z', route)]
    ppermute x16 -> x13, waiting for transfers between devices: 65.2 us -> 54.5 us  [z_ring(): lax.ppermute(block, 'z', [(i, (i + step) % CHAIN) for i in range(CHAIN)])]
    ppermute x13, starting transfers between devices: 14.9 us -> 22.2 us  [y_ring(): lax.ppermute(block, 'y', [(i, (i + step) % pair) for i in range(pair)])]
    unnamed x112 -> x104, local copies, waits for them, and re-layouts: 6.15 us -> 11.9 us
    pallas_call x10, Pallas kernels: 28.9 us -> 23.4 us  [product(): pl.pallas_call(functools.partial(product_kernel, span[0]), grid_spec=pltp...]
    ppermute x16 -> x13, starting transfers between devices: 22.9 us -> 18.2 us  [z_ring(): lax.ppermute(block, 'z', [(i, (i + step) % CHAIN) for i in range(CHAIN)])]
  transfers between devices with their start and end apart: 41 -> 44, of which waited for: 18 -> 16; matrix products, arithmetic and copies ran while one was open for 8% -> 9% of each run, Pallas kernels for 32% -> 31%
where the time goes in v3:
time: 343 us; the launch traced here: 337 us
  Pallas kernels  112 us (33%)
  waiting for transfers between devices  96.9 us (28%)
  starting transfers between devices  81.9 us (24%)
  other arithmetic  27.6 us (8%)
  local copies, waits for them, and re-layouts  17.1 us (5%)
    ppermute x13, waiting for transfers between devices, z_ring(): lax.ppermute(block, 'z', [(i, (i + step) % CHAIN) for i in range(CHAIN)])  54.5 us
    ppermute x14, starting transfers between devices, z_shift(): return lax.ppermute(block, 'z', route)  35.4 us
    pallas_call x4, Pallas kernels, project(): pl.pallas_call(functools.partial(project_kernel, normed, lanes), grid=(st...  34 us
    pallas_call x4, Pallas kernels, input_strips(): pl.pallas_call(functools.partial(strip_kernel, pieces, partial is not Non...  32.3 us
    ppermute x14, waiting for transfers between devices, z_shift(): return lax.ppermute(block, 'z', route)  29.5 us
    pallas_call x10, Pallas kernels, product(): pl.pallas_call(functools.partial(product_kernel, span[0]), grid_spec=pltp...  23.4 us
    ppermute x13, starting transfers between devices, y_ring(): lax.ppermute(block, 'y', [(i, (i + step) % pair) for i in range(pair)])  22.2 us
    ppermute x13, starting transfers between devices, z_ring(): lax.ppermute(block, 'z', [(i, (i + step) % CHAIN) for i in range(CHAIN)])  18.2 us
  transfers between devices with their start and end apart: 44, of which 16 were waited for; matrix products, arithmetic and copies ran while one was open for 9% of the time, Pallas kernels for 31%

profile of v3, /device:TPU:0, one launch (start us, length us, event | category | flops | bytes accessed | tf_op | source)
XLA Modules:
  0.0 337.2 jit_solution(13917134460482718700)
XLA Ops:
  1.9 8.7 %shard_map.119 = (f32[256,256]{1,0:T(8,128)}, f32[256,512]{1,0:T(8,128)}) custom-call(f32[256,3840]{1,0:T(8,128)} %source_ref.5, f32[3840,512]{1,0:T(8,128)} %refs_0_.15, f32[3840,512]{1,0:T(8,128)} %refs_0_.15, f32[3840,512]{1,0:T(8,128)} %refs_0_.15, f32[3840,512]{1,0:T(8,128)} %refs_1_.11, f32[3840,512]{1,0:T(8,128)} %refs_1_.11, f32[3840,512]{1,0:T(8,128)} %refs_1_.11, ...), custom_call_target="tpu_custom_call" | custom-call | flops 1024 | bytes 1024 | tf_op jit(solution)/shard_map/pallas_call | solution.py:200
  10.6 4.9 %collective-permute-start.3 = (f32[256,512]{1,0:T(8,128)}, f32[256,512]{1,0:T(8,128)S(1)}, u32[]{:S(2)}, u32[]{:S(2)}) collective-permute-start(f32[256,512]{1,0:T(8,128)} %get-tuple-element.53.refs_11_), channel_id=1, source_target_pairs={{0,8},{8,16},{16,24},{1,9},{9,17},{17,25},{2,10},{10,18},{18,26},{... | collective-permute-start | bytes 1572872 | tf_op jit(solution)/shard_map/ppermute | solution.py:384
  15.6 8.7 %shard_map.120 = (f32[256,256]{1,0:T(8,128)}, f32[256,512]{1,0:T(8,128)}) custom-call(f32[256,3840]{1,0:T(8,128)} %source_ref.5, f32[3840,512]{1,0:T(8,128)} %refs_0_.15, f32[3840,512]{1,0:T(8,128)} %refs_0_.15, f32[3840,512]{1,0:T(8,128)} %refs_0_.15, f32[3840,512]{1,0:T(8,128)} %refs_1_.11, f32[3840,512]{1,0:T(8,128)} %refs_1_.11, f32[3840,512]{1,0:T(8,128)} %refs_1_.11, ...), custom_call_target="tpu_custom_call" | custom-call | flops 1024 | bytes 1024 | tf_op jit(solution)/shard_map/pallas_call | solution.py:200
  24.3 3.6 %collective-permute-start.6 = (f32[256,512]{1,0:T(8,128)}, f32[256,512]{1,0:T(8,128)S(1)}, u32[]{:S(2)}, u32[]{:S(2)}) collective-permute-start(f32[256,512]{1,0:T(8,128)} %get-tuple-element.55.refs_11_), channel_id=1, source_target_pairs={{0,8},{8,16},{16,24},{1,9},{9,17},{17,25},{2,10},{10,18},{18,26},{... | collective-permute-start | bytes 1572872 | tf_op jit(solution)/shard_map/ppermute | solution.py:384
  27.9 8.2 %shard_map.121.refs_0_ = f32[256,512]{1,0:T(8,128)} custom-call(f32[256,3840]{1,0:T(8,128)} %source_ref.5, f32[3840,1024]{1,0:T(8,128)} %refs_0_.13, f32[3840,1024]{1,0:T(8,128)} %refs_0_.13, f32[3840,1024]{1,0:T(8,128)} %refs_0_.13), custom_call_target="tpu_custom_call" | custom-call | flops 12079595520 | bytes 1024 | tf_op jit(solution)/shard_map/pallas_call | solution.py:200
  38.5 3.5 %collective-permute-start.4 = (f32[256,512]{1,0:T(8,128)S(1)}, f32[256,512]{1,0:T(8,128)S(1)}, u32[]{:S(2)}, u32[]{:S(2)}) collective-permute-start(f32[256,512]{1,0:T(8,128)S(1)} %collective-permute-done.3.refs_9_), channel_id=1, source_target_pairs={{0,8},{8,16},{16,24},{1,9},{9,17},{17,25},{2,10},{10,18},{18,26},{... | collective-permute-start | bytes 1572872 | tf_op jit(solution)/shard_map/ppermute | solution.py:384
  43.4 8.3 %shard_map.122.refs_0_ = f32[256,512]{1,0:T(8,128)} custom-call(f32[256,3840]{1,0:T(8,128)} %source_ref.5, f32[3840,1024]{1,0:T(8,128)} %refs_0_.13, f32[3840,1024]{1,0:T(8,128)} %refs_0_.13, f32[3840,1024]{1,0:T(8,128)} %refs_0_.13), custom_call_target="tpu_custom_call" | custom-call | flops 12079595520 | bytes 1024 | tf_op jit(solution)/shard_map/pallas_call | solution.py:200
  61.8 5.1 %collective-permute-start.9 = (f32[256,512]{1,0:T(8,128)S(1)}, f32[256,512]{1,0:T(8,128)S(1)}, u32[]{:S(2)}, u32[]{:S(2)}) collective-permute-start(f32[256,512]{1,0:T(8,128)S(1)} %collective-permute-done.6.refs_9_), channel_id=1, source_target_pairs={{0,8},{8,16},{16,24},{1,9},{9,17},{17,25},{2,10},{10,18},{18,26},{... | collective-permute-start | bytes 1572872 | tf_op jit(solution)/shard_map/ppermute | solution.py:384
  70.4 8.0 %collective-permute-done.1 = f32[240,256]{1,0:T(8,128)} collective-permute-done((f32[240,256]{1,0:T(8,128)}, f32[240,256]{1,0:T(8,128)}, u32[]{:S(2)}, u32[]{:S(2)}) %collective-permute-start.1) | collective-permute-done | bytes 245792 | tf_op jit(solution)/shard_map/ppermute | solution.py:384
  80.1 9.2 %shard_map.124 = (f32[256,512]{1,0:T(8,128)S(1)}, f32[256,512]{1,0:T(8,128)S(1)}, f32[256,512]{1,0:T(8,128)S(1)}, f32[256,512]{1,0:T(8,128)S(1)}, f32[256,512]{1...) custom-call(f32[256,512]{1,0:T(8,128)S(1)} %copy-done.15, f32[256,512]{1,0:T(8,128)S(1)} %get-tuple-element.108.refs_1_, ...), custom_call_target="tpu_custom_call" | custom-call | flops 1024 | bytes 1024 | tf_op jit(solution)/shard_map/pallas_call | solution.py:138
  92.9 5.2 %collective-permute-start.13 = (f32[256,512]{1,0:T(8,128)S(1)}, f32[256,512]{1,0:T(8,128)S(1)}, u32[]{:S(2)}, u32[]{:S(2)}) collective-permute-start(f32[256,512]{1,0:T(8,128)S(1)} %get-tuple-element.72.refs_1_.refs_0_), channel_id=1, source_target_pairs={{0,8},{8,16},{16,24},{24,0},{1,9},{9,17},{17,25},{25,1},{2,10},{10... | collective-permute-start | bytes 1572872 | tf_op jit(solution)/shard_map/ppermute | solution.py:387
  99.6 8.1 %shard_map.125 = (f32[256,512]{1,0:T(8,128)S(1)}, f32[256,512]{1,0:T(8,128)S(1)}, f32[256,512]{1,0:T(8,128)S(1)}, f32[256,512]{1,0:T(8,128)}, f32[256,512]{1,0:T...) custom-call(f32[256,512]{1,0:T(8,128)S(1)} %copy-done.14, f32[256,512]{1,0:T(8,128)S(1)} %get-tuple-element.107.refs_1_, ...), custom_call_target="tpu_custom_call" | custom-call | flops 1024 | bytes 1024 | tf_op jit(solution)/shard_map/pallas_call | solution.py:138
  118.0 7.6 %shard_map.127.refs_4_ = f32[2,960,256]{2,1,0:T(8,128)} custom-call(s32[2]{0:T(128)} %pad_add_fusion.1.strips_ref, f32[3840,1024]{1,0:T(8,128)} %refs_0_.13, f32[256,512]{1,0:T(8,128)} %copy-done.7, f32[256,512]{1,0:T(8,128)} %copy-done.9), custom_call_target="tpu_custom_call" | custom-call | flops 1024 | bytes 1024 | tf_op jit(solution)/shard_map/pallas_call | solution.py:346
  132.7 5.4 %collective-permute-done.15.refs_2_ = f32[256,512]{1,0:T(8,128)S(1)} collective-permute-done((f32[256,512]{1,0:T(8,128)S(1)}, f32[256,512]{1,0:T(8,128)S(1)}, u32[]{:S(2)}, u32[]{:S(2)}) %collective-permute-start.15) | collective-permute-done | bytes 524320 | tf_op jit(solution)/shard_map/ppermute | solution.py:387
  142.2 4.8 %collective-permute-start.17 = (f32[240,256]{1,0:T(8,128)S(1)}, f32[240,256]{1,0:T(8,128)S(1)}, u32[]{:S(2)}, u32[]{:S(2)}) collective-permute-start(f32[240,256]{1,0:T(8,128)S(1)} %get-tuple-element.103), channel_id=1, source_target_pairs={{0,8},{8,16},{16,24},{1,9},{9,17},{17,25},{2,10},{10,18},{18,26},{... | collective-permute-start | bytes 737288 | tf_op jit(solution)/shard_map/ppermute | solution.py:384
  149.1 12.8 %collective-permute-done.16.far_ref = f32[256,512]{1,0:T(8,128)S(1)} collective-permute-done((f32[256,512]{1,0:T(8,128)S(1)}, f32[256,512]{1,0:T(8,128)S(1)}, u32[]{:S(2)}, u32[]{:S(2)}) %collective-permute-start.16) | collective-permute-done | bytes 524320 | tf_op jit(solution)/shard_map/ppermute | solution.py:384
  167.7 7.6 %shard_map.128.refs_4_ = f32[2,960,256]{2,1,0:T(8,128)} custom-call(s32[2]{0:T(128)} %pad_add_fusion.strips_ref, f32[3840,1024]{1,0:T(8,128)} %refs_0_.13, f32[256,512]{1,0:T(8,128)} %copy-done.7, f32[256,512]{1,0:T(8,128)} %copy-done.9), custom_call_target="tpu_custom_call" | custom-call | flops 1024 | bytes 1024 | tf_op jit(solution)/shard_map/pallas_call | solution.py:346
  178.1 6.7 %collective-permute-done.24.refs_3_ = f32[256,512]{1,0:T(8,128)S(1)} collective-permute-done((f32[256,512]{1,0:T(8,128)S(1)}, f32[256,512]{1,0:T(8,128)S(1)}, u32[]{:S(2)}, u32[]{:S(2)}) %collective-permute-start.24) | collective-permute-done | bytes 524320 | tf_op jit(solution)/shard_map/ppermute | solution.py:387
  188.9 4.5 %collective-permute-start.30 = (f32[3,480,256]{2,1,0:T(8,128)}, f32[3,480,256]{2,1,0:T(8,128)}, u32[]{:S(2)}, u32[]{:S(2)}) collective-permute-start(f32[3,480,256]{2,1,0:T(8,128)} %fusion.3), channel_id=1, source_target_pairs={{0,2},{1,3},{2,0},{3,1},{4,6},{5,7},{6,4},{7,5},{8,10},{9,11},{10,... | collective-permute-start | bytes 4423688 | tf_op jit(solution)/shard_map/ppermute | solution.py:455
  197.6 3.9 %collective-permute-done.26.refs_2_ = f32[256,512]{1,0:T(8,128)} collective-permute-done((f32[256,512]{1,0:T(8,128)S(1)}, f32[256,512]{1,0:T(8,128)}, u32[]{:S(2)}, u32[]{:S(2)}) %collective-permute-start.26) | collective-permute-done | bytes 524320 | tf_op jit(solution)/shard_map/ppermute | solution.py:387
  201.5 7.2 %collective-permute-done.25.far_ref = f32[256,512]{1,0:T(8,128)} collective-permute-done((f32[256,512]{1,0:T(8,128)}, f32[256,512]{1,0:T(8,128)}, u32[]{:S(2)}, u32[]{:S(2)}) %collective-permute-start.25) | collective-permute-done | bytes 524320 | tf_op jit(solution)/shard_map/ppermute | solution.py:384
  210.9 8.6 %shard_map.131 = f32[2,960,256]{2,1,0:T(8,128)} custom-call(s32[2]{0:T(128)} %pad_add_fusion.1.strips_ref, f32[3840,512]{1,0:T(8,128)} %refs_0_.15, f32[3840,512]{1,0:T(8,128)} %refs_1_.11, f32[256,512]{1,0:T(8,128)} %copy-done.3, f32[256,512]{1,0:T(8,128)} %copy-done.1, f32[2,960,256]{2,1,0:T(8,128)} %shard_map.127.refs_4_), custom_call_target="tpu_custom_call" | custom-call | flops 1024 | bytes 1024 | tf_op jit(solution)/shard_map/pallas_call | solution.py:346
  226.4 3.2 shard_map.134
  232.4 8.4 %shard_map.130 = f32[2,960,256]{2,1,0:T(8,128)} custom-call(s32[2]{0:T(128)} %pad_add_fusion.strips_ref, f32[3840,512]{1,0:T(8,128)} %refs_0_.15, f32[3840,512]{1,0:T(8,128)} %refs_1_.11, f32[256,512]{1,0:T(8,128)} %copy-done.3, f32[256,512]{1,0:T(8,128)} %copy-done.1, f32[2,960,256]{2,1,0:T(8,128)} %shard_map.128.refs_4_), custom_call_target="tpu_custom_call" | custom-call | flops 1024 | bytes 1024 | tf_op jit(solution)/shard_map/pallas_call | solution.py:346
  243.8 8.7 %collective-permute-done.32.refs_3_ = f32[256,512]{1,0:T(8,128)} collective-permute-done((f32[256,512]{1,0:T(8,128)}, f32[256,512]{1,0:T(8,128)}, u32[]{:S(2)}, u32[]{:S(2)}) %collective-permute-start.32) | collective-permute-done | bytes 524320 | tf_op jit(solution)/shard_map/ppermute | solution.py:387
  252.6 3.5 %shard_map.136 = f32[480,512]{1,0:T(8,128)S(1)} custom-call(s32[2]{0:T(128)S(1)} %pad_add_fusion.2.place_ref, bf16[4,960,256]{2,1,0:T(8,128)(2,1)S(1)} %get-tuple-element.92.high_ref, bf16[4,960,256]{2,1,0:T(8,128)(2,1)S(1)} %get-tuple-element.93.low_ref, f32[256,512]{1,0:T(8,128)S(1)} %copy-done.11, f32[256,512]{1,0:T(8,128)S(1)} %collective-permute-done.22.refs_1_, ...), custom_call_target="tpu_custom_call" | custom-call | flops 1024 | bytes 1024 | tf_op jit(solution)/shard_map/pallas_call | solution.py:312
  263.7 11.2 %collective-permute-done.38.refs_1_ = f32[256,512]{1,0:T(8,128)S(1)} collective-permute-done((f32[256,512]{1,0:T(8,128)S(1)}, f32[256,512]{1,0:T(8,128)S(1)}, u32[]{:S(2)}, u32[]{:S(2)}) %collective-permute-start.38) | collective-permute-done | bytes 524320 | tf_op jit(solution)/shard_map/ppermute | solution.py:387
  274.9 11.2 %collective-permute-done.36.refs_3_ = f32[256,512]{1,0:T(8,128)S(1)} collective-permute-done((f32[256,512]{1,0:T(8,128)S(1)}, f32[256,512]{1,0:T(8,128)S(1)}, u32[]{:S(2)}, u32[]{:S(2)}) %collective-permute-start.36) | collective-permute-done | bytes 524320 | tf_op jit(solution)/shard_map/ppermute | solution.py:387
  291.2 5.8 %collective-permute-done.39.refs_2_ = f32[256,512]{1,0:T(8,128)S(1)} collective-permute-done((f32[256,512]{1,0:T(8,128)S(1)}, f32[256,512]{1,0:T(8,128)S(1)}, u32[]{:S(2)}, u32[]{:S(2)}) %collective-permute-start.39) | collective-permute-done | bytes 524320 | tf_op jit(solution)/shard_map/ppermute | solution.py:387
  300.8 3.5 %shard_map.135 = f32[480,512]{1,0:T(8,128)S(1)} custom-call(s32[2]{0:T(128)S(1)} %pad_add_fusion.2.place_ref, bf16[4,960,256]{2,1,0:T(8,128)(2,1)S(1)} %get-tuple-element.92.high_ref, bf16[4,960,256]{2,1,0:T(8,128)(2,1)S(1)} %get-tuple-element.93.low_ref, f32[256,512]{1,0:T(8,128)S(1)} %copy-done.11, f32[256,512]{1,0:T(8,128)S(1)} %collective-permute-done.22.refs_1_, ...), custom_call_target="tpu_custom_call" | custom-call | flops 1024 | bytes 1024 | tf_op jit(solution)/shard_map/pallas_call | solution.py:312
  321.6 4.4 %collective-permute-done.43 = f32[480,256]{1,0:T(8,128)S(1)} collective-permute-done((f32[480,256]{1,0:T(8,128)S(1)}, f32[480,256]{1,0:T(8,128)S(1)}, u32[]{:S(2)}, u32[]{:S(2)}) %collective-permute-start.43) | collective-permute-done | bytes 491552 | tf_op jit(solution)/shard_map/ppermute | solution.py:390
  327.1 8.4 %collective-permute-done.41 = f32[480,256]{1,0:T(8,128)S(1)} collective-permute-done((f32[480,256]{1,0:T(8,128)S(1)}, f32[480,256]{1,0:T(8,128)S(1)}, u32[]{:S(2)}, u32[]{:S(2)}) %collective-permute-start.41) | collective-permute-done | bytes 491552 | tf_op jit(solution)/shard_map/ppermute | solution.py:390
  (225 shorter events, 116.1 us)
Async XLA Ops:
  10.6 25.5 %collective-permute-start.3 = (f32[256,512]{1,0:T(8,128)}, f32[256,512]{1,0:T(8,128)S(1)}, u32[]{:S(2)}, u32[]{:S(2)}) collective-permute-start(f32[256,512]{1,0:T(8,128)} %get-tuple-element.53.refs_11_), channel_id=1, source_target_pairs={{0,8},{8,16},{16,24},{1,9},{9,17},{17,25},{2,10},{10,18},{18,26},{... | collective-permute-start | bytes 1572872 | tf_op jit(solution)/shard_map/ppermute | solution.py:384
  24.3 17.7 %collective-permute-start.6 = (f32[256,512]{1,0:T(8,128)}, f32[256,512]{1,0:T(8,128)S(1)}, u32[]{:S(2)}, u32[]{:S(2)}) collective-permute-start(f32[256,512]{1,0:T(8,128)} %get-tuple-element.55.refs_11_), channel_id=1, source_target_pairs={{0,8},{8,16},{16,24},{1,9},{9,17},{17,25},{2,10},{10,18},{18,26},{... | collective-permute-start | bytes 1572872 | tf_op jit(solution)/shard_map/ppermute | solution.py:384
  37.0 23.4 %collective-permute-start.5 = (f32[256,512]{1,0:T(8,128)}, f32[256,512]{1,0:T(8,128)}, u32[]{:S(2)}, u32[]{:S(2)}) collective-permute-start(f32[256,512]{1,0:T(8,128)} %broadcast_select_fusion.3), channel_id=1, source_target_pairs={{0,4},{4,0},{1,5},{5,1},{2,6},{6,2},{3,7},{7,3},{8,12},{12,8},{9,1... | collective-permute-start | bytes 1572872 | tf_op jit(solution)/shard_map/ppermute | solution.py:390
  38.5 23.2 %collective-permute-start.4 = (f32[256,512]{1,0:T(8,128)S(1)}, f32[256,512]{1,0:T(8,128)S(1)}, u32[]{:S(2)}, u32[]{:S(2)}) collective-permute-start(f32[256,512]{1,0:T(8,128)S(1)} %collective-permute-done.3.refs_9_), channel_id=1, source_target_pairs={{0,8},{8,16},{16,24},{1,9},{9,17},{17,25},{2,10},{10,18},{18,26},{... | collective-permute-start | bytes 1572872 | tf_op jit(solution)/shard_map/ppermute | solution.py:384
  42.9 24.0 %collective-permute-start.7 = (f32[256,512]{1,0:T(8,128)}, f32[256,512]{1,0:T(8,128)S(1)}, u32[]{:S(2)}, u32[]{:S(2)}) collective-permute-start(f32[256,512]{1,0:T(8,128)} %broadcast_select_fusion.2), channel_id=1, source_target_pairs={{0,4},{4,0},{1,5},{5,1},{2,6},{6,2},{3,7},{7,3},{8,12},{12,8},{9,1... | collective-permute-start | bytes 1572872 | tf_op jit(solution)/shard_map/ppermute | solution.py:390
  58.7 19.6 %collective-permute-start.1 = (f32[240,256]{1,0:T(8,128)}, f32[240,256]{1,0:T(8,128)}, u32[]{:S(2)}, u32[]{:S(2)}) collective-permute-start(f32[240,256]{1,0:T(8,128)} %get-tuple-element.105), channel_id=1, source_target_pairs={{16,0},{24,8},{17,1},{25,9},{18,2},{26,10},{19,3},{27,11},{20,4},{... | collective-permute-start | bytes 737288 | tf_op jit(solution)/shard_map/ppermute | solution.py:384
  60.5 17.9 %collective-permute-start = (f32[240,256]{1,0:T(8,128)}, f32[240,256]{1,0:T(8,128)S(1)}, u32[]{:S(2)}, u32[]{:S(2)}) collective-permute-start(f32[240,256]{1,0:T(8,128)} %get-tuple-element.106), channel_id=1, source_target_pairs={{8,0},{16,8},{24,16},{9,1},{17,9},{25,17},{10,2},{18,10},{26,18},{... | collective-permute-start | bytes 737288 | tf_op jit(solution)/shard_map/ppermute | solution.py:384
  78.5 21.2 %collective-permute-start.10 = (f32[256,512]{1,0:T(8,128)S(1)}, f32[256,512]{1,0:T(8,128)S(1)}, u32[]{:S(2)}, u32[]{:S(2)}) collective-permute-start(f32[256,512]{1,0:T(8,128)S(1)} %broadcast_select_fusion), channel_id=1, source_target_pairs={{0,4},{4,0},{1,5},{5,1},{2,6},{6,2},{3,7},{7,3},{8,12},{12,8},{9,1... | collective-permute-start | bytes 1572872 | tf_op jit(solution)/shard_map/ppermute | solution.py:390
  92.9 17.6 %collective-permute-start.13 = (f32[256,512]{1,0:T(8,128)S(1)}, f32[256,512]{1,0:T(8,128)S(1)}, u32[]{:S(2)}, u32[]{:S(2)}) collective-permute-start(f32[256,512]{1,0:T(8,128)S(1)} %get-tuple-element.72.refs_1_.refs_0_), channel_id=1, source_target_pairs={{0,8},{8,16},{16,24},{24,0},{1,9},{9,17},{17,25},{25,1},{2,10},{10... | collective-permute-start | bytes 1572872 | tf_op jit(solution)/shard_map/ppermute | solution.py:387
  98.1 28.8 %collective-permute-start.11 = (f32[256,512]{1,0:T(8,128)}, f32[256,512]{1,0:T(8,128)S(1)}, u32[]{:S(2)}, u32[]{:S(2)}) collective-permute-start(f32[256,512]{1,0:T(8,128)} %get-tuple-element.68), channel_id=1, source_target_pairs={{0,4},{4,0},{1,5},{5,1},{2,6},{6,2},{3,7},{7,3},{8,12},{12,8},{9,1... | collective-permute-start | bytes 1572872 | tf_op jit(solution)/shard_map/ppermute | solution.py:390
  110.7 19.3 %collective-permute-start.14 = (f32[256,512]{1,0:T(8,128)}, f32[256,512]{1,0:T(8,128)}, u32[]{:S(2)}, u32[]{:S(2)}) collective-permute-start(f32[256,512]{1,0:T(8,128)} %select_add_fusion.1), channel_id=1, source_target_pairs={{8,0},{16,8},{24,16},{9,1},{17,9},{25,17},{10,2},{18,10},{26,18},{... | collective-permute-start | bytes 1572872 | tf_op jit(solution)/shard_map/ppermute | solution.py:384
  112.1 26.0 %collective-permute-start.15 = (f32[256,512]{1,0:T(8,128)S(1)}, f32[256,512]{1,0:T(8,128)S(1)}, u32[]{:S(2)}, u32[]{:S(2)}) collective-permute-start(f32[256,512]{1,0:T(8,128)S(1)} %collective-permute-done.13.refs_1_), channel_id=1, source_target_pairs={{0,8},{8,16},{16,24},{24,0},{1,9},{9,17},{17,25},{25,1},{2,10},{10... | collective-permute-start | bytes 1572872 | tf_op jit(solution)/shard_map/ppermute | solution.py:387
  115.9 59.4 %collective-permute-start.20 = (f32[256,512]{1,0:T(8,128)}, f32[256,512]{1,0:T(8,128)S(1)}, u32[]{:S(2)}, u32[]{:S(2)}) collective-permute-start(f32[256,512]{1,0:T(8,128)} %get-tuple-element.80), channel_id=1, source_target_pairs={{0,4},{4,0},{1,5},{5,1},{2,6},{6,2},{3,7},{7,3},{8,12},{12,8},{9,1... | collective-permute-start | bytes 1572872 | tf_op jit(solution)/shard_map/ppermute | solution.py:390
  116.4 31.6 %collective-permute-start.21 = (f32[256,512]{1,0:T(8,128)}, f32[256,512]{1,0:T(8,128)S(1)}, u32[]{:S(2)}, u32[]{:S(2)}) collective-permute-start(f32[256,512]{1,0:T(8,128)} %get-tuple-element.82), channel_id=1, source_target_pairs={{0,4},{4,0},{1,5},{5,1},{2,6},{6,2},{3,7},{7,3},{8,12},{12,8},{9,1... | collective-permute-start | bytes 1572872 | tf_op jit(solution)/shard_map/ppermute | solution.py:390
  138.1 23.7 %collective-permute-start.16 = (f32[256,512]{1,0:T(8,128)S(1)}, f32[256,512]{1,0:T(8,128)S(1)}, u32[]{:S(2)}, u32[]{:S(2)}) collective-permute-start(f32[256,512]{1,0:T(8,128)S(1)} %add_add_fusion.1), channel_id=1, source_target_pairs={{8,0},{16,8},{24,16},{9,1},{17,9},{25,17},{10,2},{18,10},{26,18},{... | collective-permute-start | bytes 1572872 | tf_op jit(solution)/shard_map/ppermute | solution.py:384
  139.4 22.4 %collective-permute-start.22 = (f32[256,512]{1,0:T(8,128)S(1)}, f32[256,512]{1,0:T(8,128)S(1)}, u32[]{:S(2)}, u32[]{:S(2)}) collective-permute-start(f32[256,512]{1,0:T(8,128)S(1)} %copy-done.10), channel_id=1, source_target_pairs={{0,8},{8,16},{16,24},{24,0},{1,9},{9,17},{17,25},{25,1},{2,10},{10... | collective-permute-start | bytes 1572872 | tf_op jit(solution)/shard_map/ppermute | solution.py:387
  142.2 20.9 %collective-permute-start.17 = (f32[240,256]{1,0:T(8,128)S(1)}, f32[240,256]{1,0:T(8,128)S(1)}, u32[]{:S(2)}, u32[]{:S(2)}) collective-permute-start(f32[240,256]{1,0:T(8,128)S(1)} %get-tuple-element.103), channel_id=1, source_target_pairs={{0,8},{8,16},{16,24},{1,9},{9,17},{17,25},{2,10},{10,18},{18,26},{... | collective-permute-start | bytes 737288 | tf_op jit(solution)/shard_map/ppermute | solution.py:384
  165.1 21.0 %collective-permute-start.29 = (f32[3,240,256]{2,1,0:T(8,128)}, f32[3,240,256]{2,1,0:T(8,128)}, u32[]{:S(2)}, u32[]{:S(2)}) collective-permute-start(f32[3,240,256]{2,1,0:T(8,128)} %pad_maximum_fusion.4), channel_id=1, source_target_pairs={{0,1},{1,0},{2,3},{3,2},{4,5},{5,4},{6,7},{7,6},{8,9},{9,8},{10,11... | collective-permute-start | bytes 2211848 | tf_op jit(solution)/shard_map/ppermute | solution.py:451
  165.1 19.7 %collective-permute-start.24 = (f32[256,512]{1,0:T(8,128)S(1)}, f32[256,512]{1,0:T(8,128)S(1)}, u32[]{:S(2)}, u32[]{:S(2)}) collective-permute-start(f32[256,512]{1,0:T(8,128)S(1)} %collective-permute-done.15.refs_2_), channel_id=1, source_target_pairs={{0,8},{8,16},{16,24},{24,0},{1,9},{9,17},{17,25},{25,1},{2,10},{10... | collective-permute-start | bytes 1572872 | tf_op jit(solution)/shard_map/ppermute | solution.py:387
  184.8 23.9 %collective-permute-start.25 = (f32[256,512]{1,0:T(8,128)}, f32[256,512]{1,0:T(8,128)}, u32[]{:S(2)}, u32[]{:S(2)}) collective-permute-start(f32[256,512]{1,0:T(8,128)} %add_add_fusion), channel_id=1, source_target_pairs={{8,0},{16,8},{24,16},{9,1},{17,9},{25,17},{10,2},{18,10},{26,18},{... | collective-permute-start | bytes 1572872 | tf_op jit(solution)/shard_map/ppermute | solution.py:384
  188.9 32.0 %collective-permute-start.30 = (f32[3,480,256]{2,1,0:T(8,128)}, f32[3,480,256]{2,1,0:T(8,128)}, u32[]{:S(2)}, u32[]{:S(2)}) collective-permute-start(f32[3,480,256]{2,1,0:T(8,128)} %fusion.3), channel_id=1, source_target_pairs={{0,2},{1,3},{2,0},{3,1},{4,6},{5,7},{6,4},{7,5},{8,10},{9,11},{10,... | collective-permute-start | bytes 4423688 | tf_op jit(solution)/shard_map/ppermute | solution.py:455
  219.6 39.3 %collective-permute-start.27 = (f32[2,960,256]{2,1,0:T(8,128)}, f32[2,960,256]{2,1,0:T(8,128)}, u32[]{:S(2)}, u32[]{:S(2)}) collective-permute-start(f32[2,960,256]{2,1,0:T(8,128)} %shard_map.131), channel_id=1, source_target_pairs={{0,1},{1,0},{2,3},{3,2},{4,5},{5,4},{6,7},{7,6},{8,9},{9,8},{10,11... | collective-permute-start | bytes 5898248 | tf_op jit(solution)/shard_map/ppermute | solution.py:451
  229.6 22.9 %collective-permute-start.32 = (f32[256,512]{1,0:T(8,128)}, f32[256,512]{1,0:T(8,128)}, u32[]{:S(2)}, u32[]{:S(2)}) collective-permute-start(f32[256,512]{1,0:T(8,128)} %collective-permute-done.26.refs_2_), channel_id=1, source_target_pairs={{0,8},{8,16},{16,24},{24,0},{1,9},{9,17},{17,25},{25,1},{2,10},{10... | collective-permute-start | bytes 1572872 | tf_op jit(solution)/shard_map/ppermute | solution.py:387
  229.7 34.0 %collective-permute-start.31 = (f32[480,512]{1,0:T(8,128)}, f32[480,512]{1,0:T(8,128)}, u32[]{:S(2)}, u32[]{:S(2)}) collective-permute-start(f32[480,512]{1,0:T(8,128)} %shard_map.134), channel_id=1, source_target_pairs={{0,4},{4,0},{1,5},{5,1},{2,6},{6,2},{3,7},{7,3},{8,12},{12,8},{9,1... | collective-permute-start | bytes 2949128 | tf_op jit(solution)/shard_map/ppermute | solution.py:390
  241.2 22.5 %collective-permute-start.35 = (f32[256,512]{1,0:T(8,128)S(1)}, f32[256,512]{1,0:T(8,128)S(1)}, u32[]{:S(2)}, u32[]{:S(2)}) collective-permute-start(f32[256,512]{1,0:T(8,128)S(1)} %collective-permute-done.34.refs_1_), channel_id=1, source_target_pairs={{0,8},{8,16},{16,24},{24,0},{1,9},{9,17},{17,25},{25,1},{2,10},{10... | collective-permute-start | bytes 1572872 | tf_op jit(solution)/shard_map/ppermute | solution.py:387
  252.5 22.4 %collective-permute-start.38 = (f32[256,512]{1,0:T(8,128)S(1)}, f32[256,512]{1,0:T(8,128)S(1)}, u32[]{:S(2)}, u32[]{:S(2)}) collective-permute-start(f32[256,512]{1,0:T(8,128)S(1)} %copy-done.2), channel_id=1, source_target_pairs={{0,8},{8,16},{16,24},{24,0},{1,9},{9,17},{17,25},{25,1},{2,10},{10... | collective-permute-start | bytes 1572872 | tf_op jit(solution)/shard_map/ppermute | solution.py:387
  256.1 35.1 %collective-permute-start.33 = (f32[480,512]{1,0:T(8,128)S(1)}, f32[480,512]{1,0:T(8,128)S(1)}, u32[]{:S(2)}, u32[]{:S(2)}) collective-permute-start(f32[480,512]{1,0:T(8,128)S(1)} %shard_map.136), channel_id=1, source_target_pairs={{0,4},{4,0},{1,5},{5,1},{2,6},{6,2},{3,7},{7,3},{8,12},{12,8},{9,1... | collective-permute-start | bytes 2949128 | tf_op jit(solution)/shard_map/ppermute | solution.py:390
  260.7 36.2 %collective-permute-start.28 = (f32[960,256]{1,0:T(8,128)S(1)}, f32[960,256]{1,0:T(8,128)S(1)}, u32[]{:S(2)}, u32[]{:S(2)}) collective-permute-start(f32[960,256]{1,0:T(8,128)S(1)} %slice_bitcast_fusion), channel_id=1, source_target_pairs={{0,2},{1,3},{2,0},{3,1},{4,6},{5,7},{6,4},{7,5},{8,10},{9,11},{10,... | collective-permute-start | bytes 2949128 | tf_op jit(solution)/shard_map/ppermute | solution.py:455
  263.6 22.5 %collective-permute-start.36 = (f32[256,512]{1,0:T(8,128)S(1)}, f32[256,512]{1,0:T(8,128)S(1)}, u32[]{:S(2)}, u32[]{:S(2)}) collective-permute-start(f32[256,512]{1,0:T(8,128)S(1)} %collective-permute-done.35.refs_2_), channel_id=1, source_target_pairs={{0,8},{8,16},{16,24},{24,0},{1,9},{9,17},{17,25},{25,1},{2,10},{10... | collective-permute-start | bytes 1572872 | tf_op jit(solution)/shard_map/ppermute | solution.py:387
  274.9 22.1 %collective-permute-start.39 = (f32[256,512]{1,0:T(8,128)S(1)}, f32[256,512]{1,0:T(8,128)S(1)}, u32[]{:S(2)}, u32[]{:S(2)}) collective-permute-start(f32[256,512]{1,0:T(8,128)S(1)} %collective-permute-done.38.refs_1_), channel_id=1, source_target_pairs={{0,8},{8,16},{16,24},{24,0},{1,9},{9,17},{17,25},{25,1},{2,10},{10... | collective-permute-start | bytes 1572872 | tf_op jit(solution)/shard_map/ppermute | solution.py:387
  288.4 32.9 %collective-permute-start.37 = (f32[480,512]{1,0:T(8,128)S(1)}, f32[480,512]{1,0:T(8,128)S(1)}, u32[]{:S(2)}, u32[]{:S(2)}) collective-permute-start(f32[480,512]{1,0:T(8,128)S(1)} %shard_map.138), channel_id=1, source_target_pairs={{0,4},{4,0},{1,5},{5,1},{2,6},{6,2},{3,7},{7,3},{8,12},{12,8},{9,1... | collective-permute-start | bytes 2949128 | tf_op jit(solution)/shard_map/ppermute | solution.py:390
  315.5 20.0 %collective-permute-start.41 = (f32[480,256]{1,0:T(8,128)S(1)}, f32[480,256]{1,0:T(8,128)S(1)}, u32[]{:S(2)}, u32[]{:S(2)}) collective-permute-start(f32[480,256]{1,0:T(8,128)S(1)} %shard_map.140), channel_id=1, source_target_pairs={{0,4},{4,0},{1,5},{5,1},{2,6},{6,2},{3,7},{7,3},{8,12},{12,8},{9,1... | collective-permute-start | bytes 1474568 | tf_op jit(solution)/shard_map/ppermute | solution.py:390
  (64 other events, 748.7 us)

commit v4 on v3

--- a/solution.py
+++ b/solution.py
@@ -558,18 +558,18 @@
         q_hop(0)
         mine_q = query_strips(mine_at)
         q_hop(1)
-        near_return(1, [mine_q, q_rings[0][3]], [q_rings[1][2]])
         k_hop(0)
+        near_return(1, [mine_q, q_rings[0][3]], [q_rings[1][2], k_rings[0][1], *turned])
+        q_hop(1)
         q_terms = [terms(q_rings[0])]
-        q_hop(1, *q_terms[0])
-        k_hop(0)
+        k_hop(0, *q_terms[0])
         theirs = kv_strips(theirs_at, theirs_q)
         q_sent = [exchange(q_terms[0])]
         k_hop(1, theirs)
         q_terms.append(terms(q_rings[1]))
         sums = kv_strips(mine_at, mine_q) + to_core(theirs)
         from_chips = [to_chip(sums[step], step) for step in range(1, chips)]
-        k_hop(0, sums, *q_terms[1])
+        k_hop(0, *q_terms[1])
         k_hop(1, *q_sent[0])
         k_terms = [terms(k_rings[0])]
         q_sent.append(exchange(q_terms[1]))

time: 343 us -> 367 us (1.070)
  waiting for transfers between devices: 96.9 us -> 127 us
  starting transfers between devices: 81.9 us -> 70.6 us
    ppermute x14, waiting for transfers between devices: 29.5 us -> 56.8 us  [z_shift(): return lax.ppermute(block, 'z', route)]
    ppermute x13, starting transfers between devices: 18.2 us -> 9.93 us  [z_ring(): lax.ppermute(block, 'z', [(i, (i + step) % CHAIN) for i in range(CHAIN)])]
    ppermute x14, starting transfers between devices: 35.4 us -> 41 us  [z_shift(): return lax.ppermute(block, 'z', route)]
    ppermute x13, starting transfers between devices: 22.2 us -> 16.6 us  [y_ring(): lax.ppermute(block, 'y', [(i, (i + step) % pair) for i in range(pair)])]
    unnamed x104 -> x132, local copies, waits for them, and re-layouts: 11.9 us -> 12.3 us
  transfers between devices with their start and end apart: 44 -> 44, of which waited for: 16 -> 17; matrix products, arithmetic and copies ran while one was open for 9% -> 9% of each run, Pallas kernels for 31% -> 27%
where the time goes in v4:
time: 367 us; the launch traced here: 361 us
  waiting for transfers between devices  127 us (35%)
  Pallas kernels  115 us (31%)
  starting transfers between devices  70.6 us (19%)
  other arithmetic  26.5 us (7%)
  local copies, waits for them, and re-layouts  19.6 us (5%)
    ppermute x14, waiting for transfers between devices, z_shift(): return lax.ppermute(block, 'z', route)  56.8 us
    ppermute x13, waiting for transfers between devices, z_ring(): lax.ppermute(block, 'z', [(i, (i + step) % CHAIN) for i in range(CHAIN)])  54.1 us
    ppermute x14, starting transfers between devices, z_shift(): return lax.ppermute(block, 'z', route)  41 us
    pallas_call x4, Pallas kernels, project(): pl.pallas_call(functools.partial(project_kernel, normed, lanes), grid=(st...  34 us
    pallas_call x4, Pallas kernels, input_strips(): pl.pallas_call(functools.partial(strip_kernel, pieces, partial is not Non...  32.4 us
    pallas_call x10, Pallas kernels, product(): pl.pallas_call(functools.partial(product_kernel, span[0]), grid_spec=pltp...  25.6 us
    pallas_call x2, Pallas kernels, attention(): pl.pallas_call(functools.partial(attention_kernel, blocks, per_kv), out_s...  18.5 us
    ppermute x13, starting transfers between devices, y_ring(): lax.ppermute(block, 'y', [(i, (i + step) % pair) for i in range(pair)])  16.6 us
  transfers between devices with their start and end apart: 44, of which 17 were waited for; matrix products, arithmetic and copies ran while one was open for 9% of the time, Pallas kernels for 27%

profile of v4, /device:TPU:0, one launch (start us, length us, event | category | flops | bytes accessed | tf_op | source)
XLA Modules:
  0.0 361.1 jit_solution(17338442507619302973)
XLA Ops:
  1.9 8.7 %shard_map.119 = (f32[256,256]{1,0:T(8,128)}, f32[256,512]{1,0:T(8,128)}) custom-call(f32[256,3840]{1,0:T(8,128)} %source_ref.5, f32[3840,512]{1,0:T(8,128)} %refs_0_.15, f32[3840,512]{1,0:T(8,128)} %refs_0_.15, f32[3840,512]{1,0:T(8,128)} %refs_0_.15, f32[3840,512]{1,0:T(8,128)} %refs_1_.11, f32[3840,512]{1,0:T(8,128)} %refs_1_.11, f32[3840,512]{1,0:T(8,128)} %refs_1_.11, ...), custom_call_target="tpu_custom_call" | custom-call | flops 1024 | bytes 1024 | tf_op jit(solution)/shard_map/pallas_call | solution.py:200
  10.6 5.0 %collective-permute-start.3 = (f32[256,512]{1,0:T(8,128)}, f32[256,512]{1,0:T(8,128)S(1)}, u32[]{:S(2)}, u32[]{:S(2)}) collective-permute-start(f32[256,512]{1,0:T(8,128)} %get-tuple-element.53.refs_11_), channel_id=1, source_target_pairs={{0,8},{8,16},{16,24},{1,9},{9,17},{17,25},{2,10},{10,18},{18,26},{... | collective-permute-start | bytes 1572872 | tf_op jit(solution)/shard_map/ppermute | solution.py:384
  15.6 8.7 %shard_map.120 = (f32[256,256]{1,0:T(8,128)}, f32[256,512]{1,0:T(8,128)}) custom-call(f32[256,3840]{1,0:T(8,128)} %source_ref.5, f32[3840,512]{1,0:T(8,128)} %refs_0_.15, f32[3840,512]{1,0:T(8,128)} %refs_0_.15, f32[3840,512]{1,0:T(8,128)} %refs_0_.15, f32[3840,512]{1,0:T(8,128)} %refs_1_.11, f32[3840,512]{1,0:T(8,128)} %refs_1_.11, f32[3840,512]{1,0:T(8,128)} %refs_1_.11, ...), custom_call_target="tpu_custom_call" | custom-call | flops 1024 | bytes 1024 | tf_op jit(solution)/shard_map/pallas_call | solution.py:200
  24.3 3.6 %collective-permute-start.6 = (f32[256,512]{1,0:T(8,128)}, f32[256,512]{1,0:T(8,128)S(1)}, u32[]{:S(2)}, u32[]{:S(2)}) collective-permute-start(f32[256,512]{1,0:T(8,128)} %get-tuple-element.55.refs_11_), channel_id=1, source_target_pairs={{0,8},{8,16},{16,24},{1,9},{9,17},{17,25},{2,10},{10,18},{18,26},{... | collective-permute-start | bytes 1572872 | tf_op jit(solution)/shard_map/ppermute | solution.py:384
  28.0 8.2 %shard_map.121.refs_0_ = f32[256,512]{1,0:T(8,128)} custom-call(f32[256,3840]{1,0:T(8,128)} %source_ref.5, f32[3840,1024]{1,0:T(8,128)} %refs_0_.13, f32[3840,1024]{1,0:T(8,128)} %refs_0_.13, f32[3840,1024]{1,0:T(8,128)} %refs_0_.13), custom_call_target="tpu_custom_call" | custom-call | flops 12079595520 | bytes 1024 | tf_op jit(solution)/shard_map/pallas_call | solution.py:200
  38.6 3.5 collective-permute-start.4
  45.8 8.4 %shard_map.122.refs_0_ = f32[256,512]{1,0:T(8,128)} custom-call(f32[256,3840]{1,0:T(8,128)} %source_ref.5, f32[3840,1024]{1,0:T(8,128)} %refs_0_.13, f32[3840,1024]{1,0:T(8,128)} %refs_0_.13, f32[3840,1024]{1,0:T(8,128)} %refs_0_.13), custom_call_target="tpu_custom_call" | custom-call | flops 12079595520 | bytes 1024 | tf_op jit(solution)/shard_map/pallas_call | solution.py:200
  68.9 3.9 %collective-permute-done.2 = f32[240,256]{1,0:T(8,128)} collective-permute-done((f32[240,256]{1,0:T(8,128)}, f32[240,256]{1,0:T(8,128)}, u32[]{:S(2)}, u32[]{:S(2)}) %collective-permute-start.2) | collective-permute-done | bytes 245792 | tf_op jit(solution)/shard_map/ppermute | solution.py:384
  72.8 7.5 %collective-permute-done.1 = f32[240,256]{1,0:T(8,128)S(1)} collective-permute-done((f32[240,256]{1,0:T(8,128)}, f32[240,256]{1,0:T(8,128)S(1)}, u32[]{:S(2)}, u32[]{:S(2)}) %collective-permute-start.1) | collective-permute-done | bytes 245792 | tf_op jit(solution)/shard_map/ppermute | solution.py:384
  81.6 9.2 %shard_map.124 = (f32[256,512]{1,0:T(8,128)S(1)}, f32[256,512]{1,0:T(8,128)S(1)}, f32[256,512]{1,0:T(8,128)S(1)}, f32[256,512]{1,0:T(8,128)}, f32[256,512]{1,0:T...) custom-call(f32[256,512]{1,0:T(8,128)S(1)} %copy-done.13, f32[256,512]{1,0:T(8,128)S(1)} %get-tuple-element.108.refs_1_, ...), custom_call_target="tpu_custom_call" | custom-call | flops 1024 | bytes 1024 | tf_op jit(solution)/shard_map/pallas_call | solution.py:138
  96.4 7.8 %collective-permute-start.19 = (f32[240,256]{1,0:T(8,128)}, f32[240,256]{1,0:T(8,128)}, u32[]{:S(2)}, u32[]{:S(2)}) collective-permute-start(f32[240,256]{1,0:T(8,128)} %get-tuple-element.101), channel_id=1, source_target_pairs={{0,24},{1,25},{2,26},{3,27},{4,28},{5,29},{6,30},{7,31}} | collective-permute-start | bytes 737288 | tf_op jit(solution)/shard_map/ppermute | solution.py:384
  111.6 9.4 %shard_map.125 = (f32[256,512]{1,0:T(8,128)S(1)}, f32[256,512]{1,0:T(8,128)S(1)}, f32[256,512]{1,0:T(8,128)S(1)}, f32[256,512]{1,0:T(8,128)S(1)}, f32[256,512]{1...) custom-call(f32[256,512]{1,0:T(8,128)S(1)} %copy-done.12, f32[256,512]{1,0:T(8,128)S(1)} %copy-done.21, ...), custom_call_target="tpu_custom_call" | custom-call | flops 1024 | bytes 1024 | tf_op jit(solution)/shard_map/pallas_call | solution.py:138
  121.0 6.9 %collective-permute-start.17 = (f32[240,256]{1,0:T(8,128)S(1)}, f32[240,256]{1,0:T(8,128)S(1)}, u32[]{:S(2)}, u32[]{:S(2)}) collective-permute-start(f32[240,256]{1,0:T(8,128)S(1)} %copy-done.60), channel_id=1, source_target_pairs={{0,8},{8,16},{16,24},{1,9},{9,17},{17,25},{2,10},{10,18},{18,26},{... | collective-permute-start | bytes 737288 | tf_op jit(solution)/shard_map/ppermute | solution.py:384
  136.6 20.2 %collective-permute-done.15.refs_2_ = f32[256,512]{1,0:T(8,128)S(1)} collective-permute-done((f32[256,512]{1,0:T(8,128)}, f32[256,512]{1,0:T(8,128)S(1)}, u32[]{:S(2)}, u32[]{:S(2)}) %collective-permute-start.15) | collective-permute-done | bytes 524320 | tf_op jit(solution)/shard_map/ppermute | solution.py:387
  163.5 7.7 %shard_map.127.refs_4_ = f32[2,960,256]{2,1,0:T(8,128)} custom-call(s32[2]{0:T(128)} %pad_add_fusion.1.strips_ref, f32[3840,1024]{1,0:T(8,128)} %refs_0_.13, f32[256,512]{1,0:T(8,128)} %copy-done.6, f32[256,512]{1,0:T(8,128)} %copy-done.8), custom_call_target="tpu_custom_call" | custom-call | flops 1024 | bytes 1024 | tf_op jit(solution)/shard_map/pallas_call | solution.py:346
  171.3 2.7 fusion.3
  175.5 9.2 %collective-permute-done.16.far_ref = f32[256,512]{1,0:T(8,128)S(1)} collective-permute-done((f32[256,512]{1,0:T(8,128)}, f32[256,512]{1,0:T(8,128)S(1)}, u32[]{:S(2)}, u32[]{:S(2)}) %collective-permute-start.16) | collective-permute-done | bytes 524320 | tf_op jit(solution)/shard_map/ppermute | solution.py:384
  186.0 2.7 collective-permute-start.25
  190.3 30.5 %collective-permute-done.23 = f32[256,512]{1,0:T(8,128)S(1)} collective-permute-done((f32[256,512]{1,0:T(8,128)S(1)}, f32[256,512]{1,0:T(8,128)S(1)}, u32[]{:S(2)}, u32[]{:S(2)}) %collective-permute-start.23) | collective-permute-done | bytes 524320 | tf_op jit(solution)/shard_map/ppermute | solution.py:384
  222.4 7.6 %shard_map.128.refs_4_ = f32[2,960,256]{2,1,0:T(8,128)} custom-call(s32[2]{0:T(128)} %pad_add_fusion.strips_ref, f32[3840,1024]{1,0:T(8,128)} %refs_0_.13, f32[256,512]{1,0:T(8,128)} %copy-done.6, f32[256,512]{1,0:T(8,128)} %copy-done.8), custom_call_target="tpu_custom_call" | custom-call | flops 1024 | bytes 1024 | tf_op jit(solution)/shard_map/pallas_call | solution.py:346
  242.8 5.5 %collective-permute-done.26.far_ref = f32[256,512]{1,0:T(8,128)} collective-permute-done((f32[256,512]{1,0:T(8,128)}, f32[256,512]{1,0:T(8,128)}, u32[]{:S(2)}, u32[]{:S(2)}) %collective-permute-start.26) | collective-permute-done | bytes 524320 | tf_op jit(solution)/shard_map/ppermute | solution.py:384
  250.5 8.7 %shard_map.132 = f32[2,960,256]{2,1,0:T(8,128)} custom-call(s32[2]{0:T(128)} %pad_add_fusion.1.strips_ref, f32[3840,512]{1,0:T(8,128)} %refs_0_.15, f32[3840,512]{1,0:T(8,128)} %refs_1_.11, f32[256,512]{1,0:T(8,128)} %copy-done.3, f32[256,512]{1,0:T(8,128)} %copy-done.1, f32[2,960,256]{2,1,0:T(8,128)} %shard_map.127.refs_4_), custom_call_target="tpu_custom_call" | custom-call | flops 1024 | bytes 1024 | tf_op jit(solution)/shard_map/pallas_call | solution.py:346
  259.8 4.4 %shard_map.134 = f32[480,512]{1,0:T(8,128)} custom-call(s32[2]{0:T(128)S(1)} %pad_add_fusion.2.place_ref, bf16[4,960,256]{2,1,0:T(8,128)(2,1)S(1)} %get-tuple-element.91.high_ref, bf16[4,960,256]{2,1,0:T(8,128)(2,1)S(1)} %get-tuple-element.92.low_ref, f32[256,512]{1,0:T(8,128)S(1)} %copy-done.7, f32[256,512]{1,0:T(8,128)} %collective-permute-done.13.refs_1_, ...), custom_call_target="tpu_custom_call" | custom-call | flops 1024 | bytes 1024 | tf_op jit(solution)/shard_map/pallas_call | solution.py:312
  266.3 8.4 %shard_map.131 = f32[2,960,256]{2,1,0:T(8,128)} custom-call(s32[2]{0:T(128)} %pad_add_fusion.strips_ref, f32[3840,512]{1,0:T(8,128)} %refs_0_.15, f32[3840,512]{1,0:T(8,128)} %refs_1_.11, f32[256,512]{1,0:T(8,128)} %copy-done.3, f32[256,512]{1,0:T(8,128)} %copy-done.1, f32[2,960,256]{2,1,0:T(8,128)} %shard_map.128.refs_4_), custom_call_target="tpu_custom_call" | custom-call | flops 1024 | bytes 1024 | tf_op jit(solution)/shard_map/pallas_call | solution.py:346
  276.1 3.5 shard_map.136
  289.1 9.3 %collective-permute-done.38.refs_1_ = f32[256,512]{1,0:T(8,128)S(1)} collective-permute-done((f32[256,512]{1,0:T(8,128)S(1)}, f32[256,512]{1,0:T(8,128)S(1)}, u32[]{:S(2)}, u32[]{:S(2)}) %collective-permute-start.38) | collective-permute-done | bytes 524320 | tf_op jit(solution)/shard_map/ppermute | solution.py:387
  298.4 11.2 %collective-permute-done.36.refs_3_ = f32[256,512]{1,0:T(8,128)S(1)} collective-permute-done((f32[256,512]{1,0:T(8,128)S(1)}, f32[256,512]{1,0:T(8,128)S(1)}, u32[]{:S(2)}, u32[]{:S(2)}) %collective-permute-start.36) | collective-permute-done | bytes 524320 | tf_op jit(solution)/shard_map/ppermute | solution.py:387
  313.5 7.0 %collective-permute-done.39.refs_2_ = f32[256,512]{1,0:T(8,128)S(1)} collective-permute-done((f32[256,512]{1,0:T(8,128)S(1)}, f32[256,512]{1,0:T(8,128)S(1)}, u32[]{:S(2)}, u32[]{:S(2)}) %collective-permute-start.39) | collective-permute-done | bytes 524320 | tf_op jit(solution)/shard_map/ppermute | solution.py:387
  322.0 3.4 shard_map.133
  325.4 3.5 shard_map.135
  344.9 6.1 %collective-permute-done.43 = f32[480,256]{1,0:T(8,128)S(1)} collective-permute-done((f32[480,256]{1,0:T(8,128)S(1)}, f32[480,256]{1,0:T(8,128)S(1)}, u32[]{:S(2)}, u32[]{:S(2)}) %collective-permute-start.43) | collective-permute-done | bytes 491552 | tf_op jit(solution)/shard_map/ppermute | solution.py:390
  352.2 7.3 %collective-permute-done.41 = f32[480,256]{1,0:T(8,128)S(1)} collective-permute-done((f32[480,256]{1,0:T(8,128)S(1)}, f32[480,256]{1,0:T(8,128)S(1)}, u32[]{:S(2)}, u32[]{:S(2)}) %collective-permute-start.41) | collective-permute-done | bytes 491552 | tf_op jit(solution)/shard_map/ppermute | solution.py:390
  (253 shorter events, 109.2 us)
Async XLA Ops:
  10.6 25.6 %collective-permute-start.3 = (f32[256,512]{1,0:T(8,128)}, f32[256,512]{1,0:T(8,128)S(1)}, u32[]{:S(2)}, u32[]{:S(2)}) collective-permute-start(f32[256,512]{1,0:T(8,128)} %get-tuple-element.53.refs_11_), channel_id=1, source_target_pairs={{0,8},{8,16},{16,24},{1,9},{9,17},{17,25},{2,10},{10,18},{18,26},{... | collective-permute-start | bytes 1572872 | tf_op jit(solution)/shard_map/ppermute | solution.py:384
  37.1 24.6 %collective-permute-start.5 = (f32[256,512]{1,0:T(8,128)}, f32[256,512]{1,0:T(8,128)}, u32[]{:S(2)}, u32[]{:S(2)}) collective-permute-start(f32[256,512]{1,0:T(8,128)} %broadcast_select_fusion.3), channel_id=1, source_target_pairs={{0,4},{4,0},{1,5},{5,1},{2,6},{6,2},{3,7},{7,3},{8,12},{12,8},{9,1... | collective-permute-start | bytes 1572872 | tf_op jit(solution)/shard_map/ppermute | solution.py:390
  38.6 24.5 %collective-permute-start.4 = (f32[256,512]{1,0:T(8,128)S(1)}, f32[256,512]{1,0:T(8,128)S(1)}, u32[]{:S(2)}, u32[]{:S(2)}) collective-permute-start(f32[256,512]{1,0:T(8,128)S(1)} %collective-permute-done.3.refs_9_), channel_id=1, source_target_pairs={{0,8},{8,16},{16,24},{1,9},{9,17},{17,25},{2,10},{10,18},{18,26},{... | collective-permute-start | bytes 1572872 | tf_op jit(solution)/shard_map/ppermute | solution.py:384
  43.0 22.0 %collective-permute-start.7 = (f32[256,512]{1,0:T(8,128)}, f32[256,512]{1,0:T(8,128)}, u32[]{:S(2)}, u32[]{:S(2)}) collective-permute-start(f32[256,512]{1,0:T(8,128)} %broadcast_select_fusion.2), channel_id=1, source_target_pairs={{0,4},{4,0},{1,5},{5,1},{2,6},{6,2},{3,7},{7,3},{8,12},{12,8},{9,1... | collective-permute-start | bytes 1572872 | tf_op jit(solution)/shard_map/ppermute | solution.py:390
  43.5 21.5 %collective-permute-start.9 = (f32[256,512]{1,0:T(8,128)S(1)}, f32[256,512]{1,0:T(8,128)S(1)}, u32[]{:S(2)}, u32[]{:S(2)}) collective-permute-start(f32[256,512]{1,0:T(8,128)S(1)} %collective-permute-done.6.refs_9_), channel_id=1, source_target_pairs={{0,8},{8,16},{16,24},{1,9},{9,17},{17,25},{2,10},{10,18},{18,26},{... | collective-permute-start | bytes 1572872 | tf_op jit(solution)/shard_map/ppermute | solution.py:384
  61.7 18.7 %collective-permute-start.1 = (f32[240,256]{1,0:T(8,128)}, f32[240,256]{1,0:T(8,128)S(1)}, u32[]{:S(2)}, u32[]{:S(2)}) collective-permute-start(f32[240,256]{1,0:T(8,128)} %get-tuple-element.105), channel_id=1, source_target_pairs={{16,0},{24,8},{17,1},{25,9},{18,2},{26,10},{19,3},{27,11},{20,4},{... | collective-permute-start | bytes 737288 | tf_op jit(solution)/shard_map/ppermute | solution.py:384
  67.1 40.3 %collective-permute-start.10 = (f32[256,512]{1,0:T(8,128)}, f32[256,512]{1,0:T(8,128)}, u32[]{:S(2)}, u32[]{:S(2)}) collective-permute-start(f32[256,512]{1,0:T(8,128)} %broadcast_select_fusion), channel_id=1, source_target_pairs={{0,4},{4,0},{1,5},{5,1},{2,6},{6,2},{3,7},{7,3},{8,12},{12,8},{9,1... | collective-permute-start | bytes 1572872 | tf_op jit(solution)/shard_map/ppermute | solution.py:390
  96.4 24.5 %collective-permute-start.19 = (f32[240,256]{1,0:T(8,128)}, f32[240,256]{1,0:T(8,128)}, u32[]{:S(2)}, u32[]{:S(2)}) collective-permute-start(f32[240,256]{1,0:T(8,128)} %get-tuple-element.101), channel_id=1, source_target_pairs={{0,24},{1,25},{2,26},{3,27},{4,28},{5,29},{6,30},{7,31}} | collective-permute-start | bytes 737288 | tf_op jit(solution)/shard_map/ppermute | solution.py:384
  104.2 23.9 %collective-permute-start.13 = (f32[256,512]{1,0:T(8,128)S(1)}, f32[256,512]{1,0:T(8,128)}, u32[]{:S(2)}, u32[]{:S(2)}) collective-permute-start(f32[256,512]{1,0:T(8,128)S(1)} %get-tuple-element.72.refs_1_.refs_0_), channel_id=1, source_target_pairs={{0,8},{8,16},{16,24},{24,0},{1,9},{9,17},{17,25},{25,1},{2,10},{10... | collective-permute-start | bytes 1572872 | tf_op jit(solution)/shard_map/ppermute | solution.py:387
  104.2 23.9 %collective-permute-start.12 = (f32[256,512]{1,0:T(8,128)}, f32[256,512]{1,0:T(8,128)}, u32[]{:S(2)}, u32[]{:S(2)}) collective-permute-start(f32[256,512]{1,0:T(8,128)} %get-tuple-element.70), channel_id=1, source_target_pairs={{0,4},{4,0},{1,5},{5,1},{2,6},{6,2},{3,7},{7,3},{8,12},{12,8},{9,1... | collective-permute-start | bytes 1572872 | tf_op jit(solution)/shard_map/ppermute | solution.py:390
  105.3 22.7 %collective-permute-start.18 = (f32[240,256]{1,0:T(8,128)}, f32[240,256]{1,0:T(8,128)}, u32[]{:S(2)}, u32[]{:S(2)}) collective-permute-start(f32[240,256]{1,0:T(8,128)} %get-tuple-element.102), channel_id=1, source_target_pairs={{0,16},{8,24},{1,17},{9,25},{2,18},{10,26},{3,19},{11,27},{4,20},{... | collective-permute-start | bytes 737288 | tf_op jit(solution)/shard_map/ppermute | solution.py:384
  107.4 49.5 %collective-permute-start.11 = (f32[256,512]{1,0:T(8,128)}, f32[256,512]{1,0:T(8,128)S(1)}, u32[]{:S(2)}, u32[]{:S(2)}) collective-permute-start(f32[256,512]{1,0:T(8,128)} %copy-done.48), channel_id=1, source_target_pairs={{0,4},{4,0},{1,5},{5,1},{2,6},{6,2},{3,7},{7,3},{8,12},{12,8},{9,1... | collective-permute-start | bytes 1572872 | tf_op jit(solution)/shard_map/ppermute | solution.py:390
  128.2 28.6 %collective-permute-start.14 = (f32[256,512]{1,0:T(8,128)S(1)}, f32[256,512]{1,0:T(8,128)S(1)}, u32[]{:S(2)}, u32[]{:S(2)}) collective-permute-start(f32[256,512]{1,0:T(8,128)S(1)} %select_add_fusion.1), channel_id=1, source_target_pairs={{8,0},{16,8},{24,16},{9,1},{17,9},{25,17},{10,2},{18,10},{26,18},{... | collective-permute-start | bytes 1572872 | tf_op jit(solution)/shard_map/ppermute | solution.py:384
  129.7 27.2 %collective-permute-start.15 = (f32[256,512]{1,0:T(8,128)}, f32[256,512]{1,0:T(8,128)S(1)}, u32[]{:S(2)}, u32[]{:S(2)}) collective-permute-start(f32[256,512]{1,0:T(8,128)} %collective-permute-done.13.refs_1_), channel_id=1, source_target_pairs={{0,8},{8,16},{16,24},{24,0},{1,9},{9,17},{17,25},{25,1},{2,10},{10... | collective-permute-start | bytes 1572872 | tf_op jit(solution)/shard_map/ppermute | solution.py:387
  134.4 36.9 %collective-permute-start.28 = (f32[3,240,256]{2,1,0:T(8,128)}, f32[3,240,256]{2,1,0:T(8,128)}, u32[]{:S(2)}, u32[]{:S(2)}) collective-permute-start(f32[3,240,256]{2,1,0:T(8,128)} %pad_maximum_fusion.4), channel_id=1, source_target_pairs={{0,1},{1,0},{2,3},{3,2},{4,5},{5,4},{6,7},{7,6},{8,9},{9,8},{10,11... | collective-permute-start | bytes 2211848 | tf_op jit(solution)/shard_map/ppermute | solution.py:451
  134.5 40.9 %collective-permute-start.21 = (f32[256,512]{1,0:T(8,128)}, f32[256,512]{1,0:T(8,128)}, u32[]{:S(2)}, u32[]{:S(2)}) collective-permute-start(f32[256,512]{1,0:T(8,128)} %copy-done.49), channel_id=1, source_target_pairs={{0,4},{4,0},{1,5},{5,1},{2,6},{6,2},{3,7},{7,3},{8,12},{12,8},{9,1... | collective-permute-start | bytes 1572872 | tf_op jit(solution)/shard_map/ppermute | solution.py:390
  158.9 25.8 %collective-permute-start.16 = (f32[256,512]{1,0:T(8,128)}, f32[256,512]{1,0:T(8,128)S(1)}, u32[]{:S(2)}, u32[]{:S(2)}) collective-permute-start(f32[256,512]{1,0:T(8,128)} %add_add_fusion.1), channel_id=1, source_target_pairs={{8,0},{16,8},{24,16},{9,1},{17,9},{25,17},{10,2},{18,10},{26,18},{... | collective-permute-start | bytes 1572872 | tf_op jit(solution)/shard_map/ppermute | solution.py:384
  160.2 24.5 %collective-permute-start.22 = (f32[256,512]{1,0:T(8,128)S(1)}, f32[256,512]{1,0:T(8,128)S(1)}, u32[]{:S(2)}, u32[]{:S(2)}) collective-permute-start(f32[256,512]{1,0:T(8,128)S(1)} %get-tuple-element.85.refs_2_.refs_0_), channel_id=1, source_target_pairs={{0,8},{8,16},{16,24},{24,0},{1,9},{9,17},{17,25},{25,1},{2,10},{10... | collective-permute-start | bytes 1572872 | tf_op jit(solution)/shard_map/ppermute | solution.py:387
  174.0 62.6 %collective-permute-start.29 = (f32[3,480,256]{2,1,0:T(8,128)}, f32[3,480,256]{2,1,0:T(8,128)}, u32[]{:S(2)}, u32[]{:S(2)}) collective-permute-start(f32[3,480,256]{2,1,0:T(8,128)} %fusion.3), channel_id=1, source_target_pairs={{0,2},{1,3},{2,0},{3,1},{4,6},{5,7},{6,4},{7,5},{8,10},{9,11},{10,... | collective-permute-start | bytes 4423688 | tf_op jit(solution)/shard_map/ppermute | solution.py:455
  184.8 36.0 %collective-permute-start.23 = (f32[256,512]{1,0:T(8,128)S(1)}, f32[256,512]{1,0:T(8,128)S(1)}, u32[]{:S(2)}, u32[]{:S(2)}) collective-permute-start(f32[256,512]{1,0:T(8,128)S(1)} %select_add_fusion), channel_id=1, source_target_pairs={{8,0},{16,8},{24,16},{9,1},{17,9},{25,17},{10,2},{18,10},{26,18},{... | collective-permute-start | bytes 1572872 | tf_op jit(solution)/shard_map/ppermute | solution.py:384
  186.0 45.5 %collective-permute-start.25 = (f32[256,512]{1,0:T(8,128)S(1)}, f32[256,512]{1,0:T(8,128)S(1)}, u32[]{:S(2)}, u32[]{:S(2)}) collective-permute-start(f32[256,512]{1,0:T(8,128)S(1)} %collective-permute-done.15.refs_2_), channel_id=1, source_target_pairs={{0,8},{8,16},{16,24},{24,0},{1,9},{9,17},{17,25},{25,1},{2,10},{10... | collective-permute-start | bytes 1572872 | tf_op jit(solution)/shard_map/ppermute | solution.py:387
  188.7 42.9 %collective-permute-start.20 = (f32[256,512]{1,0:T(8,128)}, f32[256,512]{1,0:T(8,128)S(1)}, u32[]{:S(2)}, u32[]{:S(2)}) collective-permute-start(f32[256,512]{1,0:T(8,128)} %get-tuple-element.80), channel_id=1, source_target_pairs={{0,4},{4,0},{1,5},{5,1},{2,6},{6,2},{3,7},{7,3},{8,12},{12,8},{9,1... | collective-permute-start | bytes 1572872 | tf_op jit(solution)/shard_map/ppermute | solution.py:390
  259.2 21.9 %collective-permute-start.30 = (f32[2,960,256]{2,1,0:T(8,128)}, f32[2,960,256]{2,1,0:T(8,128)}, u32[]{:S(2)}, u32[]{:S(2)}) collective-permute-start(f32[2,960,256]{2,1,0:T(8,128)} %shard_map.132), channel_id=1, source_target_pairs={{0,1},{1,0},{2,3},{3,2},{4,5},{5,4},{6,7},{7,6},{8,9},{9,8},{10,11... | collective-permute-start | bytes 5898248 | tf_op jit(solution)/shard_map/ppermute | solution.py:451
  264.2 24.9 %collective-permute-start.32 = (f32[480,512]{1,0:T(8,128)}, f32[480,512]{1,0:T(8,128)}, u32[]{:S(2)}, u32[]{:S(2)}) collective-permute-start(f32[480,512]{1,0:T(8,128)} %shard_map.134), channel_id=1, source_target_pairs={{0,4},{4,0},{1,5},{5,1},{2,6},{6,2},{3,7},{7,3},{8,12},{12,8},{9,1... | collective-permute-start | bytes 2949128 | tf_op jit(solution)/shard_map/ppermute | solution.py:390
  265.7 21.5 %collective-permute-start.35 = (f32[256,512]{1,0:T(8,128)S(1)}, f32[256,512]{1,0:T(8,128)S(1)}, u32[]{:S(2)}, u32[]{:S(2)}) collective-permute-start(f32[256,512]{1,0:T(8,128)S(1)} %collective-permute-done.27.refs_1_), channel_id=1, source_target_pairs={{0,8},{8,16},{16,24},{24,0},{1,9},{9,17},{17,25},{25,1},{2,10},{10... | collective-permute-start | bytes 1572872 | tf_op jit(solution)/shard_map/ppermute | solution.py:387
  276.0 22.4 %collective-permute-start.38 = (f32[256,512]{1,0:T(8,128)S(1)}, f32[256,512]{1,0:T(8,128)S(1)}, u32[]{:S(2)}, u32[]{:S(2)}) collective-permute-start(f32[256,512]{1,0:T(8,128)S(1)} %copy-done.2), channel_id=1, source_target_pairs={{0,8},{8,16},{16,24},{24,0},{1,9},{9,17},{17,25},{25,1},{2,10},{10... | collective-permute-start | bytes 1572872 | tf_op jit(solution)/shard_map/ppermute | solution.py:387
  279.5 34.0 %collective-permute-start.34 = (f32[480,512]{1,0:T(8,128)S(1)}, f32[480,512]{1,0:T(8,128)S(1)}, u32[]{:S(2)}, u32[]{:S(2)}) collective-permute-start(f32[480,512]{1,0:T(8,128)S(1)} %shard_map.136), channel_id=1, source_target_pairs={{0,4},{4,0},{1,5},{5,1},{2,6},{6,2},{3,7},{7,3},{8,12},{12,8},{9,1... | collective-permute-start | bytes 2949128 | tf_op jit(solution)/shard_map/ppermute | solution.py:390
  283.0 37.5 %collective-permute-start.31 = (f32[960,256]{1,0:T(8,128)S(1)}, f32[960,256]{1,0:T(8,128)S(1)}, u32[]{:S(2)}, u32[]{:S(2)}) collective-permute-start(f32[960,256]{1,0:T(8,128)S(1)} %slice_bitcast_fusion), channel_id=1, source_target_pairs={{0,2},{1,3},{2,0},{3,1},{4,6},{5,7},{6,4},{7,5},{8,10},{9,11},{10,... | collective-permute-start | bytes 2949128 | tf_op jit(solution)/shard_map/ppermute | solution.py:455
  287.2 22.5 %collective-permute-start.36 = (f32[256,512]{1,0:T(8,128)S(1)}, f32[256,512]{1,0:T(8,128)S(1)}, u32[]{:S(2)}, u32[]{:S(2)}) collective-permute-start(f32[256,512]{1,0:T(8,128)S(1)} %collective-permute-done.35.refs_2_), channel_id=1, source_target_pairs={{0,8},{8,16},{16,24},{24,0},{1,9},{9,17},{17,25},{25,1},{2,10},{10... | collective-permute-start | bytes 1572872 | tf_op jit(solution)/shard_map/ppermute | solution.py:387
  298.4 22.1 %collective-permute-start.39 = (f32[256,512]{1,0:T(8,128)S(1)}, f32[256,512]{1,0:T(8,128)S(1)}, u32[]{:S(2)}, u32[]{:S(2)}) collective-permute-start(f32[256,512]{1,0:T(8,128)S(1)} %collective-permute-done.38.refs_1_), channel_id=1, source_target_pairs={{0,8},{8,16},{16,24},{24,0},{1,9},{9,17},{17,25},{25,1},{2,10},{10... | collective-permute-start | bytes 1572872 | tf_op jit(solution)/shard_map/ppermute | solution.py:387
  311.9 23.1 %collective-permute-start.37 = (f32[480,512]{1,0:T(8,128)S(1)}, f32[480,512]{1,0:T(8,128)S(1)}, u32[]{:S(2)}, u32[]{:S(2)}) collective-permute-start(f32[480,512]{1,0:T(8,128)S(1)} %shard_map.138), channel_id=1, source_target_pairs={{0,4},{4,0},{1,5},{5,1},{2,6},{6,2},{3,7},{7,3},{8,12},{12,8},{9,1... | collective-permute-start | bytes 2949128 | tf_op jit(solution)/shard_map/ppermute | solution.py:390
  340.0 19.5 %collective-permute-start.41 = (f32[480,256]{1,0:T(8,128)S(1)}, f32[480,256]{1,0:T(8,128)S(1)}, u32[]{:S(2)}, u32[]{:S(2)}) collective-permute-start(f32[480,256]{1,0:T(8,128)S(1)} %shard_map.140), channel_id=1, source_target_pairs={{0,4},{4,0},{1,5},{5,1},{2,6},{6,2},{3,7},{7,3},{8,12},{12,8},{9,1... | collective-permute-start | bytes 1474568 | tf_op jit(solution)/shard_map/ppermute | solution.py:390
  (78 other events, 944.5 us)

commit v5 on v2

--- a/solution.py
+++ b/solution.py
@@ -433,17 +433,16 @@
         for group in groups:
             fours.append(z_shift(after(two[group], own[-1]), 1))
         for group in groups:
-            three_back = farthest(group, fours[group], *ones, *fours[:group], hidden_rows)
+            three_back = farthest(group, fours[group], *ones, *fours, hidden_rows)
             windows.append([fours[group], three_back, two[group], ones[group], own[group]])
     else:
         for group in groups:
             windows.append([shifted(own[group], d) for d in range(reach, 0, -1)] + [own[group]])
-    shared = after(hidden_rows, *fours) if fours else hidden_rows
     pieces = []
     for step in range(CHAIN - 1, 0, -1):
         target = (along + step) % CHAIN
         start = target * slab + member * piece
-        pieces.append(z_ring(lax.dynamic_slice_in_dim(shared, start, piece, 0), step))
+        pieces.append(z_ring(lax.dynamic_slice_in_dim(hidden_rows, start, piece, 0), step))
     chips = members // CORES
     chip, core = member // CORES, member % CORES
 
@@ -533,10 +532,9 @@
         got = follow(block, lambda b: z_shift(b, -1), extra)
         held.append((two_back + jnp.where(across == 0, from_three, from_one) + got, from_one))
 
-    def near_return(group, extra, before):
+    def near_return(group, *extra):
         block, from_one = held[group]
         far = follow(block, lambda b: z_shift(b, -1), extra)
-        far = after(far, *before) if before else far
         mine = parts[group][-1]
         d_kv.append(settle(mine, from_one, far, keep, key_raw[group], *tables))
         k_rings.append([d_kv[group]])
@@ -545,30 +543,29 @@
         q_hop(0)
         far_return(0, q_rings[0][1], *attended)
         q_hop(0)
-        near_return(0, [q_rings[0][2]], [])
+        near_return(0, q_rings[0][2])
         q_hop(1)
         theirs_q = query_strips(theirs_at)
         far_return(1, theirs_q, q_rings[1][1])
         q_hop(0)
         mine_q = query_strips(mine_at)
         q_hop(1)
+        near_return(1, mine_q, q_rings[0][3])
         k_hop(0)
-        near_return(1, [mine_q, q_rings[0][3], q_rings[1][2]], [k_rings[0][1]])
         q_terms = [terms(q_rings[0])]
         q_hop(1, *q_terms[0])
         k_hop(0)
         theirs = kv_strips(theirs_at, theirs_q)
         q_sent = [exchange(q_terms[0])]
-        k_hop(1)
+        k_hop(1, theirs)
         q_terms.append(terms(q_rings[1]))
         k_hop(0, *q_terms[1])
         sums = kv_strips(mine_at, mine_q)
-        k_hop(1, theirs, *q_sent[0])
+        k_hop(1, sums, *q_sent[0])
         k_terms = [terms(k_rings[0])]
         q_sent.append(exchange(q_terms[1]))
-        last = after(k_rings[1][-1], sent[-2], sums, *k_terms[0], *q_sent[1])
-        tails = [z_ring(last[:, head:], 1)]
-        tails.append(z_ring(after(last[:, :head], tails[0]), 1))
+        last = after(k_rings[1][-1], sent[-2], *k_terms[0], *q_sent[1])
+        tails = [z_ring(last[:, head:], 1), z_ring(last[:, :head], 1)]
         tail_rings = [k_rings[1] + [tail] for tail in tails]
         tail_spans = [(head, head), (0, head)]
     else:

time: 350 us -> 342 us (0.977)
  waiting for transfers between devices: 127 us -> 117 us
  local copies, waits for them, and re-layouts: 10.2 us -> 16.4 us
    ppermute x8, waiting for transfers between devices: 52.2 us -> 27.9 us  [z_shift(): return lax.ppermute(block, 'z', route)]
    ppermute x16, waiting for transfers between devices: 65.2 us -> 81.2 us  [z_ring(): lax.ppermute(block, 'z', [(i, (i + step) % CHAIN) for i in range(CHAIN)])]
    unnamed x112 -> x122, local copies, waits for them, and re-layouts: 6.15 us -> 11.5 us
  transfers between devices with their start and end apart: 41 -> 41, of which waited for: 18 -> 18; matrix products, arithmetic and copies ran while one was open for 8% -> 9% of each run, Pallas kernels for 32% -> 32%
where the time goes in v5:
time: 342 us; the launch traced here: 337 us
  waiting for transfers between devices  117 us (34%)
  Pallas kernels  115 us (34%)
  starting transfers between devices  59.6 us (17%)
  other arithmetic  26.4 us (8%)
  local copies, waits for them, and re-layouts  16.4 us (5%)
    ppermute x16, waiting for transfers between devices, z_ring(): lax.ppermute(block, 'z', [(i, (i + step) % CHAIN) for i in range(CHAIN)])  81.2 us
    pallas_call x4, Pallas kernels, project(): pl.pallas_call(functools.partial(project_kernel, normed, lanes), grid=(st...  34 us
    pallas_call x4, Pallas kernels, input_strips(): pl.pallas_call(functools.partial(strip_kernel, pieces, partial is not Non...  32.3 us
    ppermute x8, waiting for transfers between devices, z_shift(): return lax.ppermute(block, 'z', route)  27.9 us
    pallas_call x10, Pallas kernels, product(): pl.pallas_call(functools.partial(product_kernel, span[0]), grid_spec=pltp...  26.6 us
    ppermute x16, starting transfers between devices, z_ring(): lax.ppermute(block, 'z', [(i, (i + step) % CHAIN) for i in range(CHAIN)])  23.7 us
    ppermute x8, starting transfers between devices, z_shift(): return lax.ppermute(block, 'z', route)  19.6 us
    pallas_call x2, Pallas kernels, attention(): pl.pallas_call(functools.partial(attention_kernel, blocks, per_kv), out_s...  17.8 us
  transfers between devices with their start and end apart: 41, of which 18 were waited for; matrix products, arithmetic and copies ran while one was open for 9% of the time, Pallas kernels for 32%

profile of v5, /device:TPU:0, one launch (start us, length us, event | category | flops | bytes accessed | tf_op | source)
XLA Modules:
  0.0 336.8 jit_solution(7215924117127622263)
XLA Ops:
  1.9 8.7 %shard_map.119 = (f32[256,256]{1,0:T(8,128)}, f32[256,512]{1,0:T(8,128)}) custom-call(f32[256,3840]{1,0:T(8,128)} %source_ref.5, f32[3840,512]{1,0:T(8,128)} %refs_0_.15, f32[3840,512]{1,0:T(8,128)} %refs_0_.15, f32[3840,512]{1,0:T(8,128)} %refs_0_.15, f32[3840,512]{1,0:T(8,128)} %refs_1_.11, f32[3840,512]{1,0:T(8,128)} %refs_1_.11, f32[3840,512]{1,0:T(8,128)} %refs_1_.11, ...), custom_call_target="tpu_custom_call" | custom-call | flops 1024 | bytes 1024 | tf_op jit(solution)/shard_map/pallas_call | solution.py:200
  10.6 4.9 %collective-permute-start.3 = (f32[256,512]{1,0:T(8,128)}, f32[256,512]{1,0:T(8,128)S(1)}, u32[]{:S(2)}, u32[]{:S(2)}) collective-permute-start(f32[256,512]{1,0:T(8,128)} %get-tuple-element.50.refs_11_), channel_id=1, source_target_pairs={{0,8},{8,16},{16,24},{1,9},{9,17},{17,25},{2,10},{10,18},{18,26},{... | collective-permute-start | bytes 1572872 | tf_op jit(solution)/shard_map/ppermute | solution.py:384
  15.6 8.7 %shard_map.120 = (f32[256,256]{1,0:T(8,128)}, f32[256,512]{1,0:T(8,128)}) custom-call(f32[256,3840]{1,0:T(8,128)} %source_ref.5, f32[3840,512]{1,0:T(8,128)} %refs_0_.15, f32[3840,512]{1,0:T(8,128)} %refs_0_.15, f32[3840,512]{1,0:T(8,128)} %refs_0_.15, f32[3840,512]{1,0:T(8,128)} %refs_1_.11, f32[3840,512]{1,0:T(8,128)} %refs_1_.11, f32[3840,512]{1,0:T(8,128)} %refs_1_.11, ...), custom_call_target="tpu_custom_call" | custom-call | flops 1024 | bytes 1024 | tf_op jit(solution)/shard_map/pallas_call | solution.py:200
  24.3 3.6 %collective-permute-start.6 = (f32[256,512]{1,0:T(8,128)}, f32[256,512]{1,0:T(8,128)S(1)}, u32[]{:S(2)}, u32[]{:S(2)}) collective-permute-start(f32[256,512]{1,0:T(8,128)} %get-tuple-element.52.refs_11_), channel_id=1, source_target_pairs={{0,8},{8,16},{16,24},{1,9},{9,17},{17,25},{2,10},{10,18},{18,26},{... | collective-permute-start | bytes 1572872 | tf_op jit(solution)/shard_map/ppermute | solution.py:384
  27.9 8.2 %shard_map.121.refs_0_ = f32[256,512]{1,0:T(8,128)} custom-call(f32[256,3840]{1,0:T(8,128)} %source_ref.5, f32[3840,1024]{1,0:T(8,128)} %refs_0_.13, f32[3840,1024]{1,0:T(8,128)} %refs_0_.13, f32[3840,1024]{1,0:T(8,128)} %refs_0_.13), custom_call_target="tpu_custom_call" | custom-call | flops 12079595520 | bytes 1024 | tf_op jit(solution)/shard_map/pallas_call | solution.py:200
  38.6 4.3 %collective-permute-start.4 = (f32[256,512]{1,0:T(8,128)S(1)}, f32[256,512]{1,0:T(8,128)}, u32[]{:S(2)}, u32[]{:S(2)}) collective-permute-start(f32[256,512]{1,0:T(8,128)S(1)} %collective-permute-done.3.refs_9_), channel_id=1, source_target_pairs={{0,8},{8,16},{16,24},{1,9},{9,17},{17,25},{2,10},{10,18},{18,26},{... | collective-permute-start | bytes 1572872 | tf_op jit(solution)/shard_map/ppermute | solution.py:384
  45.8 8.4 %shard_map.122.refs_0_ = f32[256,512]{1,0:T(8,128)} custom-call(f32[256,3840]{1,0:T(8,128)} %source_ref.5, f32[3840,1024]{1,0:T(8,128)} %refs_0_.13, f32[3840,1024]{1,0:T(8,128)} %refs_0_.13, f32[3840,1024]{1,0:T(8,128)} %refs_0_.13), custom_call_target="tpu_custom_call" | custom-call | flops 12079595520 | bytes 1024 | tf_op jit(solution)/shard_map/pallas_call | solution.py:200
  62.6 3.4 %collective-permute-start = (f32[240,256]{1,0:T(8,128)}, f32[240,256]{1,0:T(8,128)S(1)}, u32[]{:S(2)}, u32[]{:S(2)}) collective-permute-start(f32[240,256]{1,0:T(8,128)} %get-tuple-element.97), channel_id=1, source_target_pairs={{0,24},{8,0},{16,8},{24,16},{1,25},{9,1},{17,9},{25,17},{2,26},{10... | collective-permute-start | bytes 737288 | tf_op jit(solution)/shard_map/ppermute | solution.py:387
  68.2 2.7 collective-permute-done.2
  71.0 7.5 %collective-permute-done.1 = f32[240,256]{1,0:T(8,128)S(1)} collective-permute-done((f32[240,256]{1,0:T(8,128)}, f32[240,256]{1,0:T(8,128)S(1)}, u32[]{:S(2)}, u32[]{:S(2)}) %collective-permute-start.1) | collective-permute-done | bytes 245792 | tf_op jit(solution)/shard_map/ppermute | solution.py:387
  80.2 9.3 %shard_map.124 = (f32[256,512]{1,0:T(8,128)S(1)}, f32[256,512]{1,0:T(8,128)S(1)}, f32[256,512]{1,0:T(8,128)S(1)}, f32[256,512]{1,0:T(8,128)S(1)}, f32[256,512]{1...) custom-call(f32[256,512]{1,0:T(8,128)S(1)} %copy-done.14, f32[256,512]{1,0:T(8,128)S(1)} %get-tuple-element.99.refs_1_, ...), custom_call_target="tpu_custom_call" | custom-call | flops 1024 | bytes 1024 | tf_op jit(solution)/shard_map/pallas_call | solution.py:138
  92.0 5.9 %collective-permute-start.13 = (f32[256,512]{1,0:T(8,128)S(1)}, f32[256,512]{1,0:T(8,128)}, u32[]{:S(2)}, u32[]{:S(2)}) collective-permute-start(f32[256,512]{1,0:T(8,128)S(1)} %get-tuple-element.69.refs_1_.refs_0_), channel_id=1, source_target_pairs={{0,8},{8,16},{16,24},{24,0},{1,9},{9,17},{17,25},{25,1},{2,10},{10... | collective-permute-start | bytes 1572872 | tf_op jit(solution)/shard_map/ppermute | solution.py:387
  99.9 8.4 %shard_map.125 = (f32[256,512]{1,0:T(8,128)S(1)}, f32[256,512]{1,0:T(8,128)S(1)}, f32[256,512]{1,0:T(8,128)S(1)}, f32[256,512]{1,0:T(8,128)S(1)}, f32[256,512]{1...) custom-call(f32[256,512]{1,0:T(8,128)S(1)} %copy-done.13, f32[256,512]{1,0:T(8,128)S(1)} %get-tuple-element.98.refs_1_, ...), custom_call_target="tpu_custom_call" | custom-call | flops 1024 | bytes 1024 | tf_op jit(solution)/shard_map/pallas_call | solution.py:138
  120.2 19.7 %collective-permute-done.15.refs_2_ = f32[256,512]{1,0:T(8,128)S(1)} collective-permute-done((f32[256,512]{1,0:T(8,128)}, f32[256,512]{1,0:T(8,128)S(1)}, u32[]{:S(2)}, u32[]{:S(2)}) %collective-permute-start.15) | collective-permute-done | bytes 524320 | tf_op jit(solution)/shard_map/ppermute | solution.py:387
  150.6 7.7 %shard_map.127.refs_4_ = f32[2,960,256]{2,1,0:T(8,128)} custom-call(s32[2]{0:T(128)} %pad_add_fusion.1.strips_ref, f32[3840,1024]{1,0:T(8,128)} %refs_0_.13, f32[256,512]{1,0:T(8,128)} %copy-done.5, f32[256,512]{1,0:T(8,128)} %copy-done.7), custom_call_target="tpu_custom_call" | custom-call | flops 1024 | bytes 1024 | tf_op jit(solution)/shard_map/pallas_call | solution.py:346
  161.4 3.3 collective-permute-done.19.refs_1_
  171.8 7.6 %shard_map.128.refs_4_ = f32[2,960,256]{2,1,0:T(8,128)} custom-call(s32[2]{0:T(128)} %pad_add_fusion.strips_ref, f32[3840,1024]{1,0:T(8,128)} %refs_0_.13, f32[256,512]{1,0:T(8,128)} %copy-done.5, f32[256,512]{1,0:T(8,128)} %copy-done.7), custom_call_target="tpu_custom_call" | custom-call | flops 1024 | bytes 1024 | tf_op jit(solution)/shard_map/pallas_call | solution.py:346
  179.4 12.9 %collective-permute-done.20 = f32[256,512]{1,0:T(8,128)} collective-permute-done((f32[256,512]{1,0:T(8,128)}, f32[256,512]{1,0:T(8,128)}, u32[]{:S(2)}, u32[]{:S(2)}) %collective-permute-start.20) | collective-permute-done | bytes 524320 | tf_op jit(solution)/shard_map/ppermute | solution.py:384
  206.6 4.4 %shard_map.134 = f32[480,512]{1,0:T(8,128)} custom-call(s32[2]{0:T(128)S(1)} %pad_add_fusion.2.place_ref, bf16[4,960,256]{2,1,0:T(8,128)(2,1)S(1)} %get-tuple-element.85.high_ref, bf16[4,960,256]{2,1,0:T(8,128)(2,1)S(1)} %get-tuple-element.86.low_ref, f32[256,512]{1,0:T(8,128)S(1)} %copy-done.6, f32[256,512]{1,0:T(8,128)} %collective-permute-done.13.refs_1_, ...), custom_call_target="tpu_custom_call" | custom-call | flops 1024 | bytes 1024 | tf_op jit(solution)/shard_map/pallas_call | solution.py:312
  211.0 13.6 %collective-permute-done.22.far_ref = f32[256,512]{1,0:T(8,128)} collective-permute-done((f32[256,512]{1,0:T(8,128)}, f32[256,512]{1,0:T(8,128)}, u32[]{:S(2)}, u32[]{:S(2)}) %collective-permute-start.22) | collective-permute-done | bytes 524320 | tf_op jit(solution)/shard_map/ppermute | solution.py:384
  228.9 8.6 %shard_map.131 = f32[2,960,256]{2,1,0:T(8,128)} custom-call(s32[2]{0:T(128)} %pad_add_fusion.1.strips_ref, f32[3840,512]{1,0:T(8,128)} %refs_0_.15, f32[3840,512]{1,0:T(8,128)} %refs_1_.11, f32[256,512]{1,0:T(8,128)} %copy-done.3, f32[256,512]{1,0:T(8,128)} %copy-done.1, f32[2,960,256]{2,1,0:T(8,128)} %shard_map.127.refs_4_), custom_call_target="tpu_custom_call" | custom-call | flops 1024 | bytes 1024 | tf_op jit(solution)/shard_map/pallas_call | solution.py:346
  237.7 4.4 %shard_map.136 = f32[480,512]{1,0:T(8,128)} custom-call(s32[2]{0:T(128)S(1)} %pad_add_fusion.2.place_ref, bf16[4,960,256]{2,1,0:T(8,128)(2,1)S(1)} %get-tuple-element.85.high_ref, bf16[4,960,256]{2,1,0:T(8,128)(2,1)S(1)} %get-tuple-element.86.low_ref, f32[256,512]{1,0:T(8,128)S(1)} %copy-done.8, f32[256,512]{1,0:T(8,128)} %collective-permute-done.19.refs_1_, ...), custom_call_target="tpu_custom_call" | custom-call | flops 1024 | bytes 1024 | tf_op jit(solution)/shard_map/pallas_call | solution.py:312
  243.1 8.4 %shard_map.130 = f32[2,960,256]{2,1,0:T(8,128)} custom-call(s32[2]{0:T(128)} %pad_add_fusion.strips_ref, f32[3840,512]{1,0:T(8,128)} %refs_0_.15, f32[3840,512]{1,0:T(8,128)} %refs_1_.11, f32[256,512]{1,0:T(8,128)} %copy-done.3, f32[256,512]{1,0:T(8,128)} %copy-done.1, f32[2,960,256]{2,1,0:T(8,128)} %shard_map.128.refs_4_), custom_call_target="tpu_custom_call" | custom-call | flops 1024 | bytes 1024 | tf_op jit(solution)/shard_map/pallas_call | solution.py:346
  254.2 2.8 collective-permute-start.33
  257.1 8.4 %collective-permute-done.35.refs_1_ = f32[256,512]{1,0:T(8,128)S(1)} collective-permute-done((f32[256,512]{1,0:T(8,128)}, f32[256,512]{1,0:T(8,128)S(1)}, u32[]{:S(2)}, u32[]{:S(2)}) %collective-permute-start.35) | collective-permute-done | bytes 524320 | tf_op jit(solution)/shard_map/ppermute | solution.py:387
  265.4 11.2 %collective-permute-done.33.refs_3_ = f32[256,512]{1,0:T(8,128)S(1)} collective-permute-done((f32[256,512]{1,0:T(8,128)S(1)}, f32[256,512]{1,0:T(8,128)S(1)}, u32[]{:S(2)}, u32[]{:S(2)}) %collective-permute-start.33) | collective-permute-done | bytes 524320 | tf_op jit(solution)/shard_map/ppermute | solution.py:387
  279.0 8.7 %collective-permute-done.36.refs_2_ = f32[256,512]{1,0:T(8,128)S(1)} collective-permute-done((f32[256,512]{1,0:T(8,128)S(1)}, f32[256,512]{1,0:T(8,128)S(1)}, u32[]{:S(2)}, u32[]{:S(2)}) %collective-permute-start.36) | collective-permute-done | bytes 524320 | tf_op jit(solution)/shard_map/ppermute | solution.py:387
  288.4 10.4 %collective-permute-done.39.refs_3_ = f32[256,256]{1,0:T(8,128)S(1)} collective-permute-done((f32[256,256]{1,0:T(8,128)S(1)}, f32[256,256]{1,0:T(8,128)S(1)}, u32[]{:S(2)}, u32[]{:S(2)}) %collective-permute-start.39) | collective-permute-done | bytes 262176 | tf_op jit(solution)/shard_map/ppermute | solution.py:387
  300.4 2.8 collective-permute-done.37.refs_3_
  309.6 3.4 %shard_map.133 = f32[480,512]{1,0:T(8,128)S(1)} custom-call(s32[2]{0:T(128)S(1)} %pad_add_fusion.2.place_ref, bf16[4,960,256]{2,1,0:T(8,128)(2,1)S(1)} %get-tuple-element.85.high_ref, bf16[4,960,256]{2,1,0:T(8,128)(2,1)S(1)} %get-tuple-element.86.low_ref, f32[256,512]{1,0:T(8,128)S(1)} %copy-done.6, f32[256,512]{1,0:T(8,128)} %collective-permute-done.13.refs_1_, ...), custom_call_target="tpu_custom_call" | custom-call | flops 1024 | bytes 1024 | tf_op jit(solution)/shard_map/pallas_call | solution.py:312
  314.5 3.5 %shard_map.135 = f32[480,512]{1,0:T(8,128)S(1)} custom-call(s32[2]{0:T(128)S(1)} %pad_add_fusion.2.place_ref, bf16[4,960,256]{2,1,0:T(8,128)(2,1)S(1)} %get-tuple-element.85.high_ref, bf16[4,960,256]{2,1,0:T(8,128)(2,1)S(1)} %get-tuple-element.86.low_ref, f32[256,512]{1,0:T(8,128)S(1)} %copy-done.8, f32[256,512]{1,0:T(8,128)} %collective-permute-done.19.refs_1_, ...), custom_call_target="tpu_custom_call" | custom-call | flops 1024 | bytes 1024 | tf_op jit(solution)/shard_map/pallas_call | solution.py:312
  326.4 6.4 %collective-permute-done.38 = f32[480,256]{1,0:T(8,128)S(1)} collective-permute-done((f32[480,256]{1,0:T(8,128)S(1)}, f32[480,256]{1,0:T(8,128)S(1)}, u32[]{:S(2)}, u32[]{:S(2)}) %collective-permute-start.38) | collective-permute-done | bytes 491552 | tf_op jit(solution)/shard_map/ppermute | solution.py:390
  (233 shorter events, 102.5 us)
Async XLA Ops:
  10.6 25.5 %collective-permute-start.3 = (f32[256,512]{1,0:T(8,128)}, f32[256,512]{1,0:T(8,128)S(1)}, u32[]{:S(2)}, u32[]{:S(2)}) collective-permute-start(f32[256,512]{1,0:T(8,128)} %get-tuple-element.50.refs_11_), channel_id=1, source_target_pairs={{0,8},{8,16},{16,24},{1,9},{9,17},{17,25},{2,10},{10,18},{18,26},{... | collective-permute-start | bytes 1572872 | tf_op jit(solution)/shard_map/ppermute | solution.py:384
  24.3 18.5 %collective-permute-start.6 = (f32[256,512]{1,0:T(8,128)}, f32[256,512]{1,0:T(8,128)S(1)}, u32[]{:S(2)}, u32[]{:S(2)}) collective-permute-start(f32[256,512]{1,0:T(8,128)} %get-tuple-element.52.refs_11_), channel_id=1, source_target_pairs={{0,8},{8,16},{16,24},{1,9},{9,17},{17,25},{2,10},{10,18},{18,26},{... | collective-permute-start | bytes 1572872 | tf_op jit(solution)/shard_map/ppermute | solution.py:384
  37.0 24.9 %collective-permute-start.5 = (f32[256,512]{1,0:T(8,128)}, f32[256,512]{1,0:T(8,128)}, u32[]{:S(2)}, u32[]{:S(2)}) collective-permute-start(f32[256,512]{1,0:T(8,128)} %broadcast_select_fusion.3), channel_id=1, source_target_pairs={{0,4},{4,0},{1,5},{5,1},{2,6},{6,2},{3,7},{7,3},{8,12},{12,8},{9,1... | collective-permute-start | bytes 1572872 | tf_op jit(solution)/shard_map/ppermute | solution.py:390
  38.6 24.0 %collective-permute-start.4 = (f32[256,512]{1,0:T(8,128)S(1)}, f32[256,512]{1,0:T(8,128)}, u32[]{:S(2)}, u32[]{:S(2)}) collective-permute-start(f32[256,512]{1,0:T(8,128)S(1)} %collective-permute-done.3.refs_9_), channel_id=1, source_target_pairs={{0,8},{8,16},{16,24},{1,9},{9,17},{17,25},{2,10},{10,18},{18,26},{... | collective-permute-start | bytes 1572872 | tf_op jit(solution)/shard_map/ppermute | solution.py:384
  43.7 22.3 %collective-permute-start.7 = (f32[256,512]{1,0:T(8,128)}, f32[256,512]{1,0:T(8,128)}, u32[]{:S(2)}, u32[]{:S(2)}) collective-permute-start(f32[256,512]{1,0:T(8,128)} %broadcast_select_fusion.2), channel_id=1, source_target_pairs={{0,4},{4,0},{1,5},{5,1},{2,6},{6,2},{3,7},{7,3},{8,12},{12,8},{9,1... | collective-permute-start | bytes 1572872 | tf_op jit(solution)/shard_map/ppermute | solution.py:390
  44.2 21.8 %collective-permute-start.8 = (f32[256,512]{1,0:T(8,128)S(1)}, f32[256,512]{1,0:T(8,128)S(1)}, u32[]{:S(2)}, u32[]{:S(2)}) collective-permute-start(f32[256,512]{1,0:T(8,128)S(1)} %collective-permute-done.6.refs_9_), channel_id=1, source_target_pairs={{0,8},{8,16},{16,24},{1,9},{9,17},{17,25},{2,10},{10,18},{18,26},{... | collective-permute-start | bytes 1572872 | tf_op jit(solution)/shard_map/ppermute | solution.py:384
  62.6 16.9 %collective-permute-start = (f32[240,256]{1,0:T(8,128)}, f32[240,256]{1,0:T(8,128)S(1)}, u32[]{:S(2)}, u32[]{:S(2)}) collective-permute-start(f32[240,256]{1,0:T(8,128)} %get-tuple-element.97), channel_id=1, source_target_pairs={{0,24},{8,0},{16,8},{24,16},{1,25},{9,1},{17,9},{25,17},{2,26},{10... | collective-permute-start | bytes 737288 | tf_op jit(solution)/shard_map/ppermute | solution.py:387
  79.6 20.3 %collective-permute-start.10 = (f32[256,512]{1,0:T(8,128)S(1)}, f32[256,512]{1,0:T(8,128)S(1)}, u32[]{:S(2)}, u32[]{:S(2)}) collective-permute-start(f32[256,512]{1,0:T(8,128)S(1)} %broadcast_select_fusion), channel_id=1, source_target_pairs={{0,4},{4,0},{1,5},{5,1},{2,6},{6,2},{3,7},{7,3},{8,12},{12,8},{9,1... | collective-permute-start | bytes 1572872 | tf_op jit(solution)/shard_map/ppermute | solution.py:390
  92.0 19.1 %collective-permute-start.13 = (f32[256,512]{1,0:T(8,128)S(1)}, f32[256,512]{1,0:T(8,128)}, u32[]{:S(2)}, u32[]{:S(2)}) collective-permute-start(f32[256,512]{1,0:T(8,128)S(1)} %get-tuple-element.69.refs_1_.refs_0_), channel_id=1, source_target_pairs={{0,8},{8,16},{16,24},{24,0},{1,9},{9,17},{17,25},{25,1},{2,10},{10... | collective-permute-start | bytes 1572872 | tf_op jit(solution)/shard_map/ppermute | solution.py:387
  99.2 40.7 %collective-permute-start.11 = (f32[256,512]{1,0:T(8,128)}, f32[256,512]{1,0:T(8,128)S(1)}, u32[]{:S(2)}, u32[]{:S(2)}) collective-permute-start(f32[256,512]{1,0:T(8,128)} %get-tuple-element.65), channel_id=1, source_target_pairs={{0,4},{4,0},{1,5},{5,1},{2,6},{6,2},{3,7},{7,3},{8,12},{12,8},{9,1... | collective-permute-start | bytes 1572872 | tf_op jit(solution)/shard_map/ppermute | solution.py:390
  112.9 27.0 %collective-permute-start.14 = (f32[256,512]{1,0:T(8,128)S(1)}, f32[256,512]{1,0:T(8,128)}, u32[]{:S(2)}, u32[]{:S(2)}) collective-permute-start(f32[256,512]{1,0:T(8,128)S(1)} %select_add_fusion.1), channel_id=1, source_target_pairs={{8,0},{16,8},{24,16},{9,1},{17,9},{25,17},{10,2},{18,10},{26,18},{... | collective-permute-start | bytes 1572872 | tf_op jit(solution)/shard_map/ppermute | solution.py:384
  114.2 25.7 %collective-permute-start.15 = (f32[256,512]{1,0:T(8,128)}, f32[256,512]{1,0:T(8,128)S(1)}, u32[]{:S(2)}, u32[]{:S(2)}) collective-permute-start(f32[256,512]{1,0:T(8,128)} %collective-permute-done.13.refs_1_), channel_id=1, source_target_pairs={{0,8},{8,16},{16,24},{24,0},{1,9},{9,17},{17,25},{25,1},{2,10},{10... | collective-permute-start | bytes 1572872 | tf_op jit(solution)/shard_map/ppermute | solution.py:387
  117.9 27.9 %collective-permute-start.25 = (f32[3,240,256]{2,1,0:T(8,128)}, f32[3,240,256]{2,1,0:T(8,128)}, u32[]{:S(2)}, u32[]{:S(2)}) collective-permute-start(f32[3,240,256]{2,1,0:T(8,128)} %pad_maximum_fusion.4), channel_id=1, source_target_pairs={{0,1},{1,0},{2,3},{3,2},{4,5},{5,4},{6,7},{7,6},{8,9},{9,8},{10,11... | collective-permute-start | bytes 2211848 | tf_op jit(solution)/shard_map/ppermute | solution.py:450
  117.9 40.4 %collective-permute-start.18 = (f32[256,512]{1,0:T(8,128)}, f32[256,512]{1,0:T(8,128)S(1)}, u32[]{:S(2)}, u32[]{:S(2)}) collective-permute-start(f32[256,512]{1,0:T(8,128)} %copy-done.51), channel_id=1, source_target_pairs={{0,4},{4,0},{1,5},{5,1},{2,6},{6,2},{3,7},{7,3},{8,12},{12,8},{9,1... | collective-permute-start | bytes 1572872 | tf_op jit(solution)/shard_map/ppermute | solution.py:390
  141.7 18.9 %collective-permute-start.16 = (f32[256,512]{1,0:T(8,128)S(1)}, f32[256,512]{1,0:T(8,128)S(1)}, u32[]{:S(2)}, u32[]{:S(2)}) collective-permute-start(f32[256,512]{1,0:T(8,128)S(1)} %add_add_fusion.1), channel_id=1, source_target_pairs={{8,0},{16,8},{24,16},{9,1},{17,9},{25,17},{10,2},{18,10},{26,18},{... | collective-permute-start | bytes 1572872 | tf_op jit(solution)/shard_map/ppermute | solution.py:384
  143.0 21.7 %collective-permute-start.19 = (f32[256,512]{1,0:T(8,128)S(1)}, f32[256,512]{1,0:T(8,128)}, u32[]{:S(2)}, u32[]{:S(2)}) collective-permute-start(f32[256,512]{1,0:T(8,128)S(1)} %get-tuple-element.80.refs_2_.refs_0_), channel_id=1, source_target_pairs={{0,8},{8,16},{16,24},{24,0},{1,9},{9,17},{17,25},{25,1},{2,10},{10... | collective-permute-start | bytes 1572872 | tf_op jit(solution)/shard_map/ppermute | solution.py:387
  148.4 50.0 %collective-permute-start.26 = (f32[3,480,256]{2,1,0:T(8,128)}, f32[3,480,256]{2,1,0:T(8,128)}, u32[]{:S(2)}, u32[]{:S(2)}) collective-permute-start(f32[3,480,256]{2,1,0:T(8,128)} %fusion.3), channel_id=1, source_target_pairs={{0,2},{1,3},{2,0},{3,1},{4,6},{5,7},{6,4},{7,5},{8,10},{9,11},{10,... | collective-permute-start | bytes 4423688 | tf_op jit(solution)/shard_map/ppermute | solution.py:454
  164.8 27.6 %collective-permute-start.20 = (f32[256,512]{1,0:T(8,128)}, f32[256,512]{1,0:T(8,128)}, u32[]{:S(2)}, u32[]{:S(2)}) collective-permute-start(f32[256,512]{1,0:T(8,128)} %select_add_fusion), channel_id=1, source_target_pairs={{8,0},{16,8},{24,16},{9,1},{17,9},{25,17},{10,2},{18,10},{26,18},{... | collective-permute-start | bytes 1572872 | tf_op jit(solution)/shard_map/ppermute | solution.py:384
  166.1 26.5 %collective-permute-start.17 = (f32[256,512]{1,0:T(8,128)S(1)}, f32[256,512]{1,0:T(8,128)S(1)}, u32[]{:S(2)}, u32[]{:S(2)}) collective-permute-start(f32[256,512]{1,0:T(8,128)S(1)} %copy-done.50), channel_id=1, source_target_pairs={{0,4},{4,0},{1,5},{5,1},{2,6},{6,2},{3,7},{7,3},{8,12},{12,8},{9,1... | collective-permute-start | bytes 1572872 | tf_op jit(solution)/shard_map/ppermute | solution.py:390
  168.6 26.3 %collective-permute-start.21 = (f32[256,512]{1,0:T(8,128)S(1)}, f32[256,512]{1,0:T(8,128)S(1)}, u32[]{:S(2)}, u32[]{:S(2)}) collective-permute-start(f32[256,512]{1,0:T(8,128)S(1)} %collective-permute-done.15.refs_2_), channel_id=1, source_target_pairs={{0,8},{8,16},{16,24},{24,0},{1,9},{9,17},{17,25},{25,1},{2,10},{10... | collective-permute-start | bytes 1572872 | tf_op jit(solution)/shard_map/ppermute | solution.py:387
  194.8 29.8 %collective-permute-start.22 = (f32[256,512]{1,0:T(8,128)}, f32[256,512]{1,0:T(8,128)}, u32[]{:S(2)}, u32[]{:S(2)}) collective-permute-start(f32[256,512]{1,0:T(8,128)} %add_add_fusion), channel_id=1, source_target_pairs={{8,0},{16,8},{24,16},{9,1},{17,9},{25,17},{10,2},{18,10},{26,18},{... | collective-permute-start | bytes 1572872 | tf_op jit(solution)/shard_map/ppermute | solution.py:384
  206.4 31.2 %collective-permute-start.31 = (f32[256,512]{1,0:T(8,128)S(1)}, f32[256,512]{1,0:T(8,128)S(1)}, u32[]{:S(2)}, u32[]{:S(2)}) collective-permute-start(f32[256,512]{1,0:T(8,128)S(1)} %shard_map.126.refs_2_.refs_0_), channel_id=1, source_target_pairs={{0,8},{8,16},{16,24},{24,0},{1,9},{9,17},{17,25},{25,1},{2,10},{10... | collective-permute-start | bytes 1572872 | tf_op jit(solution)/shard_map/ppermute | solution.py:387
  224.6 32.4 %collective-permute-start.27 = (f32[480,512]{1,0:T(8,128)}, f32[480,512]{1,0:T(8,128)}, u32[]{:S(2)}, u32[]{:S(2)}) collective-permute-start(f32[480,512]{1,0:T(8,128)} %shard_map.134), channel_id=1, source_target_pairs={{0,4},{4,0},{1,5},{5,1},{2,6},{6,2},{3,7},{7,3},{8,12},{12,8},{9,1... | collective-permute-start | bytes 2949128 | tf_op jit(solution)/shard_map/ppermute | solution.py:390
  237.5 67.4 %collective-permute-start.23 = (f32[2,960,256]{2,1,0:T(8,128)}, f32[2,960,256]{2,1,0:T(8,128)}, u32[]{:S(2)}, u32[]{:S(2)}) collective-permute-start(f32[2,960,256]{2,1,0:T(8,128)} %shard_map.131), channel_id=1, source_target_pairs={{0,1},{1,0},{2,3},{3,2},{4,5},{5,4},{6,7},{7,6},{8,9},{9,8},{10,11... | collective-permute-start | bytes 5898248 | tf_op jit(solution)/shard_map/ppermute | solution.py:450
  237.6 27.8 %collective-permute-start.35 = (f32[256,512]{1,0:T(8,128)}, f32[256,512]{1,0:T(8,128)S(1)}, u32[]{:S(2)}, u32[]{:S(2)}) collective-permute-start(f32[256,512]{1,0:T(8,128)} %copy-done.1), channel_id=1, source_target_pairs={{0,8},{8,16},{16,24},{24,0},{1,9},{9,17},{17,25},{25,1},{2,10},{10... | collective-permute-start | bytes 1572872 | tf_op jit(solution)/shard_map/ppermute | solution.py:387
  242.9 36.1 %collective-permute-start.30 = (f32[480,512]{1,0:T(8,128)}, f32[480,512]{1,0:T(8,128)}, u32[]{:S(2)}, u32[]{:S(2)}) collective-permute-start(f32[480,512]{1,0:T(8,128)} %shard_map.136), channel_id=1, source_target_pairs={{0,4},{4,0},{1,5},{5,1},{2,6},{6,2},{3,7},{7,3},{8,12},{12,8},{9,1... | collective-permute-start | bytes 2949128 | tf_op jit(solution)/shard_map/ppermute | solution.py:390
  254.2 22.5 %collective-permute-start.33 = (f32[256,512]{1,0:T(8,128)S(1)}, f32[256,512]{1,0:T(8,128)S(1)}, u32[]{:S(2)}, u32[]{:S(2)}) collective-permute-start(f32[256,512]{1,0:T(8,128)S(1)} %collective-permute-done.32.refs_2_), channel_id=1, source_target_pairs={{0,8},{8,16},{16,24},{24,0},{1,9},{9,17},{17,25},{25,1},{2,10},{10... | collective-permute-start | bytes 1572872 | tf_op jit(solution)/shard_map/ppermute | solution.py:387
  265.4 22.2 %collective-permute-start.36 = (f32[256,512]{1,0:T(8,128)S(1)}, f32[256,512]{1,0:T(8,128)S(1)}, u32[]{:S(2)}, u32[]{:S(2)}) collective-permute-start(f32[256,512]{1,0:T(8,128)S(1)} %collective-permute-done.35.refs_1_), channel_id=1, source_target_pairs={{0,8},{8,16},{16,24},{24,0},{1,9},{9,17},{17,25},{25,1},{2,10},{10... | collective-permute-start | bytes 1572872 | tf_op jit(solution)/shard_map/ppermute | solution.py:387
  288.4 44.5 %collective-permute-start.34 = (f32[480,512]{1,0:T(8,128)S(1)}, f32[480,512]{1,0:T(8,128)S(1)}, u32[]{:S(2)}, u32[]{:S(2)}) collective-permute-start(f32[480,512]{1,0:T(8,128)S(1)} %shard_map.138), channel_id=1, source_target_pairs={{0,4},{4,0},{1,5},{5,1},{2,6},{6,2},{3,7},{7,3},{8,12},{12,8},{9,1... | collective-permute-start | bytes 2949128 | tf_op jit(solution)/shard_map/ppermute | solution.py:390
  300.4 25.9 %collective-permute-start.40 = (f32[480,256]{1,0:T(8,128)S(1)}, f32[480,256]{1,0:T(8,128)S(1)}, u32[]{:S(2)}, u32[]{:S(2)}) collective-permute-start(f32[480,256]{1,0:T(8,128)S(1)} %shard_map.142), channel_id=1, source_target_pairs={{0,4},{4,0},{1,5},{5,1},{2,6},{6,2},{3,7},{7,3},{8,12},{12,8},{9,1... | collective-permute-start | bytes 1474568 | tf_op jit(solution)/shard_map/ppermute | solution.py:390
  304.9 27.9 %collective-permute-start.38 = (f32[480,256]{1,0:T(8,128)S(1)}, f32[480,256]{1,0:T(8,128)S(1)}, u32[]{:S(2)}, u32[]{:S(2)}) collective-permute-start(f32[480,256]{1,0:T(8,128)S(1)} %shard_map.140), channel_id=1, source_target_pairs={{0,4},{4,0},{1,5},{5,1},{2,6},{6,2},{3,7},{7,3},{8,12},{12,8},{9,1... | collective-permute-start | bytes 1474568 | tf_op jit(solution)/shard_map/ppermute | solution.py:390
  306.9 28.4 %collective-permute-start.24 = (f32[960,256]{1,0:T(8,128)S(1)}, f32[960,256]{1,0:T(8,128)S(1)}, u32[]{:S(2)}, u32[]{:S(2)}) collective-permute-start(f32[960,256]{1,0:T(8,128)S(1)} %slice_bitcast_fusion), channel_id=1, source_target_pairs={{0,2},{1,3},{2,0},{3,1},{4,6},{5,7},{6,4},{7,5},{8,10},{9,11},{10,... | collective-permute-start | bytes 2949128 | tf_op jit(solution)/shard_map/ppermute | solution.py:454
  (70 other events, 801.4 us)
